TPU v7x, 32 devices: a whole 2x2x4 slice. The times are simulated.
32 devices in a mesh: rep: 8 (over y, x, core), shard: 4 (over z).
Axes of the slice: x: 2, y: 2, z: 4, core: 2. Of those that a mesh axis runs over, the one named last changes fastest.
Arguments:
- tokens: bfloat16 [8192, 2048], P(('rep', 'shard')), may hold values from -6 to 6
- cotangent: bfloat16 [8192, 2048], P(('rep', 'shard')), may hold values from -6 to 6
- token_order: int32 [8192], replicated, may hold values from 0 to 8191, as said below
- lengths: int32 [64, 4], P(('rep', 'shard')), may hold values from 1 to 64, 128 in all within a row
- query_weight: bfloat16 [2048, 2048], P('shard'), may hold values from -0.125 to 0.125
- key_weight: bfloat16 [2048, 2048], P('shard'), may hold values from -0.125 to 0.125
- value_weight: bfloat16 [2048, 4096], P('shard'), may hold values from -0.125 to 0.125
- gate_weight: bfloat16 [2048, 4096], P('shard'), may hold values from -0.125 to 0.125
- out_weight: bfloat16 [4096, 2048], P('shard'), may hold values from -0.1875 to 0.1875
- gelu_weight: bfloat16 [2048, 4096], P('shard'), may hold values from -0.125 to 0.125
- up_weight: bfloat16 [2048, 4096], P('shard'), may hold values from -0.125 to 0.125
- down_weight: bfloat16 [4096, 2048], P('shard'), may hold values from -0.1875 to 0.1875
- gain_one: bfloat16 [2048], P('shard'), may hold values from 0.099609375 to 1.8984375
- shift_one: bfloat16 [2048], P('shard'), may hold values from -1.1953125 to 1.1953125
- gain_two: bfloat16 [2048], P('shard'), may hold values from 0.099609375 to 1.8984375
- shift_two: bfloat16 [2048], P('shard'), may hold values from -1.1953125 to 1.1953125
Outputs:
- result: bfloat16 [8192, 2048], P(('rep', 'shard'))
- token_gradient: bfloat16 [8192, 2048], P(('rep', 'shard'))
- query_gradient: float32 [2048, 2048], P('shard')
- key_gradient: float32 [2048, 2048], P('shard')
- value_gradient: float32 [2048, 4096], P('shard')
- gate_gradient: float32 [2048, 4096], P('shard')
- out_gradient: float32 [4096, 2048], P('shard')
- gelu_gradient: float32 [2048, 4096], P('shard')
- up_gradient: float32 [2048, 4096], P('shard')
- down_gradient: float32 [4096, 2048], P('shard')
- gain_one_gradient: float32 [2048], P('shard')
- shift_one_gradient: float32 [2048], P('shard')
- gain_two_gradient: float32 [2048], P('shard')
- shift_two_gradient: float32 [2048], P('shard')
Inputs may be any that keep to these rules, and one draw needn't show every extreme that they name: `token_order`: A permutation of the slots. The loader rows [s * 256, (s + 1) * 256) send exactly 8 rows into each block of 256 slots. `lengths`: each row sums to 128; its last entry is the padding at the pack's end, the others are sequences.
All inputs are finite; a program needn't handle non-finite values.
Results may differ from a plain program's by a relative error of at most 0.023.
Values may be sent and summed in bfloat16 or wider, within the bound.
A program may use at most 640 MiB of HBM per device.

v0:
```python
import jax
import jax.numpy as jnp
from jax import lax
from jax.sharding import PartitionSpec as P

HEADS = 8
KH = 256


layer_epsilon = 1e-05
head_epsilon = 1.0
rotary_base = 10000.0
left_pairing = (0, 0, 0, 0, 2, 1, 1, 3)


def norm_rows(inputs, gain, shift):
    average = jnp.mean(inputs, axis=-1, keepdims=True)
    centred = inputs - average
    spread = jnp.mean(centred * centred, axis=-1, keepdims=True)
    return centred * lax.rsqrt(spread + layer_epsilon) * gain + shift


def head_norm(retained):
    shaped = retained.reshape(retained.shape[:-1] + (HEADS, -1))
    average = jnp.mean(shaped, axis=-1, keepdims=True)
    centred = shaped - average
    spread = jnp.mean(centred * centred, axis=-1, keepdims=True)
    return (centred * lax.rsqrt(spread + head_epsilon)).reshape(retained.shape)


def gate_mix(gating, retained):
    return jax.nn.silu(gating) * head_norm(retained)


def gelu_gate(gelu_in, up_proj):
    return jax.nn.gelu(gelu_in) * up_proj


def rotate(heads_in, cosine_table, sine_table):
    half_size = heads_in.shape[-1] // 2
    former = heads_in[..., :half_size]
    latter = heads_in[..., half_size:]
    return jnp.concatenate(
        [former * cosine_table - latter * sine_table, former * sine_table + latter * cosine_table],
        axis=-1,
    )


def rotate_back(heads_in, cosine_table, sine_table):
    half_size = heads_in.shape[-1] // 2
    former = heads_in[..., :half_size]
    latter = heads_in[..., half_size:]
    return jnp.concatenate(
        [former * cosine_table + latter * sine_table, latter * cosine_table - former * sine_table],
        axis=-1,
    )


def pack_tables(length_row, pack_rows):
    entries = length_row.shape[0]
    slot_ids = jnp.arange(pack_rows, dtype=jnp.int32)
    seq_ends = jnp.cumsum(length_row, dtype=jnp.int32)
    seq_starts = seq_ends - length_row
    segment = jnp.sum(
        (slot_ids[:, None] >= seq_ends[None, :]).astype(jnp.int32), axis=1, dtype=jnp.int32
    )
    owners = segment[:, None] == jnp.arange(entries, dtype=jnp.int32)[None, :]
    begins = jnp.sum(
        jnp.where(owners, seq_starts[None, :], jnp.zeros((), jnp.int32)), axis=1, dtype=jnp.int32
    )
    places = (slot_ids - begins).astype(jnp.float32)
    usable = segment < entries - 1
    half_size = KH // 2
    frequency = jnp.power(
        jnp.float32(rotary_base),
        -jnp.arange(half_size, dtype=jnp.float32) / jnp.float32(half_size - 1),
    )
    angles = places[:, None] * frequency[None, :]
    cosine_table = jnp.cos(angles)[:, None, :]
    sine_table = jnp.sin(angles)[:, None, :]
    lag_steps = slot_ids[:, None] - slot_ids[None, :]
    linked = (segment[:, None] == segment[None, :]) & (lag_steps >= 0) & usable[None, :]
    log_rates = jnp.log(
        1.0 - jnp.power(jnp.float32(2.0), -5.0 - jnp.arange(HEADS, dtype=jnp.float32))
    )
    lag_float = jnp.where(linked, lag_steps, jnp.zeros((), jnp.int32)).astype(jnp.float32)
    decays = jnp.where(
        linked[None],
        jnp.exp(log_rates[:, None, None] * lag_float[None]),
        jnp.zeros((), jnp.float32),
    )
    return (cosine_table, sine_table, decays, usable)


def gram_rows(leading, trailing):
    return lax.dot_general(
        leading, trailing, (((0,), (0,)), ((), ())), preferred_element_type=jnp.float32
    )


def back_through(incoming, matrix):
    return lax.dot_general(
        incoming, matrix, (((1,), (1,)), ((), ())), preferred_element_type=jnp.float32
    )


def forward_dot(inputs, matrix):
    return jnp.dot(inputs, matrix, preferred_element_type=jnp.float32)


def layer_ahead(block_tokens, gathered, tables):
    (
        query_weight,
        key_weight,
        value_weight,
        gate_weight,
        out_weight,
        gelu_weight,
        up_weight,
        down_weight,
        gain_one,
        shift_one,
        gain_two,
        shift_two,
    ) = gathered
    cosine_table, sine_table, decays, usable = tables
    row_count = block_tokens.shape[0]
    inputs = block_tokens.astype(jnp.float32)
    normed = norm_rows(inputs, gain_one.astype(jnp.float32), shift_one.astype(jnp.float32)).astype(
        jnp.bfloat16
    )
    queries = forward_dot(normed, query_weight)
    keys_in = forward_dot(normed, key_weight)
    v_low = forward_dot(normed, value_weight).astype(jnp.bfloat16).reshape(row_count, HEADS, -1)
    gating = forward_dot(normed, gate_weight)
    q_rot = rotate(queries.reshape(row_count, HEADS, -1), cosine_table, sine_table).astype(
        jnp.bfloat16
    )
    k_rot = (
        rotate(keys_in.reshape(row_count, HEADS, -1), cosine_table, sine_table) * KH ** (-0.5)
    ).astype(jnp.bfloat16)
    scores = jnp.einsum("ihd,jhd->hij", q_rot, k_rot, preferred_element_type=jnp.float32)
    weights_low = (scores * decays).astype(jnp.bfloat16)
    retained = jnp.einsum(
        "hij,jhe->ihe", weights_low, v_low, preferred_element_type=jnp.float32
    ).reshape(row_count, -1)
    branch = gate_mix(gating, retained).astype(jnp.bfloat16)
    middle = inputs + forward_dot(branch, out_weight)
    normed_two = norm_rows(
        middle, gain_two.astype(jnp.float32), shift_two.astype(jnp.float32)
    ).astype(jnp.bfloat16)
    gelu_in = forward_dot(normed_two, gelu_weight)
    up_proj = forward_dot(normed_two, up_weight)
    hidden = gelu_gate(gelu_in, up_proj).astype(jnp.bfloat16)
    ending = jnp.where(usable[:, None], middle + forward_dot(hidden, down_weight), 0.0).astype(
        jnp.bfloat16
    )
    kept = (
        inputs,
        normed,
        gating,
        q_rot,
        k_rot,
        v_low,
        weights_low,
        retained,
        branch,
        middle,
        normed_two,
        gelu_in,
        up_proj,
        hidden,
    )
    return (ending, kept)


def layer_back(block_cotangent, gathered, tables, kept):
    (
        query_weight,
        key_weight,
        value_weight,
        gate_weight,
        out_weight,
        gelu_weight,
        up_weight,
        down_weight,
        gain_one,
        shift_one,
        gain_two,
        shift_two,
    ) = gathered
    cosine_table, sine_table, decays, usable = tables
    (
        inputs,
        normed,
        gating,
        q_rot,
        k_rot,
        v_low,
        weights_low,
        retained,
        branch,
        middle,
        normed_two,
        gelu_in,
        up_proj,
        hidden,
    ) = kept
    row_count = inputs.shape[0]
    back_out = jnp.where(usable[:, None], block_cotangent.astype(jnp.float32), 0.0)
    back_low = back_out.astype(jnp.bfloat16)
    back_hidden = back_through(back_low, down_weight)
    _, gelu_pullback = jax.vjp(gelu_gate, gelu_in, up_proj)
    back_gelu, back_up = gelu_pullback(back_hidden)
    gelu_low = back_gelu.astype(jnp.bfloat16)
    up_low = back_up.astype(jnp.bfloat16)
    back_normed_two = back_through(gelu_low, gelu_weight) + back_through(up_low, up_weight)
    _, second_pullback = jax.vjp(
        norm_rows, middle, gain_two.astype(jnp.float32), shift_two.astype(jnp.float32)
    )
    through_norm, gain_two_part, shift_two_part = second_pullback(back_normed_two)
    back_middle = back_out + through_norm
    middle_low = back_middle.astype(jnp.bfloat16)
    back_branch = back_through(middle_low, out_weight)
    _, mix_pullback = jax.vjp(gate_mix, gating, retained)
    back_gating, back_retained = mix_pullback(back_branch)
    gating_low = back_gating.astype(jnp.bfloat16)
    retained_low = back_retained.astype(jnp.bfloat16).reshape(row_count, HEADS, -1)
    back_weights = jnp.einsum(
        "ihe,jhe->hij", retained_low, v_low, preferred_element_type=jnp.float32
    )
    back_values = jnp.einsum(
        "hij,ihe->jhe", weights_low, retained_low, preferred_element_type=jnp.float32
    )
    values_low = back_values.reshape(row_count, -1).astype(jnp.bfloat16)
    back_scores = (back_weights * decays).astype(jnp.bfloat16)
    back_queries = jnp.einsum(
        "hij,jhd->ihd", back_scores, k_rot, preferred_element_type=jnp.float32
    )
    back_keys = jnp.einsum("hij,ihd->jhd", back_scores, q_rot, preferred_element_type=jnp.float32)
    queries_low = (
        rotate_back(back_queries, cosine_table, sine_table)
        .reshape(row_count, -1)
        .astype(jnp.bfloat16)
    )
    keys_low = (
        (rotate_back(back_keys, cosine_table, sine_table) * KH ** (-0.5))
        .reshape(row_count, -1)
        .astype(jnp.bfloat16)
    )
    back_normed = back_through(queries_low, query_weight) + back_through(keys_low, key_weight)
    back_normed = (
        back_normed + back_through(values_low, value_weight) + back_through(gating_low, gate_weight)
    )
    _, first_pullback = jax.vjp(
        norm_rows, inputs, gain_one.astype(jnp.float32), shift_one.astype(jnp.float32)
    )
    through_first, gain_one_part, shift_one_part = first_pullback(back_normed)
    back_inputs = (back_middle + through_first).astype(jnp.bfloat16)
    lefts = (normed, normed_two, branch, hidden)
    rights = (queries_low, keys_low, values_low, gating_low, middle_low, gelu_low, up_low, back_low)
    smalls = (gain_one_part, shift_one_part, gain_two_part, shift_two_part)
    return (back_inputs, lefts, rights, smalls)


def local(
    tokens,
    cotangent,
    token_order,
    lengths,
    query_weight,
    key_weight,
    value_weight,
    gate_weight,
    out_weight,
    gelu_weight,
    up_weight,
    down_weight,
    gain_one,
    shift_one,
    gain_two,
    shift_two,
):
    device_count = lax.axis_size(("rep", "shard"))
    device_index = lax.axis_index(("rep", "shard"))
    local_rows = tokens.shape[0]
    width = tokens.shape[1]
    piece_rows = local_rows // device_count
    micro_count = lengths.shape[0]
    pack_rows = local_rows // micro_count
    own_order = lax.dynamic_slice_in_dim(token_order, device_index * local_rows, local_rows)
    sending = jnp.argsort(own_order // local_rows)
    arrived = (
        lax.all_to_all(
            tokens[sending].reshape(device_count, piece_rows, width),
            ("rep", "shard"),
            split_axis=0,
            concat_axis=0,
            tiled=True,
        ),
        lax.all_to_all(
            cotangent[sending].reshape(device_count, piece_rows, width),
            ("rep", "shard"),
            split_axis=0,
            concat_axis=0,
            tiled=True,
        ),
    )
    incoming = jnp.nonzero(token_order // local_rows == device_index, size=local_rows)[0]
    slot_ids = token_order[incoming] - device_index * local_rows
    work_tokens = (
        jnp.zeros((local_rows, width), jnp.bfloat16)
        .at[slot_ids]
        .set(arrived[0].reshape(local_rows, width))
    )
    work_cotangent = (
        jnp.zeros((local_rows, width), jnp.bfloat16)
        .at[slot_ids]
        .set(arrived[1].reshape(local_rows, width))
    )
    endings = []
    backs = []
    for micro_index in range(micro_count):
        first_row = micro_index * pack_rows
        block_tokens = work_tokens[first_row : first_row + pack_rows]
        block_cotangent = work_cotangent[first_row : first_row + pack_rows]
        tables = pack_tables(lengths[micro_index], pack_rows)
        ahead_weights = (
            lax.all_gather(query_weight, "shard", axis=0, tiled=True),
            lax.all_gather(key_weight, "shard", axis=0, tiled=True),
            lax.all_gather(value_weight, "shard", axis=0, tiled=True),
            lax.all_gather(gate_weight, "shard", axis=0, tiled=True),
            lax.all_gather(out_weight, "shard", axis=0, tiled=True),
            lax.all_gather(gelu_weight, "shard", axis=0, tiled=True),
            lax.all_gather(up_weight, "shard", axis=0, tiled=True),
            lax.all_gather(down_weight, "shard", axis=0, tiled=True),
            lax.all_gather(gain_one, "shard", axis=0, tiled=True),
            lax.all_gather(shift_one, "shard", axis=0, tiled=True),
            lax.all_gather(gain_two, "shard", axis=0, tiled=True),
            lax.all_gather(shift_two, "shard", axis=0, tiled=True),
        )
        ending, kept = layer_ahead(block_tokens, ahead_weights, tables)
        behind_weights = (
            lax.all_gather(query_weight, "shard", axis=0, tiled=True),
            lax.all_gather(key_weight, "shard", axis=0, tiled=True),
            lax.all_gather(value_weight, "shard", axis=0, tiled=True),
            lax.all_gather(gate_weight, "shard", axis=0, tiled=True),
            lax.all_gather(out_weight, "shard", axis=0, tiled=True),
            lax.all_gather(gelu_weight, "shard", axis=0, tiled=True),
            lax.all_gather(up_weight, "shard", axis=0, tiled=True),
            lax.all_gather(down_weight, "shard", axis=0, tiled=True),
            lax.all_gather(gain_one, "shard", axis=0, tiled=True),
            lax.all_gather(shift_one, "shard", axis=0, tiled=True),
            lax.all_gather(gain_two, "shard", axis=0, tiled=True),
            lax.all_gather(shift_two, "shard", axis=0, tiled=True),
        )
        back_inputs, lefts, rights, smalls = layer_back(
            block_cotangent, behind_weights, tables, kept
        )
        full_parts = tuple(
            (gram_rows(lefts[left_pairing[which]], rights[which]) for which in range(8))
        )
        parts = (
            lax.psum_scatter(
                full_parts[0].astype(jnp.bfloat16), "shard", scatter_dimension=0, tiled=True
            ).astype(jnp.float32),
            lax.psum_scatter(
                full_parts[1].astype(jnp.bfloat16), "shard", scatter_dimension=0, tiled=True
            ).astype(jnp.float32),
            lax.psum_scatter(
                full_parts[2].astype(jnp.bfloat16), "shard", scatter_dimension=0, tiled=True
            ).astype(jnp.float32),
            lax.psum_scatter(
                full_parts[3].astype(jnp.bfloat16), "shard", scatter_dimension=0, tiled=True
            ).astype(jnp.float32),
            lax.psum_scatter(
                full_parts[4].astype(jnp.bfloat16), "shard", scatter_dimension=0, tiled=True
            ).astype(jnp.float32),
            lax.psum_scatter(
                full_parts[5].astype(jnp.bfloat16), "shard", scatter_dimension=0, tiled=True
            ).astype(jnp.float32),
            lax.psum_scatter(
                full_parts[6].astype(jnp.bfloat16), "shard", scatter_dimension=0, tiled=True
            ).astype(jnp.float32),
            lax.psum_scatter(
                full_parts[7].astype(jnp.bfloat16), "shard", scatter_dimension=0, tiled=True
            ).astype(jnp.float32),
            lax.psum_scatter(
                smalls[0].astype(jnp.bfloat16), "shard", scatter_dimension=0, tiled=True
            ).astype(jnp.float32),
            lax.psum_scatter(
                smalls[1].astype(jnp.bfloat16), "shard", scatter_dimension=0, tiled=True
            ).astype(jnp.float32),
            lax.psum_scatter(
                smalls[2].astype(jnp.bfloat16), "shard", scatter_dimension=0, tiled=True
            ).astype(jnp.float32),
            lax.psum_scatter(
                smalls[3].astype(jnp.bfloat16), "shard", scatter_dimension=0, tiled=True
            ).astype(jnp.float32),
        )
        if micro_index == 0:
            summed = tuple(parts)
        else:
            summed = tuple((earlier + adding for earlier, adding in zip(summed, parts)))
        endings.append(ending)
        backs.append(back_inputs)
    totals = (
        lax.psum(summed[0].astype(jnp.bfloat16), "rep").astype(jnp.float32),
        lax.psum(summed[1].astype(jnp.bfloat16), "rep").astype(jnp.float32),
        lax.psum(summed[2].astype(jnp.bfloat16), "rep").astype(jnp.float32),
        lax.psum(summed[3].astype(jnp.bfloat16), "rep").astype(jnp.float32),
        lax.psum(summed[4].astype(jnp.bfloat16), "rep").astype(jnp.float32),
        lax.psum(summed[5].astype(jnp.bfloat16), "rep").astype(jnp.float32),
        lax.psum(summed[6].astype(jnp.bfloat16), "rep").astype(jnp.float32),
        lax.psum(summed[7].astype(jnp.bfloat16), "rep").astype(jnp.float32),
        lax.psum(summed[8].astype(jnp.bfloat16), "rep").astype(jnp.float32),
        lax.psum(summed[9].astype(jnp.bfloat16), "rep").astype(jnp.float32),
        lax.psum(summed[10].astype(jnp.bfloat16), "rep").astype(jnp.float32),
        lax.psum(summed[11].astype(jnp.bfloat16), "rep").astype(jnp.float32),
    )
    work_result = jnp.concatenate(endings, axis=0)
    work_gradient = jnp.concatenate(backs, axis=0)
    returned = (
        lax.all_to_all(
            work_result[slot_ids].reshape(device_count, piece_rows, width),
            ("rep", "shard"),
            split_axis=0,
            concat_axis=0,
            tiled=True,
        ),
        lax.all_to_all(
            work_gradient[slot_ids].reshape(device_count, piece_rows, width),
            ("rep", "shard"),
            split_axis=0,
            concat_axis=0,
            tiled=True,
        ),
    )
    result = (
        jnp.zeros((local_rows, width), jnp.bfloat16)
        .at[sending]
        .set(returned[0].reshape(local_rows, width))
    )
    token_gradient = (
        jnp.zeros((local_rows, width), jnp.bfloat16)
        .at[sending]
        .set(returned[1].reshape(local_rows, width))
    )
    return (
        result,
        token_gradient,
        totals[0],
        totals[1],
        totals[2],
        totals[3],
        totals[4],
        totals[5],
        totals[6],
        totals[7],
        totals[8],
        totals[9],
        totals[10],
        totals[11],
    )


def solution(mesh):
    in_specs = (
        P(("rep", "shard"), None),
        P(("rep", "shard"), None),
        P(),
        P(("rep", "shard"), None),
        P("shard", None),
        P("shard", None),
        P("shard", None),
        P("shard", None),
        P("shard", None),
        P("shard", None),
        P("shard", None),
        P("shard", None),
        P("shard"),
        P("shard"),
        P("shard"),
        P("shard"),
    )
    out_specs = (
        P(("rep", "shard"), None),
        P(("rep", "shard"), None),
        P("shard", None),
        P("shard", None),
        P("shard", None),
        P("shard", None),
        P("shard", None),
        P("shard", None),
        P("shard", None),
        P("shard", None),
        P("shard"),
        P("shard"),
        P("shard"),
        P("shard"),
    )
    return jax.shard_map(local, mesh=mesh, in_specs=in_specs, out_specs=out_specs, check_vma=False)
```

profile of v0, /device:TPU:0, one launch (start us, length us, event | category | flops | bytes accessed | tf_op | source)
XLA Modules:
  0.0 6619.1 jit_solution(5606545270691218580)
XLA Ops:
  27.1 57.0 scatter_custom_fusion
  87.2 14.2 all-gather.1
  108.5 66.2 %all-gather = bf16[4,1,512]{2,1,0:T(2,128)(2,1)S(1)} all-gather(bf16[1,1,512]{2,1,0:T(2,128)(2,1)S(1)} %reshape.883), channel_id=1, replica_groups=mesh['rep'=8,'shard'=4] {'shard'}, dimensions={0}, use_global_device_ids=true | all-gather | bytes 5120 | tf_op jit(solution)/shard_map/all_gather | solution.py:337
  176.5 12.0 all-gather.3
  189.1 11.9 all-gather.2
  220.6 136.0 %all-gather.17.cloned.1.call-done = bf16[2048,2048]{1,0:T(8,128)(2,1)} async-done(((bf16[512,2048]{1,0:T(8,128)(2,1)}), bf16[2048,2048]{1,0:T(8,128)(2,1)}) %all-gather.17.cloned.1.call-update) | async-done | bytes 8388624 | tf_op jit(solution)/shard_map/all_gather | solution.py:329
  381.0 262.2 %all-gather.15.cloned.1.call-done = bf16[2048,4096]{1,0:T(8,128)(2,1)} async-done(((bf16[512,4096]{1,0:T(8,128)(2,1)}), bf16[2048,4096]{1,0:T(8,128)(2,1)}) %all-gather.15.cloned.1.call-update) | async-done | bytes 16777232 | tf_op jit(solution)/shard_map/all_gather | solution.py:331
  671.0 258.6 %all-gather.13.cloned.1.call-done = bf16[2048,4096]{1,0:T(8,128)(2,1)} async-done(((bf16[512,4096]{1,0:T(8,128)(2,1)}), bf16[2048,4096]{1,0:T(8,128)(2,1)}) %all-gather.13.cloned.1.call-update) | async-done | bytes 16777232 | tf_op jit(solution)/shard_map/all_gather | solution.py:332
  929.6 11.1 multiply_convert_fusion.5
  940.7 275.3 %all-gather.21.cloned.1.call-done = bf16[4096,2048]{1,0:T(8,128)(2,1)} async-done(((bf16[1024,2048]{1,0:T(8,128)(2,1)}), bf16[4096,2048]{1,0:T(8,128)(2,1)}) %all-gather.21.cloned.1.call-update) | async-done | bytes 16777232 | tf_op jit(solution)/shard_map/all_gather | solution.py:333
  1225.2 12.6 multiply_convert_fusion.3
  1244.7 257.7 %all-gather.23.cloned.1.call-done = bf16[2048,4096]{1,0:T(8,128)(2,1)} async-done(((bf16[512,4096]{1,0:T(8,128)(2,1)}), bf16[2048,4096]{1,0:T(8,128)(2,1)}) %all-gather.23.cloned.1.call-update) | async-done | bytes 16777232 | tf_op jit(solution)/shard_map/all_gather | solution.py:334
  1502.5 10.0 fusion.172
  1512.5 276.5 %all-gather.25.cloned.1.call-done = bf16[2048,4096]{1,0:T(8,128)(2,1)} async-done(((bf16[512,4096]{1,0:T(8,128)(2,1)}), bf16[2048,4096]{1,0:T(8,128)(2,1)}) %all-gather.25.cloned.1.call-update) | async-done | bytes 16777232 | tf_op jit(solution)/shard_map/all_gather | solution.py:335
  1789.0 9.7 fusion.173
  1798.8 11.5 fusion.170
  1814.0 261.6 %all-gather.27.cloned.1.call-done = bf16[4096,2048]{1,0:T(8,128)(2,1)} async-done(((bf16[1024,2048]{1,0:T(8,128)(2,1)}), bf16[4096,2048]{1,0:T(8,128)(2,1)}) %all-gather.27.cloned.1.call-update) | async-done | bytes 16777232 | tf_op jit(solution)/shard_map/all_gather | solution.py:336
  2075.6 15.6 multiply_convert_fusion
  2091.2 12.7 fusion.178
  2103.9 15.4 multiply_convert_fusion.1
  2119.3 12.9 fusion.174
  2132.3 12.9 convolution_add_fusion.2
  2145.2 14.8 multiply_reduce_fusion.5
  2164.6 15.2 fusion.91
  2201.2 15.6 fusion.90
  2365.3 126.5 %reduce-scatter.17.cloned.1.call-done = bf16[512,2048]{1,0:T(8,128)(2,1)} async-done(((bf16[2048,2048]{1,0:T(8,128)(2,1)}), bf16[512,2048]{1,0:T(8,128)(2,1)}) %reduce-scatter.17.cloned.1.call-update) | async-done | bytes 2097168 | tf_op jit(solution)/shard_map/reduce_scatter | solution.py:364
  2496.2 143.7 %reduce-scatter.23.cloned.1.call-done = bf16[512,2048]{1,0:T(8,128)(2,1)} async-done(((bf16[2048,2048]{1,0:T(8,128)(2,1)}), bf16[512,2048]{1,0:T(8,128)(2,1)}) %reduce-scatter.23.cloned.1.call-update) | async-done | bytes 2097168 | tf_op jit(solution)/shard_map/reduce_scatter | solution.py:367
  2639.9 148.0 %reduce-scatter.21.cloned.1.call-done = bf16[512,2048]{1,0:T(8,128)(2,1)} async-done(((bf16[2048,2048]{1,0:T(8,128)(2,1)}), bf16[512,2048]{1,0:T(8,128)(2,1)}) %reduce-scatter.21.cloned.1.call-update) | async-done | bytes 2097168 | tf_op jit(solution)/shard_map/reduce_scatter | solution.py:367
  2792.4 279.0 %reduce-scatter.35.cloned.1.call-done = bf16[1024,2048]{1,0:T(8,128)(2,1)} async-done(((bf16[4096,2048]{1,0:T(8,128)(2,1)}), bf16[1024,2048]{1,0:T(8,128)(2,1)}) %reduce-scatter.35.cloned.1.call-update) | async-done | bytes 4194320 | tf_op jit(solution)/shard_map/reduce_scatter | solution.py:376
  3071.4 283.4 %reduce-scatter.33.cloned.1.call-done = bf16[1024,2048]{1,0:T(8,128)(2,1)} async-done(((bf16[4096,2048]{1,0:T(8,128)(2,1)}), bf16[1024,2048]{1,0:T(8,128)(2,1)}) %reduce-scatter.33.cloned.1.call-update) | async-done | bytes 4194320 | tf_op jit(solution)/shard_map/reduce_scatter | solution.py:376
  3362.5 275.5 %reduce-scatter.27.cloned.1.call-done = bf16[512,4096]{1,0:T(8,128)(2,1)} async-done(((bf16[2048,4096]{1,0:T(8,128)(2,1)}), bf16[512,4096]{1,0:T(8,128)(2,1)}) %reduce-scatter.27.cloned.1.call-update) | async-done | bytes 4194320 | tf_op jit(solution)/shard_map/reduce_scatter | solution.py:370
  3638.0 283.4 %reduce-scatter.25.cloned.1.call-done = bf16[512,4096]{1,0:T(8,128)(2,1)} async-done(((bf16[2048,4096]{1,0:T(8,128)(2,1)}), bf16[512,4096]{1,0:T(8,128)(2,1)}) %reduce-scatter.25.cloned.1.call-update) | async-done | bytes 4194320 | tf_op jit(solution)/shard_map/reduce_scatter | solution.py:370
  3928.7 276.0 %reduce-scatter.31.cloned.1.call-done = bf16[512,4096]{1,0:T(8,128)(2,1)} async-done(((bf16[2048,4096]{1,0:T(8,128)(2,1)}), bf16[512,4096]{1,0:T(8,128)(2,1)}) %reduce-scatter.31.cloned.1.call-update) | async-done | bytes 4194320 | tf_op jit(solution)/shard_map/reduce_scatter | solution.py:373
  4204.7 283.4 %reduce-scatter.29.cloned.1.call-done = bf16[512,4096]{1,0:T(8,128)(2,1)} async-done(((bf16[2048,4096]{1,0:T(8,128)(2,1)}), bf16[512,4096]{1,0:T(8,128)(2,1)}) %reduce-scatter.29.cloned.1.call-update) | async-done | bytes 4194320 | tf_op jit(solution)/shard_map/reduce_scatter | solution.py:373
  4495.3 276.2 %reduce-scatter.39.cloned.1.call-done = bf16[512,4096]{1,0:T(8,128)(2,1)} async-done(((bf16[2048,4096]{1,0:T(8,128)(2,1)}), bf16[512,4096]{1,0:T(8,128)(2,1)}) %reduce-scatter.39.cloned.1.call-update) | async-done | bytes 4194320 | tf_op jit(solution)/shard_map/reduce_scatter | solution.py:379
  4771.5 283.4 %reduce-scatter.37.cloned.1.call-done = bf16[512,4096]{1,0:T(8,128)(2,1)} async-done(((bf16[2048,4096]{1,0:T(8,128)(2,1)}), bf16[512,4096]{1,0:T(8,128)(2,1)}) %reduce-scatter.37.cloned.1.call-update) | async-done | bytes 4194320 | tf_op jit(solution)/shard_map/reduce_scatter | solution.py:379
  5062.1 276.2 %reduce-scatter.43.cloned.1.call-done = bf16[512,4096]{1,0:T(8,128)(2,1)} async-done(((bf16[2048,4096]{1,0:T(8,128)(2,1)}), bf16[512,4096]{1,0:T(8,128)(2,1)}) %reduce-scatter.43.cloned.1.call-update) | async-done | bytes 4194320 | tf_op jit(solution)/shard_map/reduce_scatter | solution.py:382
  5338.3 283.5 %reduce-scatter.41.cloned.1.call-done = bf16[512,4096]{1,0:T(8,128)(2,1)} async-done(((bf16[2048,4096]{1,0:T(8,128)(2,1)}), bf16[512,4096]{1,0:T(8,128)(2,1)}) %reduce-scatter.41.cloned.1.call-update) | async-done | bytes 4194320 | tf_op jit(solution)/shard_map/reduce_scatter | solution.py:382
  5629.1 276.2 %reduce-scatter.47.cloned.1.call-done = bf16[1024,2048]{1,0:T(8,128)(2,1)} async-done(((bf16[4096,2048]{1,0:T(8,128)(2,1)}), bf16[1024,2048]{1,0:T(8,128)(2,1)}) %reduce-scatter.47.cloned.1.call-update) | async-done | bytes 4194320 | tf_op jit(solution)/shard_map/reduce_scatter | solution.py:385
  5905.3 283.4 %reduce-scatter.45.cloned.1.call-done = bf16[1024,2048]{1,0:T(8,128)(2,1)} async-done(((bf16[4096,2048]{1,0:T(8,128)(2,1)}), bf16[1024,2048]{1,0:T(8,128)(2,1)}) %reduce-scatter.45.cloned.1.call-update) | async-done | bytes 4194320 | tf_op jit(solution)/shard_map/reduce_scatter | solution.py:385
  6197.7 9.8 fusion.7
  6239.1 13.3 fusion.181
  6252.4 12.8 fusion.180
  6273.0 13.5 fusion.177
  6286.5 13.2 fusion.176
  6320.8 33.9 all-reduce.10
  6355.0 12.2 all-reduce.8
  6376.9 200.7 %all-reduce.13.cloned.1.call-done = (bf16[512,2048]{1,0:T(8,128)(2,1)}, bf16[512,2048]{1,0:T(8,128)(2,1)}, bf16[512,4096]{1,0:T(8,128)(2,1)}, bf16[512,4096]{1,0...) async-done(((bf16[512,2048]{1,0:T(8,128)(2,1)}, bf16[512,2048]{1,0:T(8,128)(2,1)}, ...) | async-done | bytes 29360144 | tf_op jit(solution)/shard_map/psum | solution.py:408
  (590 shorter events, 455.7 us)
Async XLA Ops:
  7.2 205.0 %all-gather.19.cloned.1.call-start = ((), (), s32[]{:S(2)}) async-start(), calls=%async_computation.23 | async-start | bytes 10485760 | tf_op jit(solution)/shard_map/all_gather | solution.py:330
  7.9 348.7 %all-gather.17.cloned.1.call-start = ((), (), s32[]{:S(2)}) async-start(), calls=%async_computation.22 | async-start | bytes 10485760 | tf_op jit(solution)/shard_map/all_gather | solution.py:329
  8.7 634.5 %all-gather.15.cloned.1.call-start = ((), (), s32[]{:S(2)}) async-start(), calls=%async_computation.21 | async-start | bytes 20971520 | tf_op jit(solution)/shard_map/all_gather | solution.py:331
  9.4 920.2 %all-gather.13.cloned.1.call-start = ((), (), s32[]{:S(2)}) async-start(), calls=%async_computation.20 | async-start | bytes 20971520 | tf_op jit(solution)/shard_map/all_gather | solution.py:332
  10.0 1206.0 %all-gather.21.cloned.1.call-start = ((), (), s32[]{:S(2)}) async-start(), calls=%async_computation.24 | async-start | bytes 20971520 | tf_op jit(solution)/shard_map/all_gather | solution.py:333
  10.6 1491.9 %all-gather.23.cloned.1.call-start = ((), (), s32[]{:S(2)}) async-start(), calls=%async_computation.25 | async-start | bytes 20971520 | tf_op jit(solution)/shard_map/all_gather | solution.py:334
  11.2 1777.9 %all-gather.25.cloned.1.call-start = ((), (), s32[]{:S(2)}) async-start(), calls=%async_computation.26 | async-start | bytes 20971520 | tf_op jit(solution)/shard_map/all_gather | solution.py:335
  17.5 85.2 %all-to-all-start = ((bf16[32,8,2048]{2,1,0:T(8,128)(2,1)}), bf16[32,8,2048]{2,1,0:T(8,128)(2,1)S(1)}, u32[]{:S(2)}, u32[]{:S(2)}) async-start(bf16[32,8,2048]{2,1,0:T(8,128)(2,1)} %bitcast.10), calls=%async_computation | async-start | bytes 2097152 | tf_op jit(solution)/shard_map/all_to_all | solution.py:294
  24.9 2050.7 %all-gather.27.cloned.1.call-start = ((), (), s32[]{:S(2)}) async-start(), calls=%async_computation.27 | async-start | bytes 20971520 | tf_op jit(solution)/shard_map/all_gather | solution.py:336
  101.4 276.6 %copy-start.154 = (f32[8]{0:T(128)}, f32[8]{0:T(128)S(1)}, u32[]{:S(2)}) copy-start(f32[8]{0:T(128)S(1)} %subtract_log_fusion) | copy-start | bytes 100
  102.7 103.5 %all-to-all-start.2 = ((bf16[32,8,2048]{2,1,0:T(8,128)(2,1)}), bf16[32,8,2048]{2,1,0:T(8,128)(2,1)}, u32[]{:S(2)}, u32[]{:S(2)}) async-start(bf16[32,8,2048]{2,1,0:T(8,128)(2,1)} %bitcast.30), calls=%async_computation.2 | async-start | bytes 2097152 | tf_op jit(solution)/shard_map/all_to_all | solution.py:301
  108.4 2256.8 %reduce-scatter.19.cloned.1.call-start = ((), (), s32[]{:S(2)}) async-start(), calls=%async_computation.29 | async-start | bytes 10485760 | tf_op jit(solution)/shard_map/reduce_scatter | solution.py:364
  176.5 2120.9 %copy-start.19 = (f32[4,1,512]{2,1,0:T(1,128)}, f32[4,1,512]{2,1,0:T(1,128)S(1)}, u32[]{:S(2)}) copy-start(f32[4,1,512]{2,1,0:T(1,128)S(1)} %convert_element_type.556) | copy-start | bytes 24580
  201.8 176.3 %copy-start.135 = (pred[128,128]{1,0:T(8,128)(4,1)}, pred[128,128]{1,0:T(8,128)(4,1)S(1)}, u32[]{:S(2)}) copy-start(pred[128,128]{1,0:T(8,128)(4,1)S(1)} %fusion.102) | copy-start | bytes 49156
  202.6 175.5 %copy-start.116 = (f32[128,128]{1,0:T(8,128)}, f32[128,128]{1,0:T(8,128)S(1)}, u32[]{:S(2)}) copy-start(f32[128,128]{1,0:T(8,128)S(1)} %select_convert_fusion) | copy-start | bytes 196612
  203.8 175.4 %copy-start.89 = (f32[128,128]{1,0:T(8,128)}, f32[128,128]{1,0:T(8,128)S(1)}, u32[]{:S(2)}) copy-start(f32[128,128]{1,0:T(8,128)S(1)} %get-tuple-element.113) | copy-start | bytes 196612
  203.8 175.4 %copy-start.91 = (f32[128,128]{1,0:T(8,128)}, f32[128,128]{1,0:T(8,128)S(1)}, u32[]{:S(2)}) copy-start(f32[128,128]{1,0:T(8,128)S(1)} %get-tuple-element.114) | copy-start | bytes 196612
  206.2 2091.1 %copy-start.2 = (bf16[256,2048]{1,0:T(8,128)(2,1)}, bf16[256,2048]{1,0:T(8,128)(2,1)S(1)}, u32[]{:S(2)}) copy-start(bf16[256,2048]{1,0:T(8,128)(2,1)S(1)} %scatter_custom_fusion.1) | copy-start | bytes 3145732
  211.1 160.0 %copy-start.101 = (f32[128]{0:T(128)}, f32[128]{0:T(128)S(1)}, u32[]{:S(2)}) copy-start(f32[128]{0:T(128)S(1)} %broadcast_multiply_fusion.5) | copy-start | bytes 1540
  211.1 145.4 %copy-start.96 = (f32[128]{0:T(128)}, f32[128]{0:T(128)S(1)}, u32[]{:S(2)}) copy-start(f32[128]{0:T(128)S(1)} %broadcast_multiply_fusion.3) | copy-start | bytes 1540
  212.1 159.0 %copy-start.110 = (f32[128]{0:T(128)}, f32[128]{0:T(128)S(1)}, u32[]{:S(2)}) copy-start(f32[128]{0:T(128)S(1)} %fusion.117) | copy-start | bytes 1540
  378.7 272.8 %copy-start.77 = (bf16[8,128,128]{2,1,0:T(8,128)(2,1)}, bf16[8,128,128]{2,1,0:T(8,128)(2,1)S(1)}, u32[]{:S(2)}) copy-start(bf16[8,128,128]{2,1,0:T(8,128)(2,1)S(1)} %fusion.41) | copy-start | bytes 786436
  379.7 271.8 %copy-start.81 = (bf16[128,8,128]{2,0,1:T(8,128)(2,1)}, bf16[128,8,128]{2,0,1:T(8,128)(2,1)S(1)}, u32[]{:S(2)}) copy-start(bf16[128,8,128]{2,0,1:T(8,128)(2,1)S(1)} %get-tuple-element.102) | copy-start | bytes 786436
  379.7 271.8 %copy-start.83 = (bf16[128,8,128]{2,0,1:T(8,128)(2,1)}, bf16[128,8,128]{2,0,1:T(8,128)(2,1)S(1)}, u32[]{:S(2)}) copy-start(bf16[128,8,128]{2,0,1:T(8,128)(2,1)S(1)} %get-tuple-element.103) | copy-start | bytes 786436
  379.7 263.5 %copy-start.97 = (f32[128]{0:T(128)S(1)}, f32[128]{0:T(128)}, u32[]{:S(2)}) copy-start(f32[128]{0:T(128)} %copy-done.96) | copy-start | bytes 1540
  379.7 263.5 %copy-start.106 = (f32[128]{0:T(128)S(1)}, f32[128]{0:T(128)}, u32[]{:S(2)}) copy-start(f32[128]{0:T(128)} %copy-done.105) | copy-start | bytes 1540
  381.0 284.4 %copy-start.79 = (bf16[8,128,128]{2,1,0:T(8,128)(2,1)}, bf16[8,128,128]{2,1,0:T(8,128)(2,1)S(1)}, u32[]{:S(2)}) copy-start(bf16[8,128,128]{2,1,0:T(8,128)(2,1)S(1)} %fusion.40) | copy-start | bytes 786436
  667.9 261.7 %copy-start.102 = (f32[128]{0:T(128)S(1)}, f32[128]{0:T(128)}, u32[]{:S(2)}) copy-start(f32[128]{0:T(128)} %copy-done.101) | copy-start | bytes 1540
  667.9 261.7 %copy-start.111 = (f32[128]{0:T(128)S(1)}, f32[128]{0:T(128)}, u32[]{:S(2)}) copy-start(f32[128]{0:T(128)} %copy-done.110) | copy-start | bytes 1540
  1810.3 265.3 %copy-start.127 = (pred[128]{0:T(512)(128)(4,1)S(1)}, pred[128]{0:T(512)(128)(4,1)}, u32[]{:S(2)}) copy-start(pred[128]{0:T(512)(128)(4,1)} %copy-done.126) | copy-start | bytes 388
  2201.0 290.8 %reduce-scatter.17.cloned.1.call-start = ((), (), s32[]{:S(2)}) async-start(), calls=%async_computation.28 | async-start | bytes 10485760 | tf_op jit(solution)/shard_map/reduce_scatter | solution.py:364
  2233.3 406.7 %reduce-scatter.23.cloned.1.call-start = ((), (), s32[]{:S(2)}) async-start(), calls=%async_computation.31 | async-start | bytes 10485760 | tf_op jit(solution)/shard_map/reduce_scatter | solution.py:367
  2240.7 547.2 %reduce-scatter.21.cloned.1.call-start = ((), (), s32[]{:S(2)}) async-start(), calls=%async_computation.30 | async-start | bytes 10485760 | tf_op jit(solution)/shard_map/reduce_scatter | solution.py:367
  2248.0 823.4 %reduce-scatter.35.cloned.1.call-start = ((), (), s32[]{:S(2)}) async-start(), calls=%async_computation.37 | async-start | bytes 20971520 | tf_op jit(solution)/shard_map/reduce_scatter | solution.py:376
  2257.5 1097.3 %reduce-scatter.33.cloned.1.call-start = ((), (), s32[]{:S(2)}) async-start(), calls=%async_computation.36 | async-start | bytes 20971520 | tf_op jit(solution)/shard_map/reduce_scatter | solution.py:376
  2267.3 1370.7 %reduce-scatter.27.cloned.1.call-start = ((), (), s32[]{:S(2)}) async-start(), calls=%async_computation.33 | async-start | bytes 20971520 | tf_op jit(solution)/shard_map/reduce_scatter | solution.py:370
  2277.7 1643.7 %reduce-scatter.25.cloned.1.call-start = ((), (), s32[]{:S(2)}) async-start(), calls=%async_computation.32 | async-start | bytes 20971520 | tf_op jit(solution)/shard_map/reduce_scatter | solution.py:370
  2287.8 1916.9 %reduce-scatter.31.cloned.1.call-start = ((), (), s32[]{:S(2)}) async-start(), calls=%async_computation.35 | async-start | bytes 20971520 | tf_op jit(solution)/shard_map/reduce_scatter | solution.py:373
  2297.3 2190.8 %reduce-scatter.29.cloned.1.call-start = ((), (), s32[]{:S(2)}) async-start(), calls=%async_computation.34 | async-start | bytes 20971520 | tf_op jit(solution)/shard_map/reduce_scatter | solution.py:373
  2306.8 2464.7 %reduce-scatter.39.cloned.1.call-start = ((), (), s32[]{:S(2)}) async-start(), calls=%async_computation.39 | async-start | bytes 20971520 | tf_op jit(solution)/shard_map/reduce_scatter | solution.py:379
  2316.5 2738.4 %reduce-scatter.37.cloned.1.call-start = ((), (), s32[]{:S(2)}) async-start(), calls=%async_computation.38 | async-start | bytes 20971520 | tf_op jit(solution)/shard_map/reduce_scatter | solution.py:379
  2326.1 3012.2 %reduce-scatter.43.cloned.1.call-start = ((), (), s32[]{:S(2)}) async-start(), calls=%async_computation.41 | async-start | bytes 20971520 | tf_op jit(solution)/shard_map/reduce_scatter | solution.py:382
  2335.7 3286.2 %reduce-scatter.41.cloned.1.call-start = ((), (), s32[]{:S(2)}) async-start(), calls=%async_computation.40 | async-start | bytes 20971520 | tf_op jit(solution)/shard_map/reduce_scatter | solution.py:382
  2345.3 3560.0 %reduce-scatter.47.cloned.1.call-start = ((), (), s32[]{:S(2)}) async-start(), calls=%async_computation.43 | async-start | bytes 20971520 | tf_op jit(solution)/shard_map/reduce_scatter | solution.py:385
  2355.3 3833.4 %reduce-scatter.45.cloned.1.call-start = ((), (), s32[]{:S(2)}) async-start(), calls=%async_computation.42 | async-start | bytes 20971520 | tf_op jit(solution)/shard_map/reduce_scatter | solution.py:385
  2364.8 4212.7 %all-reduce.13.cloned.1.call-start = ((), (), s32[]{:S(2)}) async-start(), calls=%async_computation.44 | async-start | bytes 58720256 | tf_op jit(solution)/shard_map/psum | solution.py:408
  6218.5 95.1 %all-to-all-start.1 = ((bf16[32,8,2048]{2,1,0:T(8,128)(2,1)}), bf16[32,8,2048]{2,1,0:T(8,128)(2,1)}, u32[]{:S(2)}, u32[]{:S(2)}) async-start(bf16[32,8,2048]{2,1,0:T(8,128)(2,1)} %bitcast.28), calls=%async_computation.1 | async-start | bytes 2097152 | tf_op jit(solution)/shard_map/all_to_all | solution.py:424
  6313.6 59.7 all-to-all-start.3
  (146 other events, 1311.0 us)
Sparse Core Ops, SparseCore 0:
  9.6 197.5 all-gather.18
  208.7 147.7 all-gather.16
  358.2 284.9 all-gather.14
  644.6 284.9 all-gather.12
  931.0 284.9 all-gather.20
  1217.4 284.9 all-gather.22
  1504.0 284.9 all-gather.24
  1790.6 284.9 all-gather.26
  2201.1 142.6 reduce-scatter.18
  2346.5 145.1 reduce-scatter.16
  2494.7 145.1 reduce-scatter.22
  2642.7 145.1 reduce-scatter.20
  2790.3 281.0 reduce-scatter.34
  3073.7 281.0 reduce-scatter.32
  3357.0 281.0 reduce-scatter.26
  3640.4 281.0 reduce-scatter.24
  3923.6 281.0 reduce-scatter.30
  4207.0 281.0 reduce-scatter.28
  4490.4 281.0 reduce-scatter.38
  4773.8 281.0 reduce-scatter.36
  5057.3 281.0 reduce-scatter.42
  5340.8 281.0 reduce-scatter.40
  5624.2 281.0 reduce-scatter.46
  5907.6 281.0 reduce-scatter.44
  6196.6 380.8 all-reduce.12
where the time goes:
time: 6630 us; the launch traced here: 6620 us
  waiting for transfers between devices  5710 us (86%)
  matrix products  461 us (7%)
  other arithmetic  179 us (3%)
  blocking collectives  150 us (2%)
  local copies, waits for them, and re-layouts  73 us (1%)
    reduce_scatter x2, waiting for transfers between devices, local(): lax.psum_scatter(full_parts[4].astype(jnp.bfloat16), 'shard', scatter_dim...  562 us
    reduce_scatter x2, waiting for transfers between devices, local(): lax.psum_scatter(full_parts[6].astype(jnp.bfloat16), 'shard', scatter_dim...  560 us
    reduce_scatter x2, waiting for transfers between devices, local(): lax.psum_scatter(full_parts[7].astype(jnp.bfloat16), 'shard', scatter_dim...  560 us
    reduce_scatter x2, waiting for transfers between devices, local(): lax.psum_scatter(full_parts[5].astype(jnp.bfloat16), 'shard', scatter_dim...  560 us
    reduce_scatter x2, waiting for transfers between devices, local(): lax.psum_scatter(full_parts[3].astype(jnp.bfloat16), 'shard', scatter_dim...  559 us
    reduce_scatter x2, waiting for transfers between devices, local(): lax.psum_scatter(full_parts[2].astype(jnp.bfloat16), 'shard', scatter_dim...  559 us
    reduce_scatter x2, waiting for transfers between devices, local(): lax.psum_scatter(full_parts[1].astype(jnp.bfloat16), 'shard', scatter_dim...  292 us
    all_gather x1, waiting for transfers between devices, local(): lax.all_gather(up_weight, 'shard', axis=0, tiled=True)  277 us
  transfers between devices with their start and end apart: 29, of which 23 were waited for; matrix products, arithmetic and copies ran while one was open for 8% of the time, Pallas kernels for 0%

commit v1 on v0

v1 whole, which is shorter than its diff:
```python
import functools
import math

import jax
import jax.numpy as jnp
from jax import lax
from jax.sharding import Mesh, PartitionSpec as P

HEADS = 8
KH = 256

layer_epsilon = 1e-05
head_epsilon = 1.0
rotary_base = 10000.0
bf16 = jnp.bfloat16
f32 = jnp.float32


def norm_rows(inputs, gain, shift):
    average = jnp.mean(inputs, axis=-1, keepdims=True)
    centred = inputs - average
    spread = jnp.mean(centred * centred, axis=-1, keepdims=True)
    return centred * lax.rsqrt(spread + layer_epsilon) * gain + shift


def norm_rows_back(inputs, gain, back):
    average = jnp.mean(inputs, axis=-1, keepdims=True)
    centred = inputs - average
    spread = jnp.mean(centred * centred, axis=-1, keepdims=True)
    root = lax.rsqrt(spread + layer_epsilon)
    unit = centred * root
    e = back * gain
    through = root * (
        e - jnp.mean(e, axis=-1, keepdims=True) - unit * jnp.mean(e * unit, axis=-1, keepdims=True)
    )
    return through, jnp.sum(back * unit, axis=0), jnp.sum(back, axis=0)


def head_norm(retained):
    average = jnp.mean(retained, axis=-1, keepdims=True)
    centred = retained - average
    spread = jnp.mean(centred * centred, axis=-1, keepdims=True)
    root = lax.rsqrt(spread + head_epsilon)
    return centred * root, root


def rotate(heads_in, cosine_table, sine_table):
    half_size = heads_in.shape[-1] // 2
    former = heads_in[..., :half_size]
    latter = heads_in[..., half_size:]
    return jnp.concatenate(
        [former * cosine_table - latter * sine_table, former * sine_table + latter * cosine_table],
        axis=-1,
    )


def rotate_back(heads_in, cosine_table, sine_table):
    return rotate(heads_in, cosine_table, -sine_table)


def pack_tables(lengths, pack_rows, head_ids):
    entries = lengths.shape[1]
    slot_ids = jnp.arange(pack_rows, dtype=jnp.int32)
    seq_ends = jnp.cumsum(lengths, axis=1, dtype=jnp.int32)
    seq_starts = seq_ends - lengths
    segment = jnp.sum(
        (slot_ids[None, :, None] >= seq_ends[:, None, :]).astype(jnp.int32), axis=2, dtype=jnp.int32
    )
    owners = segment[:, :, None] == jnp.arange(entries, dtype=jnp.int32)[None, None, :]
    begins = jnp.sum(jnp.where(owners, seq_starts[:, None, :], 0), axis=2, dtype=jnp.int32)
    places = (slot_ids[None, :] - begins).astype(f32)
    usable = segment < entries - 1
    half_size = KH // 2
    frequency = jnp.power(
        f32(rotary_base), -jnp.arange(half_size, dtype=f32) / f32(half_size - 1)
    )
    angles = places[:, :, None] * frequency
    cosine_table = jnp.cos(angles)
    sine_table = jnp.sin(angles)
    lag_steps = slot_ids[:, None] - slot_ids[None, :]
    linked = (
        (segment[:, :, None] == segment[:, None, :])
        & (lag_steps[None] >= 0)
        & usable[:, None, :]
    )
    log_rates = jnp.log(1.0 - jnp.power(f32(2.0), -5.0 - head_ids.astype(f32)))
    powers = jnp.exp(log_rates[:, None, None] * jnp.maximum(lag_steps, 0).astype(f32)[None])
    decays = jnp.where(linked[None], powers[:, None], f32(0.0))
    return cosine_table, sine_table, decays, usable


def gram_rows(leading, trailing):
    return lax.dot_general(
        leading, trailing, (((0,), (0,)), ((), ())), preferred_element_type=f32
    )


def back_through(incoming, matrix):
    return lax.dot_general(
        incoming, matrix, (((1,), (1,)), ((), ())), preferred_element_type=f32
    )


def forward_dot(inputs, matrix):
    return jnp.dot(inputs, matrix, preferred_element_type=f32)


def gelu_parts(v):
    c = f32(math.sqrt(2.0 / math.pi))
    t = jnp.tanh(c * (v + 0.044715 * v * v * v))
    value = 0.5 * v * (1.0 + t)
    slope = 0.5 * (1.0 + t) + 0.5 * v * (1.0 - t * t) * c * (1.0 + 3.0 * 0.044715 * v * v)
    return value, slope


def local(
    tokens,
    cotangent,
    token_order,
    lengths,
    query_weight,
    key_weight,
    value_weight,
    gate_weight,
    out_weight,
    gelu_weight,
    up_weight,
    down_weight,
    gain_one,
    shift_one,
    gain_two,
    shift_two,
):
    every = ("outer", "tp", "shard")
    device_count = lax.axis_size(every)
    device_index = lax.axis_index(every)
    outer, tp, shards = lax.axis_size("outer"), lax.axis_size("tp"), lax.axis_size("shard")
    t, z = lax.axis_index("tp"), lax.axis_index("shard")
    rows, width = tokens.shape
    packs = lengths.shape[0]
    pack_rows = rows // packs
    heads = HEADS // tp
    group_rows = tp * rows
    group_packs = tp * packs

    own_order = lax.dynamic_slice_in_dim(token_order, device_index * rows, rows)
    target = own_order // rows
    places = jnp.arange(rows, dtype=jnp.int32)
    before = (target[None, :] < target[:, None]) | (
        (target[None, :] == target[:, None]) & (places[None, :] < places[:, None])
    )
    send_place = jnp.sum(before.astype(jnp.int32), axis=1)
    send_mix = (send_place[None, :] == places[:, None]).astype(bf16)
    loader_ids = jnp.arange(token_order.shape[0], dtype=jnp.int32)
    slot_targets = device_index * rows + places
    origin = jnp.sum(
        jnp.where(token_order[None, :] == slot_targets[:, None], loader_ids[None, :], 0), axis=1
    )
    arrive_place = jnp.sum((origin[None, :] < origin[:, None]).astype(jnp.int32), axis=1)
    work_mix = (arrive_place[:, None] == places[None, :]).astype(bf16)

    def exchange(value):
        return lax.all_to_all(
            value.reshape(device_count, rows // device_count, width),
            every,
            split_axis=0,
            concat_axis=0,
            tiled=True,
        ).reshape(rows, width)

    work_tokens = forward_dot(work_mix, exchange(forward_dot(send_mix, tokens).astype(bf16)))
    work_cotangent = forward_dot(
        work_mix, exchange(forward_dot(send_mix, cotangent).astype(bf16))
    )

    def along_z(piece):
        return lax.all_gather(piece, "shard", axis=0, tiled=True)

    def columns(weight):
        part = weight.shape[1] // tp
        return along_z(lax.dynamic_slice_in_dim(weight, t * part, part, axis=1))

    small = along_z(jnp.stack([gain_one, shift_one, gain_two, shift_two])[None])
    small = jnp.transpose(small, (1, 0, 2)).reshape(4, width).astype(f32)
    gain_1, shift_1, gain_2, shift_2 = small[0], small[1], small[2], small[3]
    all_lengths = lax.all_gather(lengths, "tp", axis=0, tiled=True)
    head_ids = t * heads + jnp.arange(heads, dtype=jnp.int32)
    cosine, sine, decays, usable_all = pack_tables(all_lengths, pack_rows, head_ids)
    usable = lax.dynamic_slice_in_dim(usable_all, t * packs, packs).reshape(rows, 1)

    wq, wk, wv, wg = (columns(w) for w in (query_weight, key_weight, value_weight, gate_weight))
    out_local = out_weight.shape[0]
    out_all = out_local * shards
    out_part = out_all // tp
    spread_rows = jnp.arange(out_part, dtype=jnp.int32) + t * out_part
    held = jnp.clip(t * out_part - z * out_local, 0, max(out_local - out_part, 0))
    if out_part <= out_local:
        piece = lax.dynamic_slice_in_dim(out_weight, held, out_part, axis=0)
        mine = (t * out_part) // out_local == z
        wo = lax.psum(jnp.where(mine, piece, jnp.zeros((), bf16)), "shard")
    else:
        whole = jnp.zeros((out_all, out_weight.shape[1]), bf16)
        whole = lax.dynamic_update_slice_in_dim(whole, out_weight, z * out_local, axis=0)
        wo = lax.psum(lax.dynamic_slice_in_dim(whole, t * out_part, out_part, axis=0), "shard")

    unit_local = down_weight.shape[0]
    unit = unit_local // tp

    def unit_columns(weight):
        cut = weight.reshape(weight.shape[0], shards, tp, unit)
        cut = lax.dynamic_slice_in_dim(cut, t, 1, axis=2)
        return along_z(cut.reshape(weight.shape[0], shards * unit))

    w_gelu, w_up = unit_columns(gelu_weight), unit_columns(up_weight)
    w_down = along_z(lax.dynamic_slice_in_dim(down_weight, t * unit, unit, axis=0))

    def gather_rows(value):
        return lax.all_gather(value, "tp", axis=0, tiled=True)

    def scatter_rows(value):
        return lax.psum_scatter(
            value.astype(bf16), "tp", scatter_dimension=0, tiled=True
        ).astype(f32)

    def per_head(value):
        return value.reshape(group_packs, pack_rows, heads, -1)

    inputs = work_tokens
    normed = gather_rows(norm_rows(inputs, gain_1, shift_1).astype(bf16))
    cos_t, sin_t = cosine[:, :, None, :], sine[:, :, None, :]
    q_rot = rotate(per_head(forward_dot(normed, wq)), cos_t, sin_t).astype(bf16)
    k_rot = (rotate(per_head(forward_dot(normed, wk)), cos_t, sin_t) * KH ** (-0.5)).astype(bf16)
    v_low = per_head(forward_dot(normed, wv)).astype(bf16)
    gating = per_head(forward_dot(normed, wg))
    scores = jnp.einsum("bihd,bjhd->hbij", q_rot, k_rot, preferred_element_type=f32)
    weights_low = (scores * decays).astype(bf16)
    retained = jnp.einsum("hbij,bjhe->bihe", weights_low, v_low, preferred_element_type=f32)
    unit_retained, root_retained = head_norm(retained)
    sigma = jax.nn.sigmoid(gating)
    silu = gating * sigma
    branch = (silu * unit_retained).astype(bf16).reshape(group_rows, -1)
    middle = inputs + scatter_rows(forward_dot(branch, wo))
    normed_two = gather_rows(norm_rows(middle, gain_2, shift_2).astype(bf16))
    gelu_in = forward_dot(normed_two, w_gelu)
    up_proj = forward_dot(normed_two, w_up)
    gelu_value, gelu_slope = gelu_parts(gelu_in)
    hidden = (gelu_value * up_proj).astype(bf16)
    ending = jnp.where(usable, middle + scatter_rows(forward_dot(hidden, w_down)), 0.0).astype(bf16)

    back_out = jnp.where(usable, work_cotangent, 0.0)
    back_low = gather_rows(back_out.astype(bf16))
    back_hidden = back_through(back_low, w_down)
    gelu_low = (back_hidden * up_proj * gelu_slope).astype(bf16)
    up_low = (back_hidden * gelu_value).astype(bf16)
    back_normed_two = scatter_rows(back_through(gelu_low, w_gelu) + back_through(up_low, w_up))
    through_two, gain_two_part, shift_two_part = norm_rows_back(middle, gain_2, back_normed_two)
    back_middle = back_out + through_two
    middle_low = gather_rows(back_middle.astype(bf16))
    back_branch = back_through(middle_low, wo).reshape(group_packs, pack_rows, heads, -1)
    gating_low = (
        back_branch * unit_retained * (sigma * (1.0 + gating * (1.0 - sigma)))
    ).astype(bf16)
    e = back_branch * silu
    retained_low = (
        root_retained
        * (
            e
            - jnp.mean(e, axis=-1, keepdims=True)
            - unit_retained * jnp.mean(e * unit_retained, axis=-1, keepdims=True)
        )
    ).astype(bf16)
    back_weights = jnp.einsum("bihe,bjhe->hbij", retained_low, v_low, preferred_element_type=f32)
    values_low = jnp.einsum(
        "hbij,bihe->bjhe", weights_low, retained_low, preferred_element_type=f32
    ).astype(bf16)
    back_scores = (back_weights * decays).astype(bf16)
    back_queries = jnp.einsum("hbij,bjhd->bihd", back_scores, k_rot, preferred_element_type=f32)
    back_keys = jnp.einsum("hbij,bihd->bjhd", back_scores, q_rot, preferred_element_type=f32)
    queries_low = rotate_back(back_queries, cos_t, sin_t).astype(bf16)
    keys_low = (rotate_back(back_keys, cos_t, sin_t) * KH ** (-0.5)).astype(bf16)
    queries_low, keys_low, values_low, gating_low = (
        v.reshape(group_rows, -1) for v in (queries_low, keys_low, values_low, gating_low)
    )
    back_normed = scatter_rows(
        back_through(queries_low, wq)
        + back_through(keys_low, wk)
        + back_through(values_low, wv)
        + back_through(gating_low, wg)
    )
    through_one, gain_one_part, shift_one_part = norm_rows_back(inputs, gain_1, back_normed)
    back_inputs = (back_middle + through_one).astype(bf16)

    def settle(value):
        return lax.psum(value, "outer") if outer > 1 else value

    def column_gradient(left, right):
        part = lax.psum_scatter(
            gram_rows(left, right).astype(bf16), "shard", scatter_dimension=0, tiled=True
        )
        return settle(part)

    def by_columns(left, right):
        return lax.all_gather(
            column_gradient(left, right), "tp", axis=1, tiled=True
        ).astype(f32)

    def by_units(left, right):
        part = column_gradient(left, right).reshape(-1, shards, unit)
        gathered = lax.all_gather(part, "tp", axis=0)
        return jnp.transpose(gathered, (1, 2, 0, 3)).reshape(part.shape[0], -1).astype(f32)

    down_gradient = lax.all_gather(
        column_gradient(hidden, back_low), "tp", axis=0, tiled=True
    ).astype(f32)
    gelu_gradient = by_units(normed_two, gelu_low)
    up_gradient = by_units(normed_two, up_low)
    out_part_sum = settle(lax.psum(gram_rows(branch, middle_low).astype(bf16), "shard"))
    placed = jnp.zeros((out_all, width), bf16)
    placed = lax.dynamic_update_slice_in_dim(placed, out_part_sum, t * out_part, axis=0)
    out_gradient = lax.psum(
        lax.dynamic_slice_in_dim(placed, z * out_local, out_local, axis=0), "tp"
    ).astype(f32)
    query_gradient = by_columns(normed, queries_low)
    key_gradient = by_columns(normed, keys_low)
    value_gradient = by_columns(normed, values_low)
    gate_gradient = by_columns(normed, gating_low)
    smalls = jnp.stack([gain_one_part, shift_one_part, gain_two_part, shift_two_part])
    smalls = lax.psum(smalls, every)
    smalls = lax.dynamic_slice_in_dim(smalls, z * (width // shards), width // shards, axis=1)

    def give_back(value):
        home = exchange(gram_rows(work_mix, value).astype(bf16))
        return gram_rows(send_mix, home).astype(bf16)

    result = give_back(ending)
    token_gradient = give_back(back_inputs)
    return (
        result,
        token_gradient,
        query_gradient,
        key_gradient,
        value_gradient,
        gate_gradient,
        out_gradient,
        gelu_gradient,
        up_gradient,
        down_gradient,
        smalls[0],
        smalls[1],
        smalls[2],
        smalls[3],
    )


def solution(mesh):
    tp = math.gcd(mesh.shape["rep"], HEADS)
    grid = mesh.devices.reshape(mesh.shape["rep"] // tp, tp, mesh.shape["shard"])
    cube = Mesh(grid, ("outer", "tp", "shard"))
    tokens_at = P(("outer", "tp", "shard"), None)
    weights_at = P("shard", None)
    vectors_at = P("shard")
    in_specs = (tokens_at, tokens_at, P(), tokens_at) + (weights_at,) * 8 + (vectors_at,) * 4
    out_specs = (tokens_at, tokens_at) + (weights_at,) * 8 + (vectors_at,) * 4
    return jax.shard_map(local, mesh=cube, in_specs=in_specs, out_specs=out_specs, check_vma=False)
```

time: 6630 us -> 1800 us (0.27)
  waiting for transfers between devices: 5710 us -> 1230 us
  matrix products: 461 us -> 249 us
  other arithmetic: 179 us -> 88.9 us
    reduce_scatter x16 -> x11, waiting for transfers between devices: 3780 us -> 420 us  [the longest x4 277 us: scatter_rows(): lax.psum_scatter(value.astype(bf16), 'tp', scatter_dimension=0, tiled=True)]
    all_gather x8 -> x18, waiting for transfers between devices: 1730 us -> 522 us  [the longest x4 168 us: gather_rows(): return lax.all_gather(value, 'tp', axis=0, tiled=True)]
    dot_general x16 -> x8, matrix products: 199 us -> 92.3 us  [back_through(): lax.dot_general(incoming, matrix, (((1,), (1,)), ((), ())), preferred_ele...]
    dot_general x28 -> x18, matrix products: 138 us -> 84.5 us  [the longest x12 79.4 us: forward_dot(): return jnp.dot(inputs, matrix, preferred_element_type=f32)]
    psum x1 -> x3, waiting for transfers between devices: 201 us -> 240 us  [the longest x1 85.7 us: local(): lax.psum(gram_rows(branch, middle_low).astype(bf16), 'shard')]
  transfers between devices with their start and end apart: 29 -> 36, of which waited for: 23 -> 29; matrix products, arithmetic and copies ran while one was open for 8% -> 20% of each run, Pallas kernels for 0% -> 0%
where the time goes in v1:
time: 1800 us; the launch traced here: 1790 us
  waiting for transfers between devices  1230 us (68%)
  matrix products  249 us (14%)
  blocking collectives  95.3 us (5%)
  other arithmetic  88.9 us (5%)
  local copies, waits for them, and re-layouts  84 us (5%)
  starting transfers between devices  23.6 us (1%)
    reduce_scatter x4, waiting for transfers between devices, scatter_rows(): lax.psum_scatter(value.astype(bf16), 'tp', scatter_dimension=0, tiled=True)  277 us
    all_gather x4, waiting for transfers between devices, gather_rows(): return lax.all_gather(value, 'tp', axis=0, tiled=True)  168 us
    all_gather x7, waiting for transfers between devices, along_z(): return lax.all_gather(piece, 'shard', axis=0, tiled=True)  165 us
    reduce_scatter x7, waiting for transfers between devices, column_gradient(): lax.psum_scatter(gram_rows(left, right).astype(bf16), 'shard', scatter_di...  144 us
    all_gather x4, waiting for transfers between devices, by_columns(): lax.all_gather(column_gradient(left, right), 'tp', axis=1, tiled=True)  117 us
    dot_general x8, matrix products, back_through(): lax.dot_general(incoming, matrix, (((1,), (1,)), ((), ())), preferred_ele...  92.3 us
    psum x1, waiting for transfers between devices, local(): lax.psum(gram_rows(branch, middle_low).astype(bf16), 'shard')  85.7 us
    dot_general x12, matrix products, forward_dot(): return jnp.dot(inputs, matrix, preferred_element_type=f32)  79.4 us
  transfers between devices with their start and end apart: 36, of which 29 were waited for; matrix products, arithmetic and copies ran while one was open for 20% of the time, Pallas kernels for 0%

profile of v1, /device:TPU:0, one launch (start us, length us, event | category | flops | bytes accessed | tf_op | source)
XLA Modules:
  0.0 1786.5 jit_solution(1845267454275269753)
XLA Ops:
  19.3 47.1 %all-gather.2 = bf16[4,4,512]{2,1,0:T(4,128)(2,1)S(1)} all-gather(bf16[1,4,512]{2,1,0:T(4,128)(2,1)S(1)} %maximum_bitcast_fusion), channel_id=2, replica_groups=mesh['rep'=8,'shard'=4] {'shard'}, dimensions={0}, use_global_device_ids=true | all-gather | bytes 20480 | tf_op jit(solution)/shard_map/all_gather | solution.py:177
  80.7 8.6 all-gather.1
  90.1 34.1 %all-gather.22.cloned.1.call-done = bf16[2048,2048]{1,0:T(8,128)(2,1)} async-done(((bf16[256,2048]{1,0:T(8,128)(2,1)}), bf16[2048,2048]{1,0:T(8,128)(2,1)}) %all-gather.22.cloned.1.call-update) | async-done | bytes 8388624 | tf_op jit(solution)/shard_map/all_gather | solution.py:218
  131.5 22.8 %all-gather.28.cloned.1.call-done = bf16[2048,256]{1,0:T(8,128)(2,1)} async-done(((bf16[512,256]{1,0:T(8,128)(2,1)}), bf16[2048,256]{1,0:T(8,128)(2,1)}) %all-gather.28.cloned.1.call-update) | async-done | bytes 1048592 | tf_op jit(solution)/shard_map/all_gather | solution.py:177
  167.6 34.1 %all-gather.26.cloned.1.call-done = bf16[2048,512]{1,0:T(8,128)(2,1)} async-done(((bf16[512,512]{1,0:T(8,128)(2,1)}), bf16[2048,512]{1,0:T(8,128)(2,1)}) %all-gather.26.cloned.1.call-update) | async-done | bytes 2097168 | tf_op jit(solution)/shard_map/all_gather | solution.py:177
  201.7 8.5 convolution_convert_fusion.8
  213.6 35.3 %all-gather.24.cloned.1.call-done = bf16[2048,512]{1,0:T(8,128)(2,1)} async-done(((bf16[512,512]{1,0:T(8,128)(2,1)}), bf16[2048,512]{1,0:T(8,128)(2,1)}) %all-gather.24.cloned.1.call-update) | async-done | bytes 2097168 | tf_op jit(solution)/shard_map/all_gather | solution.py:177
  248.8 10.9 multiply_convert_fusion.4
  259.8 77.1 %all-reduce.4.cloned.1.call-done = bf16[512,2048]{1,0:T(8,128)(2,1)} async-done(((bf16[512,2048]{1,0:T(8,128)(2,1)}), bf16[512,2048]{1,0:T(8,128)(2,1)}) %all-reduce.4.cloned.1.call-update) | async-done | bytes 2097168 | tf_op jit(solution)/shard_map/psum | solution.py:200
  336.9 10.1 convolution_convert_fusion.1
  355.7 61.8 %reduce-scatter.12.cloned.1.call-done = bf16[256,2048]{1,0:T(8,128)(2,1)} async-done(((bf16[2048,2048]{1,0:T(8,128)(2,1)}), bf16[256,2048]{1,0:T(8,128)(2,1)}) %reduce-scatter.12.cloned.1.call-update) | async-done | bytes 1048592 | tf_op jit(solution)/shard_map/reduce_scatter | solution.py:221
  438.3 47.0 %all-to-all-done.2 = bf16[32,8,2048]{2,1,0:T(8,128)(2,1)S(1)} async-done(((bf16[32,8,2048]{2,1,0:T(8,128)(2,1)}), bf16[32,8,2048]{2,1,0:T(8,128)(2,1)S(1)}, u32[]{:S(2)}, u32[]{:S(2)}) %all-to-all-start.2) | async-done | bytes 1048608 | tf_op jit(solution)/shard_map/all_to_all | solution.py:163
  487.8 55.6 %all-gather.32.cloned.1.call-done = bf16[2048,2048]{1,0:T(8,128)(2,1)} async-done(((bf16[256,2048]{1,0:T(8,128)(2,1)}), bf16[2048,2048]{1,0:T(8,128)(2,1)}) %all-gather.32.cloned.1.call-update) | async-done | bytes 8388624 | tf_op jit(solution)/shard_map/all_gather | solution.py:218
  543.5 10.6 fusion.120
  554.0 37.4 %all-gather.36.cloned.1.call-done = bf16[2048,512]{0,1:T(8,128)(2,1)} async-done(((bf16[512,512]{0,1:T(8,128)(2,1)}), bf16[2048,512]{0,1:T(8,128)(2,1)}) %all-gather.36.cloned.1.call-update) | async-done | bytes 2097168 | tf_op jit(solution)/shard_map/all_gather | solution.py:177
  591.4 10.6 fusion.121
  602.0 35.7 %all-gather.38.cloned.1.call-done = bf16[512,2048]{1,0:T(8,128)(2,1)} async-done(((bf16[128,2048]{1,0:T(8,128)(2,1)}), bf16[512,2048]{1,0:T(8,128)(2,1)}) %all-gather.38.cloned.1.call-update) | async-done | bytes 2097168 | tf_op jit(solution)/shard_map/all_gather | solution.py:177
  637.7 55.5 %all-gather.40.cloned.1.call-done = bf16[2048,2048]{1,0:T(8,128)(2,1)} async-done(((bf16[256,2048]{1,0:T(8,128)(2,1)}), bf16[2048,2048]{1,0:T(8,128)(2,1)}) %all-gather.40.cloned.1.call-update) | async-done | bytes 8388624 | tf_op jit(solution)/shard_map/all_gather | solution.py:218
  693.1 13.3 multiply_convert_fusion.2
  714.8 10.2 add_convert_fusion.1
  725.1 71.4 %reduce-scatter.16.cloned.1.call-done = bf16[256,2048]{1,0:T(8,128)(2,1)} async-done(((bf16[2048,2048]{1,0:T(8,128)(2,1)}), bf16[256,2048]{1,0:T(8,128)(2,1)}) %reduce-scatter.16.cloned.1.call-update) | async-done | bytes 1048592 | tf_op jit(solution)/shard_map/reduce_scatter | solution.py:221
  802.6 9.8 convolution_convert_fusion.4
  814.0 9.4 convolution_convert_fusion.3
  825.0 9.1 convolution_convert_fusion.2
  834.2 22.4 %all-gather.42.cloned.1.call-done = bf16[2048,2048]{1,0:T(8,128)(2,1)} async-done(((bf16[256,2048]{1,0:T(8,128)(2,1)}), bf16[2048,2048]{1,0:T(8,128)(2,1)}) %all-gather.42.cloned.1.call-update) | async-done | bytes 8388624 | tf_op jit(solution)/shard_map/all_gather | solution.py:218
  856.6 13.4 multiply_reduce_fusion.1
  913.5 9.4 convolution_convert_fusion.7
  924.5 9.5 convolution_convert_fusion.6
  944.0 9.9 fusion.79
  970.7 20.3 %add_convert_fusion = bf16[2048,2048]{1,0:T(8,128)(2,1)} fusion(f32[2048,2048]{1,0:T(8,128)} %fusion.124, f32[2048,2048]{1,0:T(8,128)} %fusion.123, f32[2048,2048]{1,0:T(8,128)} %fusion.79, bf16[2048,256]{1,0:T(8,128)(2,1)S(1)} %copy-done.41, f32[2048,128]{1,0:T(8,128)S(1)} %bitcast.179, f32[2048,128]{1,0:T(8,128)S(1)} %bitcast.177), kind=kOutput, calls=%fused_computation | convolution fusion | flops 2165833728 | bytes 61865984 | tf_op jit(solution)/shard_map/dot_general | solution.py:99
  996.0 85.7 %all-reduce.6.cloned.1.call-done = bf16[512,2048]{1,0:T(8,128)(2,1)} async-done(((bf16[512,2048]{1,0:T(8,128)(2,1)}), bf16[512,2048]{1,0:T(8,128)(2,1)}) %all-reduce.6.cloned.1.call-update) | async-done | bytes 2097168 | tf_op jit(solution)/shard_map/psum | solution.py:317
  1086.4 24.4 %reduce-scatter.20.cloned.1.call-done = bf16[512,256]{1,0:T(8,128)(2,1)} async-done(((bf16[2048,256]{1,0:T(8,128)(2,1)}), bf16[512,256]{1,0:T(8,128)(2,1)}) %reduce-scatter.20.cloned.1.call-update) | async-done | bytes 262160 | tf_op jit(solution)/shard_map/reduce_scatter | solution.py:297
  1110.8 27.9 %reduce-scatter.22.cloned.1.call-done = bf16[512,256]{1,0:T(8,128)(2,1)} async-done(((bf16[2048,256]{1,0:T(8,128)(2,1)}), bf16[512,256]{1,0:T(8,128)(2,1)}) %reduce-scatter.22.cloned.1.call-update) | async-done | bytes 262160 | tf_op jit(solution)/shard_map/reduce_scatter | solution.py:297
  1138.8 45.4 %reduce-scatter.24.cloned.1.call-done = bf16[512,512]{1,0:T(8,128)(2,1)} async-done(((bf16[2048,512]{1,0:T(8,128)(2,1)}), bf16[512,512]{1,0:T(8,128)(2,1)}) %reduce-scatter.24.cloned.1.call-update) | async-done | bytes 524304 | tf_op jit(solution)/shard_map/reduce_scatter | solution.py:297
  1184.3 46.0 %reduce-scatter.26.cloned.1.call-done = bf16[512,512]{1,0:T(8,128)(2,1)} async-done(((bf16[2048,512]{1,0:T(8,128)(2,1)}), bf16[512,512]{1,0:T(8,128)(2,1)}) %reduce-scatter.26.cloned.1.call-update) | async-done | bytes 524304 | tf_op jit(solution)/shard_map/reduce_scatter | solution.py:297
  1230.4 75.0 %reduce-scatter.14.cloned.1.call-done = bf16[256,2048]{1,0:T(8,128)(2,1)} async-done(((bf16[2048,2048]{1,0:T(8,128)(2,1)}), bf16[256,2048]{1,0:T(8,128)(2,1)}) %reduce-scatter.14.cloned.1.call-update) | async-done | bytes 1048592 | tf_op jit(solution)/shard_map/reduce_scatter | solution.py:221
  1312.8 68.4 %reduce-scatter.18.cloned.1.call-done = bf16[256,2048]{1,0:T(8,128)(2,1)} async-done(((bf16[2048,2048]{1,0:T(8,128)(2,1)}), bf16[256,2048]{1,0:T(8,128)(2,1)}) %reduce-scatter.18.cloned.1.call-update) | async-done | bytes 1048592 | tf_op jit(solution)/shard_map/reduce_scatter | solution.py:221
  1391.3 38.8 %all-gather.52.cloned.1.call-done = bf16[8,512,4,128]{3,1,2,0:T(8,128)(2,1)} async-done(((bf16[1,512,4,128]{3,1,2,0:T(8,128)(2,1)}), bf16[8,512,4,128]{3,1,2,0:T(8,128)(2,1)}) %all-gather.52.cloned.1.call-update) | async-done | bytes 4194320 | tf_op jit(solution)/shard_map/all_gather | solution.py:309
  1443.1 8.9 copy.70
  1452.0 16.6 all-gather.54.cloned.1.call-done
  1481.5 8.9 copy.71
  1490.4 16.8 all-gather.56.cloned.1.call-done
  1515.3 77.1 %all-reduce.8.cloned.1.call-done = bf16[1024,2048]{1,0:T(8,128)(2,1)} async-done(((bf16[1024,2048]{1,0:T(8,128)(2,1)}), bf16[1024,2048]{1,0:T(8,128)(2,1)}) %all-reduce.8.cloned.1.call-update) | async-done | bytes 4194320 | tf_op jit(solution)/shard_map/psum | solution.py:320
  1599.1 23.5 %all-gather.44.cloned.1.call-done = bf16[512,2048]{1,0:T(8,128)(2,1)} async-done(((bf16[512,256]{1,0:T(8,128)(2,1)}), bf16[512,2048]{1,0:T(8,128)(2,1)}) %all-gather.44.cloned.1.call-update) | async-done | bytes 2097168 | tf_op jit(solution)/shard_map/all_gather | solution.py:303
  1626.7 25.8 %all-gather.46.cloned.1.call-done = bf16[512,2048]{1,0:T(8,128)(2,1)} async-done(((bf16[512,256]{1,0:T(8,128)(2,1)}), bf16[512,2048]{1,0:T(8,128)(2,1)}) %all-gather.46.cloned.1.call-update) | async-done | bytes 2097168 | tf_op jit(solution)/shard_map/all_gather | solution.py:303
  1656.7 35.2 %all-gather.48.cloned.1.call-done = bf16[512,4096]{1,0:T(8,128)(2,1)} async-done(((bf16[512,512]{1,0:T(8,128)(2,1)}), bf16[512,4096]{1,0:T(8,128)(2,1)}) %all-gather.48.cloned.1.call-update) | async-done | bytes 4194320 | tf_op jit(solution)/shard_map/all_gather | solution.py:303
  1698.6 32.7 %all-gather.50.cloned.1.call-done = bf16[512,4096]{1,0:T(8,128)(2,1)} async-done(((bf16[512,512]{1,0:T(8,128)(2,1)}), bf16[512,4096]{1,0:T(8,128)(2,1)}) %all-gather.50.cloned.1.call-update) | async-done | bytes 4194320 | tf_op jit(solution)/shard_map/all_gather | solution.py:303
  1738.1 39.5 %psum.31 = f32[4,2048]{1,0:T(4,128)S(1)} all-reduce(f32[4,2048]{1,0:T(4,128)S(1)} %pad_maximum_fusion.6), channel_id=1, replica_groups=mesh['rep'=8,'shard'=4] {'rep','shard'}, use_global_device_ids=true, to_apply=%region_36.37 | all-reduce | flops 8192 | bytes 65536 | tf_op jit(solution)/shard_map/psum | solution.py:328
  (347 shorter events, 263.5 us)
Async XLA Ops:
  8.3 423.9 %copy-start.56 = (s32[256]{0:T(256)}, s32[256]{0:T(256)S(1)}, u32[]{:S(2)}) copy-start(s32[256]{0:T(256)S(1)} %convert_reduce_fusion.3) | copy-start | bytes 3076
  11.0 56.9 %all-to-all-start = ((bf16[32,8,2048]{2,1,0:T(8,128)(2,1)}), bf16[32,8,2048]{2,1,0:T(8,128)(2,1)S(1)}, u32[]{:S(2)}, u32[]{:S(2)}) async-start(bf16[32,8,2048]{2,1,0:T(8,128)(2,1)} %fusion.15), calls=%async_computation | async-start | bytes 2097152 | tf_op jit(solution)/shard_map/all_to_all | solution.py:163
  18.4 71.7 %all-gather.30.cloned.1.call-start = ((), (), s32[]{:S(2)}) async-start(), calls=%async_computation.19 | async-start | bytes 1310720 | tf_op jit(solution)/shard_map/all_gather | solution.py:177
  19.2 105.0 %all-gather.22.cloned.1.call-start = ((), (), s32[]{:S(2)}) async-start(), calls=%async_computation.15 | async-start | bytes 9437184 | tf_op jit(solution)/shard_map/all_gather | solution.py:218
  68.0 417.3 %copy-start.58 = (s32[256]{0:T(256)}, s32[256]{0:T(256)S(1)}, u32[]{:S(2)}) copy-start(s32[256]{0:T(256)S(1)} %convert_reduce_fusion.2) | copy-start | bytes 3076
  68.5 348.9 %copy-start.4 = (f32[256,2048]{1,0:T(8,128)}, f32[256,2048]{1,0:T(8,128)S(1)}, u32[]{:S(2)}) copy-start(f32[256,2048]{1,0:T(8,128)S(1)} %get-tuple-element.80) | copy-start | bytes 6291460
  70.4 83.9 %all-gather.28.cloned.1.call-start = ((), (), s32[]{:S(2)}) async-start(), calls=%async_computation.18 | async-start | bytes 1310720 | tf_op jit(solution)/shard_map/all_gather | solution.py:177
  72.2 129.6 %all-gather.26.cloned.1.call-start = ((), (), s32[]{:S(2)}) async-start(), calls=%async_computation.17 | async-start | bytes 2621440 | tf_op jit(solution)/shard_map/all_gather | solution.py:177
  74.1 174.7 %all-gather.24.cloned.1.call-start = ((), (), s32[]{:S(2)}) async-start(), calls=%async_computation.16 | async-start | bytes 2621440 | tf_op jit(solution)/shard_map/all_gather | solution.py:177
  76.1 260.8 %all-reduce.4.cloned.1.call-start = ((), (), s32[]{:S(2)}) async-start(), calls=%async_computation.20 | async-start | bytes 4194304 | tf_op jit(solution)/shard_map/psum | solution.py:200
  80.1 337.3 %reduce-scatter.12.cloned.1.call-start = ((), (), s32[]{:S(2)}) async-start(), calls=%async_computation.21 | async-start | bytes 9437184 | tf_op jit(solution)/shard_map/reduce_scatter | solution.py:221
  80.2 80.4 %copy-start.66 = (f32[128]{0:T(128)}, f32[128]{0:T(128)S(1)}, u32[]{:S(2)}) copy-start(f32[128]{0:T(128)S(1)} %multiply_power_fusion) | copy-start | bytes 1540
  89.6 75.7 %copy-start.62 = (pred[128,128]{1,0:T(8,128)(4,1)}, pred[128,128]{1,0:T(8,128)(4,1)S(1)}, u32[]{:S(2)}) copy-start(pred[128,128]{1,0:T(8,128)(4,1)S(1)} %fusion.92) | copy-start | bytes 49156
  347.0 140.8 %all-gather.34.cloned.1.call-start = ((), (), s32[]{:S(2)}) async-start(), calls=%async_computation.23 | async-start | bytes 2621440 | tf_op jit(solution)/shard_map/all_gather | solution.py:177
  355.6 187.8 %all-gather.32.cloned.1.call-start = ((), (), s32[]{:S(2)}) async-start(), calls=%async_computation.22 | async-start | bytes 9437184 | tf_op jit(solution)/shard_map/all_gather | solution.py:218
  421.7 169.7 %all-gather.36.cloned.1.call-start = ((), (), s32[]{:S(2)}) async-start(), calls=%async_computation.24 | async-start | bytes 2621440 | tf_op jit(solution)/shard_map/all_gather | solution.py:177
  430.2 207.5 %all-gather.38.cloned.1.call-start = ((), (), s32[]{:S(2)}) async-start(), calls=%async_computation.25 | async-start | bytes 2621440 | tf_op jit(solution)/shard_map/all_gather | solution.py:177
  433.6 51.7 %all-to-all-start.2 = ((bf16[32,8,2048]{2,1,0:T(8,128)(2,1)}), bf16[32,8,2048]{2,1,0:T(8,128)(2,1)S(1)}, u32[]{:S(2)}, u32[]{:S(2)}) async-start(bf16[32,8,2048]{2,1,0:T(8,128)(2,1)} %fusion.17), calls=%async_computation.4 | async-start | bytes 2097152 | tf_op jit(solution)/shard_map/all_to_all | solution.py:163
  438.2 254.9 %all-gather.40.cloned.1.call-start = ((), (), s32[]{:S(2)}) async-start(), calls=%async_computation.27 | async-start | bytes 9437184 | tf_op jit(solution)/shard_map/all_gather | solution.py:218
  487.5 309.0 %reduce-scatter.16.cloned.1.call-start = ((), (), s32[]{:S(2)}) async-start(), calls=%async_computation.28 | async-start | bytes 9437184 | tf_op jit(solution)/shard_map/reduce_scatter | solution.py:221
  602.0 104.4 %copy-start.77 = (bf16[2048,512]{0,1:T(8,128)(2,1)S(1)}, bf16[2048,512]{0,1:T(8,128)(2,1)}, u32[]{:S(2)}) copy-start(bf16[2048,512]{0,1:T(8,128)(2,1)} %all-gather.34.cloned.1.call-done) | copy-start | bytes 6291460
  725.1 131.5 %all-gather.42.cloned.1.call-start = ((), (), s32[]{:S(2)}) async-start(), calls=%async_computation.29 | async-start | bytes 9437184 | tf_op jit(solution)/shard_map/all_gather | solution.py:218
  802.0 189.1 %reduce-scatter.28.cloned.1.call-start = ((), (), s32[]{:S(2)}) async-start(), calls=%async_computation.41 | async-start | bytes 2621440 | tf_op jit(solution)/shard_map/reduce_scatter | solution.py:297
  812.4 180.8 %reduce-scatter.30.cloned.1.call-start = ((), (), s32[]{:S(2)}) async-start(), calls=%async_computation.43 | async-start | bytes 2621440 | tf_op jit(solution)/shard_map/reduce_scatter | solution.py:297
  823.5 172.0 %reduce-scatter.32.cloned.1.call-start = ((), (), s32[]{:S(2)}) async-start(), calls=%async_computation.45 | async-start | bytes 2621440 | tf_op jit(solution)/shard_map/reduce_scatter | solution.py:297
  834.2 247.5 %all-reduce.6.cloned.1.call-start = ((), (), s32[]{:S(2)}) async-start(), calls=%async_computation.39 | async-start | bytes 4194304 | tf_op jit(solution)/shard_map/psum | solution.py:317
  881.6 229.2 %reduce-scatter.20.cloned.1.call-start = ((), (), s32[]{:S(2)}) async-start(), calls=%async_computation.31 | async-start | bytes 1310720 | tf_op jit(solution)/shard_map/reduce_scatter | solution.py:297
  903.0 235.7 %reduce-scatter.22.cloned.1.call-start = ((), (), s32[]{:S(2)}) async-start(), calls=%async_computation.33 | async-start | bytes 1310720 | tf_op jit(solution)/shard_map/reduce_scatter | solution.py:297
  910.4 273.9 %reduce-scatter.24.cloned.1.call-start = ((), (), s32[]{:S(2)}) async-start(), calls=%async_computation.35 | async-start | bytes 2621440 | tf_op jit(solution)/shard_map/reduce_scatter | solution.py:297
  923.0 307.4 %reduce-scatter.26.cloned.1.call-start = ((), (), s32[]{:S(2)}) async-start(), calls=%async_computation.37 | async-start | bytes 2621440 | tf_op jit(solution)/shard_map/reduce_scatter | solution.py:297
  934.0 371.4 %reduce-scatter.14.cloned.1.call-start = ((), (), s32[]{:S(2)}) async-start(), calls=%async_computation.26 | async-start | bytes 9437184 | tf_op jit(solution)/shard_map/reduce_scatter | solution.py:221
  943.9 437.3 %reduce-scatter.18.cloned.1.call-start = ((), (), s32[]{:S(2)}) async-start(), calls=%async_computation.30 | async-start | bytes 9437184 | tf_op jit(solution)/shard_map/reduce_scatter | solution.py:221
  991.0 439.0 %all-gather.52.cloned.1.call-start = ((), (), s32[]{:S(2)}) async-start(), calls=%async_computation.42 | async-start | bytes 4718592 | tf_op jit(solution)/shard_map/all_gather | solution.py:309
  993.2 475.4 %all-gather.54.cloned.1.call-start = ((), (), s32[]{:S(2)}) async-start(), calls=%async_computation.44 | async-start | bytes 4718592 | tf_op jit(solution)/shard_map/all_gather | solution.py:309
  995.3 511.8 %all-gather.56.cloned.1.call-start = ((), (), s32[]{:S(2)}) async-start(), calls=%async_computation.46 | async-start | bytes 4718592 | tf_op jit(solution)/shard_map/all_gather | solution.py:312
  995.9 596.5 %all-reduce.8.cloned.1.call-start = ((), (), s32[]{:S(2)}) async-start(), calls=%async_computation.40 | async-start | bytes 8388608 | tf_op jit(solution)/shard_map/psum | solution.py:320
  1086.3 219.1 %copy-start.8 = (f32[256,2048]{1,0:T(8,128)S(1)}, f32[256,2048]{1,0:T(8,128)}, u32[]{:S(2)}) copy-start(f32[256,2048]{1,0:T(8,128)} %copy-done.6) | copy-start | bytes 6291460
  1086.3 219.1 %copy-start.59 = (s32[256]{0:T(256)S(1)}, s32[256]{0:T(256)}, u32[]{:S(2)}) copy-start(s32[256]{0:T(256)} %copy-done.58) | copy-start | bytes 3076
  1086.3 219.1 %copy-start.65 = (pred[256]{0:T(512)(128)(4,1)S(1)}, pred[256]{0:T(512)(128)(4,1)}, u32[]{:S(2)}) copy-start(pred[256]{0:T(512)(128)(4,1)} %copy-done.64) | copy-start | bytes 772
  1086.3 536.2 %all-gather.44.cloned.1.call-start = ((), (), s32[]{:S(2)}) async-start(), calls=%async_computation.32 | async-start | bytes 2359296 | tf_op jit(solution)/shard_map/all_gather | solution.py:303
  1110.8 541.8 %all-gather.46.cloned.1.call-start = ((), (), s32[]{:S(2)}) async-start(), calls=%async_computation.34 | async-start | bytes 2359296 | tf_op jit(solution)/shard_map/all_gather | solution.py:303
  1138.7 242.5 %copy-start.44 = (f32[1,4,512]{2,0,1:T(1,128)S(1)}, f32[1,4,512]{2,0,1:T(1,128)}, u32[]{:S(2)}) copy-start(f32[1,4,512]{2,0,1:T(1,128)} %copy-done.43) | copy-start | bytes 24580
  1138.7 242.5 %copy-start.55 = (f32[256]{0:T(256)S(1)}, f32[256]{0:T(256)}, u32[]{:S(2)}) copy-start(f32[256]{0:T(256)} %copy-done.54) | copy-start | bytes 3076
  1138.7 242.5 %copy-start.61 = (f32[256]{0:T(256)S(1)}, f32[256]{0:T(256)}, u32[]{:S(2)}) copy-start(f32[256]{0:T(256)} %copy-done.60) | copy-start | bytes 3076
  1138.8 553.1 %all-gather.48.cloned.1.call-start = ((), (), s32[]{:S(2)}) async-start(), calls=%async_computation.36 | async-start | bytes 4718592 | tf_op jit(solution)/shard_map/all_gather | solution.py:303
  1184.3 547.0 %all-gather.50.cloned.1.call-start = ((), (), s32[]{:S(2)}) async-start(), calls=%async_computation.38 | async-start | bytes 4718592 | tf_op jit(solution)/shard_map/all_gather | solution.py:303
  1308.2 77.5 %all-to-all-start.1 = ((bf16[32,8,2048]{2,1,0:T(8,128)(2,1)}), bf16[32,8,2048]{2,1,0:T(8,128)(2,1)S(1)}, u32[]{:S(2)}, u32[]{:S(2)}) async-start(bf16[32,8,2048]{2,1,0:T(8,128)(2,1)} %fusion.16), calls=%async_computation.3 | async-start | bytes 2097152 | tf_op jit(solution)/shard_map/all_to_all | solution.py:163
  1386.7 391.6 %all-to-all-start.3 = ((bf16[32,8,2048]{2,1,0:T(8,128)(2,1)}), bf16[32,8,2048]{2,1,0:T(8,128)(2,1)S(1)}, u32[]{:S(2)}, u32[]{:S(2)}) async-start(bf16[32,8,2048]{2,1,0:T(8,128)(2,1)} %fusion.18), calls=%async_computation.7 | async-start | bytes 2097152 | tf_op jit(solution)/shard_map/all_to_all | solution.py:163
  (73 other events, 1003.0 us)
Sparse Core Ops, SparseCore 0:
  21.3 40.5 all-gather.29
  70.5 53.5 all-gather.21
  126.3 27.9 all-gather.27
  156.3 45.4 all-gather.25
  203.7 45.0 all-gather.23
  251.6 85.1 all-reduce.3
  347.1 70.2 reduce-scatter.11
  419.6 68.1 all-gather.33
  490.3 53.1 all-gather.31
  545.4 45.9 all-gather.35
  593.0 44.6 all-gather.37
  640.0 53.0 all-gather.39
  725.2 71.2 reduce-scatter.15
  802.2 54.3 all-gather.41
  858.8 43.8 reduce-scatter.27
  904.9 43.1 reduce-scatter.29
  950.3 43.1 reduce-scatter.31
  995.8 85.8 all-reduce.5
  1084.6 26.0 reduce-scatter.19
  1112.9 25.7 reduce-scatter.21
  1141.7 42.4 reduce-scatter.23
  1187.1 43.1 reduce-scatter.25
  1234.8 70.5 reduce-scatter.13
  1309.3 71.8 reduce-scatter.17
  1383.8 46.2 all-gather.51
  1432.0 36.5 all-gather.53
  1470.4 36.7 all-gather.55
  1511.4 80.9 all-reduce.7
  1594.3 28.2 all-gather.43
  1624.3 28.1 all-gather.45
  1654.4 37.4 all-gather.47
  1693.8 37.4 all-gather.49

commit v2 on v1

v2 whole, which is shorter than its diff:
```python
import functools
import math

import jax
import jax.numpy as jnp
from jax import lax
from jax.experimental import pallas as pl
from jax.experimental.pallas import tpu as pltpu
from jax.sharding import Mesh, PartitionSpec as P

HEADS = 8
KH = 256

layer_epsilon = 1e-05
head_epsilon = 1.0
rotary_base = 10000.0
bf16 = jnp.bfloat16
f32 = jnp.float32
MESHID = pl.DeviceIdType.MESH


def pack_tables(lengths, pack_rows, head_ids):
    entries = lengths.shape[1]
    slot_ids = jnp.arange(pack_rows, dtype=jnp.int32)
    seq_ends = jnp.cumsum(lengths, axis=1, dtype=jnp.int32)
    seq_starts = seq_ends - lengths
    segment = jnp.sum(
        (slot_ids[None, :, None] >= seq_ends[:, None, :]).astype(jnp.int32), axis=2, dtype=jnp.int32
    )
    owners = segment[:, :, None] == jnp.arange(entries, dtype=jnp.int32)[None, None, :]
    begins = jnp.sum(jnp.where(owners, seq_starts[:, None, :], 0), axis=2, dtype=jnp.int32)
    places = (slot_ids[None, :] - begins).astype(f32)
    usable = segment < entries - 1
    half_size = KH // 2
    frequency = jnp.power(
        f32(rotary_base), -jnp.arange(half_size, dtype=f32) / f32(half_size - 1)
    )
    angles = places[:, :, None] * frequency
    cosine_table = jnp.cos(angles)
    sine_table = jnp.sin(angles)
    lag_steps = slot_ids[:, None] - slot_ids[None, :]
    linked = (
        (segment[:, :, None] == segment[:, None, :])
        & (lag_steps[None] >= 0)
        & usable[:, None, :]
    )
    log_rates = jnp.log(1.0 - jnp.power(f32(2.0), -5.0 - head_ids.astype(f32)))
    powers = jnp.exp(log_rates[:, None, None] * jnp.maximum(lag_steps, 0).astype(f32)[None])
    decays = jnp.where(linked[None], powers[:, None], f32(0.0))
    return cosine_table, sine_table, decays, usable


def gram_rows(leading, trailing):
    return lax.dot_general(
        leading, trailing, (((0,), (0,)), ((), ())), preferred_element_type=f32
    )


def back_through(incoming, matrix):
    return lax.dot_general(
        incoming, matrix, (((1,), (1,)), ((), ())), preferred_element_type=f32
    )


def forward_dot(inputs, matrix):
    return jnp.dot(inputs, matrix, preferred_element_type=f32)


def gelu_parts(v):
    c = f32(math.sqrt(2.0 / math.pi))
    t = jnp.tanh(c * (v + 0.044715 * v * v * v))
    value = 0.5 * v * (1.0 + t)
    slope = 0.5 * (1.0 + t) + 0.5 * v * (1.0 - t * t) * c * (1.0 + 3.0 * 0.044715 * v * v)
    return value, slope


def flip(me, mask):
    for bit in (1, 2, 4):
        if mask & bit:
            me = me + bit - 2 * bit * ((me // bit) % 2)
    return me


def greet(far=False):
    me = lax.axis_index("tp")
    barrier = pltpu.get_barrier_semaphore()
    for mask in (1, 2, 4):
        pl.semaphore_signal(
            barrier, inc=1, device_id={"tp": flip(me, mask)}, device_id_type=MESHID
        )
    count = 3
    if far:
        for other in others():
            pl.semaphore_signal(barrier, inc=1, device_id={"shard": other}, device_id_type=MESHID)
            count += 1
    pl.semaphore_wait(barrier, count)
    return me


def others():
    shards = lax.axis_size("shard")
    return [(lax.axis_index("shard") + k) % shards for k in range(1, shards)]


def push(source, goal, send, recv, peer):
    return pltpu.make_async_remote_copy(
        src_ref=source, dst_ref=goal, send_sem=send, recv_sem=recv,
        device_id={"tp": peer}, device_id_type=MESHID,
    )


def gather_steps(me, own, out, send, recv):
    rows = own.shape[0]
    half = rows // 2
    sib, xn, yn, dn = flip(me, 1), flip(me, 2), flip(me, 4), flip(me, 6)

    def cp(i, src, goal, peer):
        return push(src, goal, send.at[i], recv.at[i], peer)

    low, high = pl.ds(0, half), pl.ds(half, half)
    first = [
        cp(0, own, out.at[me], xn),
        cp(1, own, out.at[me], yn),
        cp(2, own, out.at[me], sib),
    ]
    for c in first:
        c.start()
    first[0].wait_recv()
    c3 = cp(3, out.at[xn, low], out.at[xn, low], yn)
    c3.start()
    c4 = cp(4, out.at[xn], out.at[xn], sib)
    c4.start()
    first[1].wait_recv()
    c5 = cp(5, out.at[yn, high], out.at[yn, high], xn)
    c5.start()
    c6 = cp(6, out.at[yn], out.at[yn], sib)
    c6.start()
    c3.wait_recv()
    c7 = cp(7, out.at[dn, low], out.at[dn, low], sib)
    c7.start()
    c5.wait_recv()
    c8 = cp(8, out.at[dn, high], out.at[dn, high], sib)
    c8.start()
    first[2].wait_recv()
    for c in (c4, c6, c7, c8):
        c.wait_recv()
    for c in first + [c3, c4, c5, c6, c7, c8]:
        c.wait_send()


COLS = 512


def reduce_steps(me, pairs, transposed, tosib, fromsib, hold, hop, final, total, send, recv, between=None):
    rows, width = total.shape
    half = rows // 2
    sib, xn, yn = flip(me, 1), flip(me, 2), flip(me, 4)
    low, high = pl.ds(0, half), pl.ds(half, half)

    def product(block, tile):
        acc = None
        for act, weight in pairs:
            left = act[pl.ds(pl.multiple_of(block * rows, rows), rows), :]
            if transposed:
                part = lax.dot_general(
                    left, weight[pl.ds(pl.multiple_of(tile * COLS, COLS), COLS), 0 : act.shape[1]],
                    (((1,), (1,)), ((), ())), preferred_element_type=f32,
                )
            else:
                part = jnp.dot(
                    left, weight[:, pl.ds(pl.multiple_of(tile * COLS, COLS), COLS)],
                    preferred_element_type=f32,
                )
            acc = part if acc is None else acc + part
        return acc

    def cp(i, src, goal, peer):
        return push(src, goal, send.at[i], recv.at[i], peer)

    masks = (6, 2, 4, 0)
    over, out = [], {}

    def for_sibling(slot):
        block = flip(me, masks[slot] ^ 1)

        @pl.loop(0, width // COLS)
        def _(tile):
            at = pl.ds(pl.multiple_of(tile * COLS, COLS), COLS)
            tosib[slot, :, at] = product(block, tile).astype(bf16)

        c = cp(slot, tosib.at[slot], fromsib.at[slot], sib)
        c.start()
        over.append(c)

    def for_own_core(slot):
        block = flip(me, masks[slot])
        over[slot].wait_recv()

        @pl.loop(0, width // COLS)
        def _(tile):
            at = pl.ds(pl.multiple_of(tile * COLS, COLS), COLS)
            value = product(block, tile) + fromsib[slot, :, at].astype(f32)
            if slot < 3:
                hold[slot, :, at] = value.astype(bf16)
            else:
                total[:, at] = value

    for_sibling(0)
    for_sibling(1)
    for_own_core(0)
    dx = cp(4, hold.at[0, low], hop.at[0], xn)
    dy = cp(5, hold.at[0, high], hop.at[1], yn)
    dx.start()
    dy.start()
    for_sibling(2)
    for_own_core(1)
    xa = cp(6, hold.at[1, low], final.at[0, low], xn)
    xa.start()
    for_sibling(3)
    for_own_core(2)
    yb = cp(7, hold.at[2, high], final.at[1, high], yn)
    yb.start()
    for_own_core(3)
    if between is not None:
        between()
    dy.wait_recv()
    hold[1, high] = (hold[1, high].astype(f32) + hop[1].astype(f32)).astype(bf16)
    xb = cp(8, hold.at[1, high], final.at[0, high], xn)
    xb.start()
    dx.wait_recv()
    hold[2, low] = (hold[2, low].astype(f32) + hop[0].astype(f32)).astype(bf16)
    ya = cp(9, hold.at[2, low], final.at[1, low], yn)
    ya.start()
    xa.wait_recv()
    yb.wait_recv()
    xb.wait_recv()
    ya.wait_recv()
    for c in over + [dx, dy, xa, yb, xb, ya]:
        c.wait_send()


def summed(total, final, at):
    return total[at, :] + final[0, at, :].astype(f32) + final[1, at, :].astype(f32)


def reduce_scratch(rows, width):
    return [
        pltpu.VMEM((4, rows, width), bf16),
        pltpu.VMEM((4, rows, width), bf16),
        pltpu.VMEM((3, rows, width), bf16),
        pltpu.VMEM((2, rows // 2, width), bf16),
        pltpu.VMEM((2, rows, width), bf16),
        pltpu.VMEM((rows, width), f32),
        pltpu.SemaphoreType.DMA((10,)),
        pltpu.SemaphoreType.DMA((10,)),
    ]


CHUNK = 32


def cost(us):
    return pl.CostEstimate(flops=int(us * 1e9), bytes_accessed=int(us * 3e6), transcendentals=0)


def params(cid=None):
    if cid is None:
        return pltpu.CompilerParams(vmem_limit_bytes=60 << 20)
    return pltpu.CompilerParams(collective_id=cid, has_side_effects=True, vmem_limit_bytes=60 << 20)


def by_rows(count):
    def run(body):
        @pl.loop(0, count // CHUNK)
        def _(i):
            body(pl.ds(pl.multiple_of(i * CHUNK, CHUNK), CHUNK))

    return run


def centre(value, epsilon):
    average = jnp.mean(value, axis=-1, keepdims=True)
    centred = value - average
    spread = jnp.mean(centred * centred, axis=-1, keepdims=True)
    root = lax.rsqrt(spread + epsilon)
    return centred * root, root


def through_norm(e, unit, root):
    return root * (
        e - jnp.mean(e, axis=-1, keepdims=True) - unit * jnp.mean(e * unit, axis=-1, keepdims=True)
    )


def leading(rows, columns):
    return pl.BlockSpec((rows, columns), lambda *_: (0, 0))


ANY = pl.BlockSpec(memory_space=pl.ANY)
WHOLE = pl.BlockSpec(memory_space=pltpu.VMEM)


def gather_scratch(rows, width):
    return [
        pltpu.VMEM((rows, width), bf16),
        pltpu.SemaphoreType.DMA((9,)),
        pltpu.SemaphoreType.DMA((9,)),
        pltpu.SemaphoreType.DMA,
    ]


def gather_all(me, own, out, send, recv, local_sem):
    mine = pltpu.make_async_copy(own, out.at[me], local_sem)
    mine.start()
    gather_steps(me, own, out, send, recv)
    mine.wait()


def entry_kernel(
    came, mix, gains, lens, x_out, normed_all, lens_all, small,
    own, send, recv, sem, send2, recv2, sem2, all_gains, send3, recv3,
):
    me = greet(True)
    z = lax.axis_index("shard")
    copies = []
    for k, other in enumerate(others()):
        c = pltpu.make_async_remote_copy(
            src_ref=gains,
            dst_ref=all_gains.at[z],
            send_sem=send3.at[k],
            recv_sem=recv3.at[k],
            device_id={"shard": other},
            device_id_type=MESHID,
        )
        c.start()
        copies.append(c)
    all_gains[z] = gains[...]
    gather_all(me, lens, lens_all, send2, recv2, sem2)
    for c in copies:
        c.wait()
    part = gains.shape[1]
    for i in range(all_gains.shape[0]):
        small[:, i * part : (i + 1) * part] = all_gains[i]

    @by_rows(came.shape[0])
    def _(at):
        value = jnp.dot(mix[at, :], came[...], preferred_element_type=f32)
        x_out[at, :] = value.astype(bf16)
        unit, _ = centre(value, layer_epsilon)
        own[at, :] = (unit * small[0:1, :] + small[1:2, :]).astype(bf16)

    gather_all(me, own, normed_all, send, recv, sem)


def entry(came, mix, gains, lens, cid):
    rows, width = came.shape
    shards = lax.axis_size("shard")
    return pl.pallas_call(
        entry_kernel,
        out_shape=(
            jax.ShapeDtypeStruct((rows, width), bf16),
            jax.ShapeDtypeStruct((8, rows, width), bf16),
            jax.ShapeDtypeStruct((8,) + lens.shape, lens.dtype),
            jax.ShapeDtypeStruct((8, width), f32),
        ),
        in_specs=[WHOLE] * 3 + [ANY],
        out_specs=(WHOLE, ANY, ANY, WHOLE),
        scratch_shapes=gather_scratch(rows, width)
        + gather_scratch(rows, width)[1:]
        + [
            pltpu.VMEM((shards, 8, width // shards), f32),
            pltpu.SemaphoreType.DMA((shards - 1,)),
            pltpu.SemaphoreType.DMA((shards - 1,)),
        ],
        compiler_params=params(cid),
        cost_estimate=cost(50),
        name="entry",
    )(came, mix, gains, lens)


def entry_back_kernel(came, mix, usable, _after, back_out, back_all, own, send, recv, sem):
    me = greet()

    @by_rows(came.shape[0])
    def _(at):
        value = jnp.dot(mix[at, :], came[...], preferred_element_type=f32)
        value = jnp.where(usable[at, :] > 0.5, value, 0.0).astype(bf16)
        back_out[at, :] = value
        own[at, :] = value

    gather_all(me, own, back_all, send, recv, sem)


def entry_back(came, mix, usable, after, cid):
    rows, width = came.shape
    return pl.pallas_call(
        entry_back_kernel,
        out_shape=(
            jax.ShapeDtypeStruct((rows, width), bf16),
            jax.ShapeDtypeStruct((8, rows, width), bf16),
        ),
        in_specs=[WHOLE] * 3 + [ANY],
        out_specs=(WHOLE, ANY),
        scratch_shapes=gather_scratch(rows, width),
        compiler_params=params(cid),
        cost_estimate=cost(45),
        name="entry_back",
    )(came, mix, usable, after)


def deal_plan(back, count):
    heads = HEADS // count
    me = lax.axis_index("tp")
    spread = [i * heads + me // count for i in range(count)]
    packed = [(me % heads) * count + i for i in range(count)]
    goals, sources = (packed, spread) if back else (spread, packed)
    return me, goals, sources, (me // heads if back else me % count), me // count == me % heads


def deal_start(back, pieces, out, send, recv, local_sem):
    count = pieces.shape[0]
    me, goals, sources, slot, inside = deal_plan(back, count)
    barrier = pltpu.get_barrier_semaphore()
    for i in range(count):

        @pl.when(sources[i] != me)
        def _():
            pl.semaphore_signal(
                barrier, inc=1, device_id={"tp": sources[i]}, device_id_type=MESHID
            )

    pl.semaphore_wait(barrier, jnp.where(inside, count - 1, count))
    for i in range(count):

        @pl.when(goals[i] == me)
        def _():
            pltpu.make_async_copy(pieces.at[i], out.at[slot], local_sem).start()

        @pl.when(goals[i] != me)
        def _():
            push(pieces.at[i], out.at[slot], send.at[i], recv.at[slot], goals[i]).start()


def deal_wait(back, pieces, out, send, recv, local_sem):
    count = pieces.shape[0]
    me, goals, sources, slot, _ = deal_plan(back, count)
    for i in range(count):

        @pl.when(goals[i] == me)
        def _():
            pltpu.make_async_copy(pieces.at[i], out.at[slot], local_sem).wait()

        @pl.when(goals[i] != me)
        def _():
            push(pieces.at[i], out.at[slot], send.at[i], recv.at[slot], goals[i]).wait_send()

        @pl.when(sources[i] != me)
        def _():
            push(pieces.at[i], out.at[i], send.at[i], recv.at[i], sources[i]).wait_recv()


def deal_scratch(count):
    return [
        pltpu.SemaphoreType.DMA((count,)),
        pltpu.SemaphoreType.DMA((count,)),
        pltpu.SemaphoreType.DMA,
    ]


def turn(value, cosine, sine):
    half = value.shape[-1] // 2
    a, b = value[:, :half], value[:, half:]
    return jnp.concatenate([a * cosine - b * sine, a * sine + b * cosine], axis=1)


def retain_kernel(
    normed, weight, cosine, sine, decays, pieces,
    q_out, k_out, v_out, w_out, g_out, r_out, branch, wo, *sems
):
    @pl.when(pl.program_id(0) == 0)
    def _():
        deal_start(False, pieces, wo, *sems)

    packs, span = decays.shape[0], decays.shape[1]
    value_at = 2 * KH
    gate_at = value_at + v_out.shape[1]
    rows = normed[...]

    def project(begin, size):
        return jnp.dot(rows, weight[:, begin : begin + size], preferred_element_type=f32)

    q_out[...] = turn(project(0, KH), cosine[...], sine[...]).astype(bf16)
    k_out[...] = (turn(project(KH, KH), cosine[...], sine[...]) * KH ** (-0.5)).astype(bf16)
    v_out[...] = project(value_at, v_out.shape[1]).astype(bf16)
    g_out[...] = project(gate_at, g_out.shape[1])
    for p in range(packs):
        at = pl.ds(p * span, span)
        scores = lax.dot_general(
            q_out[at, :], k_out[at, :], (((1,), (1,)), ((), ())), preferred_element_type=f32
        )
        low = (scores * decays[p]).astype(bf16)
        w_out[p] = low
        retained = jnp.dot(low, v_out[at, :], preferred_element_type=f32)
        r_out[at, :] = retained
        unit, _ = centre(retained, head_epsilon)
        gating = g_out[at, :]
        branch[at, :] = (gating * jax.nn.sigmoid(gating) * unit).astype(bf16)

    @pl.when(pl.program_id(0) == pl.num_programs(0) - 1)
    def _():
        deal_wait(False, pieces, wo, *sems)


def retain(normed, weight, value_size, cosine, sine, decays, pieces, block, cid):
    total, width = normed.shape
    span = decays.shape[1]
    grid = total // block
    row = lambda w: pl.BlockSpec((block, w), lambda i: (i, 0))
    square = pl.BlockSpec((block // span, span, span), lambda i: (i, 0, 0))
    flat = lambda w, kind: jax.ShapeDtypeStruct((total, w), kind)
    return pl.pallas_call(
        retain_kernel,
        grid=(grid,),
        in_specs=[
            row(width), leading(width, 2 * KH + 2 * value_size), row(KH // 2), row(KH // 2), square,
            ANY,
        ],
        out_specs=(
            row(KH), row(KH), row(value_size), square, row(value_size), row(value_size),
            row(value_size), ANY,
        ),
        out_shape=(
            flat(KH, bf16), flat(KH, bf16), flat(value_size, bf16),
            jax.ShapeDtypeStruct(decays.shape, bf16), flat(value_size, f32),
            flat(value_size, f32), flat(value_size, bf16),
            jax.ShapeDtypeStruct(pieces.shape, bf16),
        ),
        scratch_shapes=deal_scratch(pieces.shape[0]),
        compiler_params=params(cid),
        cost_estimate=cost(24),
        name="retain",
    )(normed, weight, cosine, sine, decays, pieces)


def retain_back_kernel(
    middle_low, wo, q_in, k_in, v_in, w_in, g_in, r_in, cosine, sine, decays, pieces,
    low, dealt, *sems
):
    @pl.when(pl.program_id(0) == 0)
    def _():
        deal_start(True, pieces, dealt, *sems)

    packs, span = decays.shape[0], decays.shape[1]
    value_at = 2 * KH
    value_size = v_in.shape[1]
    gate_at = value_at + value_size
    back_branch = lax.dot_general(
        middle_low[...], wo[...], (((1,), (1,)), ((), ())), preferred_element_type=f32
    )
    cols = (((0,), (0,)), ((), ()))
    last = (((1,), (1,)), ((), ()))
    for p in range(packs):
        at = pl.ds(p * span, span)
        bb = back_branch[p * span : (p + 1) * span]
        unit, root = centre(r_in[at, :], head_epsilon)
        gating = g_in[at, :]
        sigma = jax.nn.sigmoid(gating)
        low[at, gate_at:] = (bb * unit * (sigma * (1.0 + gating * (1.0 - sigma)))).astype(bf16)
        retained_low = through_norm(bb * (gating * sigma), unit, root).astype(bf16)
        back_weights = lax.dot_general(retained_low, v_in[at, :], last, preferred_element_type=f32)
        low[at, value_at:gate_at] = lax.dot_general(
            w_in[p], retained_low, cols, preferred_element_type=f32
        ).astype(bf16)
        back_scores = (back_weights * decays[p]).astype(bf16)
        back_q = jnp.dot(back_scores, k_in[at, :], preferred_element_type=f32)
        back_k = lax.dot_general(back_scores, q_in[at, :], cols, preferred_element_type=f32)
        low[at, :KH] = turn(back_q, cosine[at, :], -sine[at, :]).astype(bf16)
        low[at, KH:value_at] = (turn(back_k, cosine[at, :], -sine[at, :]) * KH ** (-0.5)).astype(bf16)

    @pl.when(pl.program_id(0) == pl.num_programs(0) - 1)
    def _():
        deal_wait(True, pieces, dealt, *sems)


def retain_back(middle_low, wo, q, k, v, w, g, r, cosine, sine, decays, pieces, block, cid):
    total, width = middle_low.shape
    span = decays.shape[1]
    value_size = v.shape[1]
    row = lambda w: pl.BlockSpec((block, w), lambda i: (i, 0))
    square = pl.BlockSpec((block // span, span, span), lambda i: (i, 0, 0))
    return pl.pallas_call(
        retain_back_kernel,
        grid=(total // block,),
        in_specs=[
            row(width), WHOLE, row(KH), row(KH), row(value_size), square, row(value_size),
            row(value_size), row(KH // 2), row(KH // 2), square, ANY,
        ],
        out_specs=(row(2 * KH + 2 * value_size), ANY),
        out_shape=(
            jax.ShapeDtypeStruct((total, 2 * KH + 2 * value_size), bf16),
            jax.ShapeDtypeStruct(pieces.shape, bf16),
        ),
        scratch_shapes=deal_scratch(pieces.shape[0]),
        compiler_params=params(cid),
        cost_estimate=cost(20),
        name="retain_back",
    )(middle_low, wo, q, k, v, w, g, r, cosine, sine, decays, pieces)


def feed_kernel(shards, normed_two, back_low, w_two, hidden, low, w_down):
    size = hidden.shape[1]

    @pl.when(pl.program_id(0) == 0)
    def _():
        unit = size // shards
        span = w_two.shape[0] // shards
        part = w_two.shape[1] - 2 * size
        for z in range(shards):
            for c in range(span // unit):
                begin = z * span + c * unit
                w_down[z * unit : (z + 1) * unit, c * part : (c + 1) * part] = w_two[
                    begin : begin + unit, 2 * size :
                ]

    both = jnp.dot(normed_two[...], w_two[:, : 2 * size], preferred_element_type=f32)
    back = lax.dot_general(
        back_low[...], w_down[...], (((1,), (1,)), ((), ())), preferred_element_type=f32
    )
    up = both[:, size:]
    value, slope = gelu_parts(both[:, :size])
    hidden[...] = (value * up).astype(bf16)
    low[:, :size] = (back * up * slope).astype(bf16)
    low[:, size:] = (back * value).astype(bf16)


def feed(normed_two, back_low, w_two, size, shards, block):
    total, width = normed_two.shape
    row = lambda w: pl.BlockSpec((block, w), lambda i: (i, 0))
    return pl.pallas_call(
        functools.partial(feed_kernel, shards),
        grid=(total // block,),
        in_specs=[row(width), row(width), WHOLE],
        out_specs=(row(size), row(2 * size), pl.BlockSpec((size, width), lambda i: (0, 0))),
        out_shape=(
            jax.ShapeDtypeStruct((total, size), bf16),
            jax.ShapeDtypeStruct((total, 2 * size), bf16),
            jax.ShapeDtypeStruct((size, width), bf16),
        ),
        compiler_params=params(),
        cost_estimate=cost(18),
        name="feed",
    )(normed_two, back_low, w_two)


def middle_kernel(branch, wo, x, small, middle, normed_all, own, send1, recv1, sem1, *scratch):
    me = greet()
    reduce_steps(me, [(branch, wo)], False, *scratch)
    final, total = scratch[4], scratch[5]

    @by_rows(x.shape[0])
    def _(at):
        value = x[at, :].astype(f32) + summed(total, final, at)
        middle[at, :] = value
        unit, _ = centre(value, layer_epsilon)
        own[at, :] = (unit * small[2:3, :] + small[3:4, :]).astype(bf16)

    gather_all(me, own, normed_all, send1, recv1, sem1)


def make_middle(branch, wo, x, small, cid):
    rows, width = x.shape
    return pl.pallas_call(
        middle_kernel,
        out_shape=(
            jax.ShapeDtypeStruct((rows, width), f32),
            jax.ShapeDtypeStruct((8, rows, width), bf16),
        ),
        in_specs=[WHOLE] * 4,
        out_specs=(WHOLE, ANY),
        scratch_shapes=gather_scratch(rows, width) + reduce_scratch(rows, width),
        compiler_params=params(cid),
        cost_estimate=cost(85),
        name="make_middle",
    )(branch, wo, x, small)


def column_sums(out, row, value, first):
    total = jnp.sum(value, axis=0, keepdims=True)

    @pl.when(first)
    def _():
        out[row : row + 1, :] = total

    @pl.when(jnp.logical_not(first))
    def _():
        out[row : row + 1, :] += total


def back_middle_kernel(
    low, weight, middle, back_out, small, _after, _more, back_middle, parts, middle_all,
    own, send1, recv1, sem1, *scratch,
):
    me = greet()
    reduce_steps(me, [(low, weight)], True, *scratch)
    final, total = scratch[4], scratch[5]
    parts[...] = jnp.zeros_like(parts)

    @by_rows(middle.shape[0])
    def _(at):
        back = summed(total, final, at)
        unit, root = centre(middle[at, :], layer_epsilon)
        parts[0:1, :] += jnp.sum(back * unit, axis=0, keepdims=True)
        parts[1:2, :] += jnp.sum(back, axis=0, keepdims=True)
        value = back_out[at, :].astype(f32) + through_norm(back * small[2:3, :], unit, root)
        back_middle[at, :] = value
        own[at, :] = value.astype(bf16)

    gather_all(me, own, middle_all, send1, recv1, sem1)


def make_back_middle(low, weight, middle, back_out, small, after, more, cid):
    rows, width = middle.shape
    return pl.pallas_call(
        back_middle_kernel,
        out_shape=(
            jax.ShapeDtypeStruct((rows, width), f32),
            jax.ShapeDtypeStruct((8, width), f32),
            jax.ShapeDtypeStruct((8, rows, width), bf16),
        ),
        in_specs=[WHOLE] * 5 + [ANY, ANY],
        out_specs=(WHOLE, WHOLE, ANY),
        scratch_shapes=gather_scratch(rows, width) + reduce_scratch(rows, width),
        compiler_params=params(cid),
        cost_estimate=cost(90),
        name="make_back_middle",
    )(low, weight, middle, back_out, small, after, more)


def phase_one(me, values, by_x, by_y, by_sib, send, recv):
    copies = []
    for k, value in enumerate(values):
        for i, (goal, mask) in enumerate(((by_x, 2), (by_y, 4), (by_sib, 1))):
            n = 3 * k + i
            copies.append(push(value, goal[k], send.at[n], recv.at[n], flip(me, mask)))
    for c in copies:
        c.start()
    return copies


def phase_two(me, by_x, by_y, low, high, sib_x, sib_y, send, recv):
    copies = []
    for k in range(len(by_x)):
        half = by_x[k].shape[0] // 2
        for i, (source, goal, mask) in enumerate(
            (
                (by_x[k].at[pl.ds(0, half)], low[k], 4),
                (by_y[k].at[pl.ds(half, half)], high[k], 2),
                (by_x[k], sib_x[k], 1),
                (by_y[k], sib_y[k], 1),
            )
        ):
            n = 4 * k + i
            copies.append(push(source, goal, send.at[n], recv.at[n], flip(me, mask)))
    for c in copies:
        c.start()
    return copies


def phase_three(me, low, high, sib_low, sib_high, send, recv):
    copies = []
    for k in range(len(low)):
        for i, (source, goal) in enumerate(((low[k], sib_low[k]), (high[k], sib_high[k]))):
            n = 2 * k + i
            copies.append(push(source, goal, send.at[n], recv.at[n], flip(me, 1)))
    for c in copies:
        c.start()
    return copies


def pair(count):
    return [pltpu.SemaphoreType.DMA((count,)), pltpu.SemaphoreType.DMA((count,))]


def same(values, halves=False):
    return [
        jax.ShapeDtypeStruct((v.shape[0] // 2 if halves else v.shape[0], v.shape[1]), v.dtype)
        for v in values
    ]


def back_input_kernel(count, low, weight, x, back_middle, small, *refs):
    values = refs[:count]
    out, parts = refs[count : count + 2]
    by = refs[count + 2 : 4 * count + 2]
    send, recv = refs[4 * count + 2 : 4 * count + 4]
    scratch = refs[4 * count + 4 :]
    me = greet()
    copies = phase_one(
        me, values, by[:count], by[count : 2 * count], by[2 * count :], send, recv
    )
    reduce_steps(me, [(low, weight)], True, *scratch)
    final, total = scratch[4], scratch[5]
    parts[...] = jnp.zeros_like(parts)

    @by_rows(x.shape[0])
    def _(at):
        back = summed(total, final, at)
        unit, root = centre(x[at, :].astype(f32), layer_epsilon)
        parts[0:1, :] += jnp.sum(back * unit, axis=0, keepdims=True)
        parts[1:2, :] += jnp.sum(back, axis=0, keepdims=True)
        value = back_middle[at, :] + through_norm(back * small[0:1, :], unit, root)
        out[at, :] = value.astype(bf16)

    for c in copies:
        c.wait()


def make_back_input(low, weight, x, back_middle, small, values, cid):
    rows, width = x.shape
    count = len(values)
    out = pl.pallas_call(
        functools.partial(back_input_kernel, count),
        out_shape=[
            jax.ShapeDtypeStruct((rows, width), bf16),
            jax.ShapeDtypeStruct((8, width), f32),
        ]
        + same(values) * 3,
        in_specs=[WHOLE] * 5 + [ANY] * count,
        out_specs=[WHOLE] * 2 + [ANY] * (3 * count),
        scratch_shapes=pair(3 * count) + reduce_scratch(rows, width),
        compiler_params=params(cid),
        cost_estimate=cost(80),
        name="make_back_input",
    )(low, weight, x, back_middle, small, *values)
    by = out[2:]
    return out[0], out[1], by[:count], by[count : 2 * count], by[2 * count :]


def ending_kernel(count, hidden, weight, middle, usable, parts_one, parts_two, *refs):
    refs = list(refs)

    def take(n):
        got = refs[:n]
        del refs[:n]
        return got

    by_x, by_y, fresh = take(count), take(count), take(1)
    out, sums = take(2)
    low, high, sib_x, sib_y, sib_low, sib_high = (take(count) for _ in range(6))
    f_x, f_y, f_sib, f_low, f_high, f_sib_x, f_sib_y, f_sib_low, f_sib_high = (
        take(1) for _ in range(9)
    )
    parts, turned, far = take(3)
    send_s, recv_s, send_f, recv_f = take(4)
    two, three, one_f, two_f, three_f = (take(2) for _ in range(5))
    scratch = refs
    me = greet(True)
    z = lax.axis_index("shard")
    shards = lax.axis_size("shard")
    started = phase_one(me, fresh, f_x, f_y, f_sib, *one_f)
    parts[...] = jnp.zeros_like(parts)
    parts[0:2, :] = parts_one[0:2, :]
    parts[2:4, :] = parts_two[0:2, :]
    steps = [
        push(parts, turned.at[i], send_s.at[i], recv_s.at[i], flip(me, mask))
        for i, mask in enumerate((1, 2, 4))
    ]
    waiting = []

    def between():
        for i, c in enumerate(steps):
            c.start()
            c.wait()
            parts[...] += turned[i]
        part = parts.shape[1] // shards
        for k, other in enumerate(others()):
            c = pltpu.make_async_remote_copy(
                src_ref=parts.at[:, pl.ds(pl.multiple_of(other * part, part), part)],
                dst_ref=far.at[k],
                send_sem=send_f.at[k],
                recv_sem=recv_f.at[k],
                device_id={"shard": other},
                device_id_type=MESHID,
            )
            c.start()
            waiting.append(c)
        for c in started:
            c.wait()
        started.clear()
        started.extend(phase_two(me, f_x, f_y, f_low, f_high, f_sib_x, f_sib_y, *two_f))
        started.extend(phase_two(me, by_x, by_y, low, high, sib_x, sib_y, *two))

    reduce_steps(me, [(hidden, weight)], False, *scratch, between=between)
    final, total = scratch[4], scratch[5]

    @by_rows(middle.shape[0])
    def _(at):
        value = middle[at, :] + summed(total, final, at)
        out[at, :] = jnp.where(usable[at, :] > 0.5, value, 0.0).astype(bf16)

    for c in started:
        c.wait()
    last = phase_three(me, f_low, f_high, f_sib_low, f_sib_high, *three_f)
    last += phase_three(me, low, high, sib_low, sib_high, *three)
    part = parts.shape[1] // shards
    value = parts[:, pl.ds(pl.multiple_of(z * part, part), part)]
    for k, c in enumerate(waiting):
        c.wait()
        value = value + far[k]
    sums[...] = value
    for c in last:
        c.wait()


def make_ending(hidden, weight, middle, usable, parts_one, parts_two, by_x, by_y, fresh, cid):
    rows, width = middle.shape
    shards = lax.axis_size("shard")
    count = len(by_x)
    shapes = (
        [
            jax.ShapeDtypeStruct((rows, width), bf16),
            jax.ShapeDtypeStruct((8, width // shards), f32),
        ]
        + same(by_x, True) * 2
        + same(by_x) * 2
        + same(by_x, True) * 2
        + same([fresh]) * 3
        + same([fresh], True) * 2
        + same([fresh]) * 2
        + same([fresh], True) * 2
    )
    out = pl.pallas_call(
        functools.partial(ending_kernel, count),
        out_shape=shapes,
        in_specs=[WHOLE] * 6 + [ANY] * (2 * count + 1),
        out_specs=[WHOLE] * 2 + [ANY] * (len(shapes) - 2),
        scratch_shapes=[
            pltpu.VMEM((8, width), f32),
            pltpu.VMEM((3, 8, width), f32),
            pltpu.VMEM((shards - 1, 8, width // shards), f32),
        ]
        + pair(3)
        + pair(shards - 1)
        + pair(4 * count)
        + pair(2 * count)
        + pair(3)
        + pair(4)
        + pair(2)
        + reduce_scratch(rows, width),
        compiler_params=params(cid),
        cost_estimate=cost(75),
        name="make_ending",
    )(hidden, weight, middle, usable, parts_one, parts_two, *by_x, *by_y, fresh)
    rest = out[2:]
    groups = [rest[i * count : (i + 1) * count] for i in range(6)]
    f_x, f_y, f_sib, f_low, f_high, f_sib_x, f_sib_y, f_sib_low, f_sib_high = rest[6 * count :]
    whole = [fresh, f_x, f_y, f_low, f_high, f_sib, f_sib_x, f_sib_y, f_sib_low, f_sib_high]
    return out[0], out[1], groups, whole


MASKS = (0, 2, 4, 6, 6, 1, 3, 5, 7, 7)
WHEN = (2, 2, 2, 0, 1, 2, 2, 2, 0, 1)


def in_order(parts):
    value, by_x, by_y, low, high, sib, sib_x, sib_y, sib_low, sib_high = parts
    corner, sib_corner = jnp.concatenate([low, high]), jnp.concatenate([sib_low, sib_high])
    stacked = jnp.stack([value, sib, by_x, sib_x, by_y, sib_y, corner, sib_corner])
    return jnp.take(stacked, jnp.arange(8) ^ lax.axis_index("tp"), axis=0)


def widen_two_kernel(steps, shards, *refs):
    t = lax.axis_index("tp")
    late = (pl.program_id(0) >= steps // 2).astype(jnp.int32)
    seconds, downs, outs = refs[:10], refs[10:20], refs[20:30]
    gelu, up, down, out = refs[30:]
    unit = gelu.shape[1] // (8 * shards)

    def store(i):
        place = flip(t, MASKS[i])
        down[place] = downs[i][...].astype(f32)
        out[place] = outs[i][...].astype(f32)
        for z in range(shards):
            at = pl.ds(pl.multiple_of((8 * z + place) * unit, unit), unit)
            gelu[:, at] = seconds[i][:, z * unit : (z + 1) * unit].astype(f32)
            up[:, at] = seconds[i][:, (shards + z) * unit : (shards + z + 1) * unit].astype(f32)

    for i in range(10):
        if WHEN[i] == 2:
            store(i)
        else:

            @pl.when(late == WHEN[i])
            def _():
                store(i)


def widen_two(seconds, downs, outs, shards):
    rows, columns = seconds[0].shape
    count, width = downs[0].shape
    steps = 4

    def row_at(which, i):
        half = steps // 2
        return (i, jnp.minimum(i, half - 1), jnp.maximum(i - half, 0))[(which + 1) % 3]

    def specs(parts):
        return [
            pl.BlockSpec(
                (parts[0].shape[0] // steps, parts[0].shape[1]),
                functools.partial(lambda w, i: (row_at(w, i), 0), w),
            )
            for w in WHEN
        ]

    units = jax.ShapeDtypeStruct((rows, 4 * columns), f32)
    stack = jax.ShapeDtypeStruct((8, count, width), f32)
    gelu, up, down, out = pl.pallas_call(
        functools.partial(widen_two_kernel, steps, shards),
        grid=(steps,),
        in_specs=specs(seconds) + specs(downs) + specs(outs),
        out_specs=[pl.BlockSpec((rows // steps, 4 * columns), lambda i: (i, 0))] * 2
        + [pl.BlockSpec((8, count // steps, width), lambda i: (0, i, 0))] * 2,
        out_shape=[units, units, stack, stack],
        compiler_params=params(),
        cost_estimate=cost(25),
        name="widen_two",
    )(*seconds, *downs, *outs)
    return gelu, up, down.reshape(8 * count, width), out.reshape(8 * count, width)


def widen_one_kernel(edges, parts, _after, *goals):
    for goal, (begin, end) in zip(goals, zip(edges, edges[1:])):
        size = end - begin
        for i in range(8):
            goal[:, i * size : (i + 1) * size] = parts[i, :, begin:end].astype(f32)


def widen_one(parts, edges, after):
    _, rows, columns = parts.shape
    sizes = [b - a for a, b in zip(edges, edges[1:])]
    block = 64
    return pl.pallas_call(
        functools.partial(widen_one_kernel, edges),
        grid=(rows // block,),
        in_specs=[pl.BlockSpec((8, block, columns), lambda i: (0, i, 0)), ANY],
        out_specs=[pl.BlockSpec((block, 8 * size), lambda i: (i, 0)) for size in sizes],
        out_shape=[jax.ShapeDtypeStruct((rows, 8 * size), f32) for size in sizes],
        compiler_params=params(),
        cost_estimate=cost(14),
        name="widen_one",
    )(parts, after)


def local(
    tokens,
    cotangent,
    token_order,
    lengths,
    query_weight,
    key_weight,
    value_weight,
    gate_weight,
    out_weight,
    gelu_weight,
    up_weight,
    down_weight,
    gain_one,
    shift_one,
    gain_two,
    shift_two,
):
    every = ("outer", "tp", "shard")
    device_count = lax.axis_size(every)
    device_index = lax.axis_index(every)
    outer, tp, shards = lax.axis_size("outer"), lax.axis_size("tp"), lax.axis_size("shard")
    t, z = lax.axis_index("tp"), lax.axis_index("shard")
    rows, width = tokens.shape
    packs = lengths.shape[0]
    pack_rows = rows // packs
    group_rows = tp * rows
    group_packs = tp * packs

    own_order = lax.dynamic_slice_in_dim(token_order, device_index * rows, rows)
    target = own_order // rows
    places = jnp.arange(rows, dtype=jnp.int32)
    before = (target[None, :] < target[:, None]) | (
        (target[None, :] == target[:, None]) & (places[None, :] < places[:, None])
    )
    send_place = jnp.sum(before.astype(jnp.int32), axis=1)
    send_mix = (send_place[None, :] == places[:, None]).astype(bf16)
    loader_ids = jnp.arange(token_order.shape[0], dtype=jnp.int32)
    slot_targets = device_index * rows + places
    origin = jnp.sum(
        jnp.where(token_order[None, :] == slot_targets[:, None], loader_ids[None, :], 0), axis=1
    )
    arrive_place = jnp.sum((origin[None, :] < origin[:, None]).astype(jnp.int32), axis=1)
    work_mix = (arrive_place[:, None] == places[None, :]).astype(bf16)

    def exchange(value):
        return lax.all_to_all(
            value.reshape(device_count, rows // device_count, width),
            every,
            split_axis=0,
            concat_axis=0,
            tiled=True,
        ).reshape(rows, width)

    def along_z(piece):
        return lax.all_gather(piece, "shard", axis=0, tiled=True)

    def cut(weight):
        part = weight.shape[1] // tp
        return lax.dynamic_slice_in_dim(weight, t * part, part, axis=1)

    out_unit = out_weight.shape[0] // tp
    unit = down_weight.shape[0] // tp
    piece_rows = query_weight.shape[0]
    key_part, value_part = query_weight.shape[1] // tp, value_weight.shape[1] // tp
    edges = (0, key_part, 2 * key_part, 2 * key_part + value_part)
    first_size = 2 * key_part + 2 * value_part
    hidden_part = shards * unit

    def fold(value):
        cuts = piece_rows // value.shape[0]
        value = value.reshape(value.shape[0], cuts, width // cuts)
        return jnp.transpose(value, (1, 0, 2)).reshape(piece_rows, width // cuts)

    def unfold(value, count):
        cuts = piece_rows // count
        value = value.reshape(shards, cuts, count, width // cuts)
        return jnp.transpose(value, (0, 2, 1, 3)).reshape(shards, count, width)

    out_piece = lax.dynamic_slice_in_dim(out_weight, t * out_unit, out_unit, axis=0)
    w_one = along_z(
        jnp.concatenate(
            [cut(w) for w in (query_weight, key_weight, value_weight, gate_weight)]
            + [fold(out_piece)],
            axis=1,
        )
    )
    ends = jnp.cumsum(lengths, axis=1, dtype=jnp.int32)[:, -2]
    usable = (jnp.arange(pack_rows, dtype=jnp.int32)[None, :] < ends[:, None]).astype(f32)
    usable = usable.reshape(rows, 1)
    lens = jnp.pad(lengths, ((0, 8 - packs), (0, 128 - lengths.shape[1])))
    came = exchange(forward_dot(send_mix, tokens).astype(bf16))
    came_back = exchange(forward_dot(send_mix, cotangent).astype(bf16))
    gains = jnp.stack([gain_one, shift_one, gain_two, shift_two]).astype(f32)
    gains = jnp.concatenate([gains, jnp.zeros_like(gains)], axis=0)
    x, normed, all_lengths, small = entry(came, work_mix, gains, lens, 0)
    t_late = t + jnp.minimum(all_lengths[0, 0, 0], 0)

    def unit_columns(weight):
        split = weight.reshape(weight.shape[0], shards, tp, unit)
        split = lax.dynamic_slice_in_dim(split, t_late, 1, axis=2)
        return split.reshape(weight.shape[0], hidden_part)

    down_piece = lax.dynamic_slice_in_dim(down_weight, t_late * unit, unit, axis=0)
    w_two = along_z(
        jnp.concatenate(
            [unit_columns(gelu_weight), unit_columns(up_weight), fold(down_piece)], axis=1
        )
    )
    back_out, back_low = entry_back(came_back, work_mix, usable, x, 7)
    normed, back_low = normed.reshape(group_rows, width), back_low.reshape(group_rows, width)
    all_lengths = all_lengths[:, :packs, : lengths.shape[1]].reshape(group_packs, -1)
    cosine, sine, decays, _ = pack_tables(all_lengths, pack_rows, t + jnp.arange(1))
    cosine, sine = cosine.reshape(group_rows, -1), sine.reshape(group_rows, -1)
    decays = decays[0]
    out_pieces = unfold(w_one[:, first_size:], out_unit)
    q_rot, k_rot, v_low, weights_low, gating, retained, branch, wo = retain(
        normed, w_one, value_part, cosine, sine, decays, out_pieces, rows, 1
    )
    wo = wo.reshape(shards * out_unit, width)
    middle, normed_two = make_middle(branch, wo, x, small, 2)
    normed_two = normed_two.reshape(group_rows, width)

    hidden, second_low, w_down = feed(normed_two, back_low, w_two, hidden_part, shards, rows)
    down_gram = gram_rows(hidden, back_low).astype(bf16)
    second_gram = gram_rows(normed_two, second_low).astype(bf16)

    def to_owner(value):
        part = lax.psum_scatter(value, "shard", scatter_dimension=0, tiled=True)
        return lax.psum(part, "outer") if outer > 1 else part

    down_sum, second_sum = to_owner(down_gram), to_owner(second_gram)
    back_middle, parts_two, middle_low = make_back_middle(
        second_low, w_two, middle, back_out, small, down_gram, second_gram, 3
    )
    middle_low = middle_low.reshape(group_rows, width)
    out_gram = gram_rows(branch, middle_low).astype(bf16).reshape(shards, out_unit, width)
    first_low, dealt = retain_back(
        middle_low, wo, q_rot, k_rot, v_low, weights_low, gating, retained, cosine, sine, decays,
        out_gram, rows, 8,
    )
    out_sum = to_owner(dealt.reshape(shards * out_unit, width))
    first_gram = gram_rows(normed, first_low).astype(bf16)
    first_gram, second_sum, down_sum = lax.optimization_barrier((first_gram, second_sum, down_sum))
    first_sum = to_owner(first_gram)
    values = [second_sum, down_sum]
    back_inputs, parts_one, by_x, by_y, by_sib = make_back_input(
        first_low, w_one, x, back_middle, small, values, 4
    )
    ending, sums, groups, outs = make_ending(
        hidden, w_down, middle, usable, parts_one, parts_two, by_x, by_y, out_sum, 5
    )
    low, high, sib_x, sib_y, sib_low, sib_high = groups
    seconds, downs = (
        [
            values[k], by_x[k], by_y[k], low[k], high[k],
            by_sib[k], sib_x[k], sib_y[k], sib_low[k], sib_high[k],
        ]
        for k in range(2)
    )

    if unit % 128 == 0:
        gelu_gradient, up_gradient, down_gradient, out_gradient = widen_two(
            seconds, downs, outs, shards
        )
    else:
        down_gradient = in_order(downs).reshape(-1, width).astype(f32)
        out_gradient = in_order(outs).reshape(-1, width).astype(f32)
        both = in_order(seconds).reshape(tp, piece_rows, 2, shards, unit)
        both = jnp.transpose(both, (2, 1, 3, 0, 4)).reshape(2, piece_rows, -1).astype(f32)
        gelu_gradient, up_gradient = both[0], both[1]
    firsts = lax.all_gather(first_sum + sums[5, 0].astype(bf16), "tp", axis=0)
    query_gradient, key_gradient, value_gradient, gate_gradient = widen_one(
        firsts, edges + (first_size,), down_gradient
    )
    smalls = lax.psum(sums, "outer") if outer > 1 else sums

    def give_back(value):
        home = exchange(gram_rows(work_mix, value).astype(bf16))
        return gram_rows(send_mix, home).astype(bf16)

    result = give_back(ending)
    token_gradient = give_back(back_inputs)
    return (
        result,
        token_gradient,
        query_gradient,
        key_gradient,
        value_gradient,
        gate_gradient,
        out_gradient,
        gelu_gradient,
        up_gradient,
        down_gradient,
        smalls[0],
        smalls[1],
        smalls[2],
        smalls[3],
    )


def solution(mesh):
    tp = math.gcd(mesh.shape["rep"], HEADS)
    grid = mesh.devices.reshape(mesh.shape["rep"] // tp, tp, mesh.shape["shard"])
    cube = Mesh(grid, ("outer", "tp", "shard"))
    tokens_at = P(("outer", "tp", "shard"), None)
    weights_at = P("shard", None)
    vectors_at = P("shard")
    in_specs = (tokens_at, tokens_at, P(), tokens_at) + (weights_at,) * 8 + (vectors_at,) * 4
    out_specs = (tokens_at, tokens_at) + (weights_at,) * 8 + (vectors_at,) * 4
    return jax.shard_map(local, mesh=cube, in_specs=in_specs, out_specs=out_specs, check_vma=False)
```

time: 1800 us -> 857 us (0.48)
  waiting for transfers between devices: 1230 us -> 81.7 us
  Pallas kernels: 0 us -> 609 us
  matrix products: 249 us -> 60.9 us
  blocking collectives: 95.3 us -> 0 us
  other arithmetic: 88.9 us -> 15.2 us
  local copies, waits for them, and re-layouts: 84 us -> 40.4 us
    pallas_call x0 -> x11, Pallas kernels: none -> 609 us  [the longest x1 103 us: entry(): pl.pallas_call(entry_kernel, out_shape=(jax.ShapeDtypeStruct((rows, width...]
    reduce_scatter x11 -> x4, waiting for transfers between devices: 420 us -> 0.03 us  [to_owner(): part = lax.psum_scatter(value, 'shard', scatter_dimension=0, tiled=True)]
    all_gather x11 -> x1, waiting for transfers between devices: 357 us -> 24.1 us  [local(): firsts = lax.all_gather(first_sum + sums[5, 0].astype(bf16), 'tp', axis=0)]
    psum x3 -> x0, waiting for transfers between devices: 240 us -> none  [the longest x1 85.7 us: local(): lax.psum(gram_rows(branch, middle_low).astype(bf16), 'shard')]
    all_gather x7 -> x2, waiting for transfers between devices: 165 us -> 0.04 us  [along_z(): return lax.all_gather(piece, 'shard', axis=0, tiled=True)]
    dot_general x14 -> x0, matrix products: 97.4 us -> none  [the longest x8 92.3 us: back_through(): lax.dot_general(incoming, matrix, (((1,), (1,)), ((), ())), preferred_ele...]
    dot_general x12 -> x2, matrix products: 79.4 us -> 2.83 us  [forward_dot(): return jnp.dot(inputs, matrix, preferred_element_type=f32)]
    all_gather x2 -> x0, blocking collectives: 55.8 us -> none  [the longest x1 47.1 us: along_z(): return lax.all_gather(piece, 'shard', axis=0, tiled=True)]
  transfers between devices with their start and end apart: 36 -> 11, of which waited for: 29 -> 4; matrix products, arithmetic and copies ran while one was open for 20% -> 11% of each run, Pallas kernels for 0% -> 68%
where the time goes in v2:
time: 857 us; the launch traced here: 852 us
  Pallas kernels  609 us (71%)
  waiting for transfers between devices  81.7 us (10%)
  matrix products  60.9 us (7%)
  local copies, waits for them, and re-layouts  40.4 us (5%)
  starting transfers between devices  29 us (3%)
  between operations  15.6 us (2%)
  other arithmetic  15.2 us (2%)
    pallas_call x1, Pallas kernels, entry(): pl.pallas_call(entry_kernel, out_shape=(jax.ShapeDtypeStruct((rows, width...  103 us
    pallas_call x1, Pallas kernels, make_back_middle(): pl.pallas_call(back_middle_kernel, out_shape=(jax.ShapeDtypeStruct((rows,...  92.6 us
    pallas_call x1, Pallas kernels, make_middle(): pl.pallas_call(middle_kernel, out_shape=(jax.ShapeDtypeStruct((rows, widt...  90.1 us
    pallas_call x1, Pallas kernels, make_ending(): pl.pallas_call(functools.partial(ending_kernel, count), out_shape=shapes,...  86.5 us
    pallas_call x1, Pallas kernels, make_back_input(): pl.pallas_call(functools.partial(back_input_kernel, count), out_shape=[ja...  82.3 us
    dot_general x8, matrix products, gram_rows(): lax.dot_general(leading, trailing, (((0,), (0,)), ((), ())), preferred_el...  58.1 us
    all_to_all x4, waiting for transfers between devices, exchange(): lax.all_to_all(value.reshape(device_count, rows // device_count, width),...  57.5 us
    pallas_call x1, Pallas kernels, entry_back(): pl.pallas_call(entry_back_kernel, out_shape=(jax.ShapeDtypeStruct((rows,...  45.5 us
  transfers between devices with their start and end apart: 11, of which 4 were waited for; matrix products, arithmetic and copies ran while one was open for 11% of the time, Pallas kernels for 68%

profile of v2, /device:TPU:0, one launch (start us, length us, event | category | flops | bytes accessed | tf_op | source)
XLA Modules:
  0.0 851.6 jit_solution(16247350855289974450)
XLA Ops:
  7.2 1.2 constant_dynamic-slice_fusion.1
  8.7 1.0 copy.43
  11.7 1.1 dynamic-slice_dynamic-update-slice_fusion.1
  12.9 1.1 dynamic-slice_dynamic-update-slice_fusion
  14.0 1.1 constant_dynamic-update-slice_fusion
  15.1 1.3 copy-done.3
  16.8 1.4 fusion
  18.2 7.3 all-to-all-start
  27.5 6.2 copy.60
  33.7 3.3 copy.58
  37.6 1.2 select_reduce_fusion
  39.1 1.4 fusion.1
  41.3 28.1 %all-to-all-done = bf16[32,8,2048]{2,1,0:T(8,128)(2,1)S(1)} async-done(((bf16[32,8,2048]{2,1,0:T(8,128)(2,1)}), bf16[32,8,2048]{2,1,0:T(8,128)(2,1)S(1)}, u32[]{:S(2)}, u32[]{:S(2)}) %all-to-all-start) | async-done | bytes 1048608 | tf_op jit(solution)/shard_map/all_to_all | solution.py:1101
  69.4 12.0 %all-to-all-start.1 = ((bf16[32,8,2048]{2,1,0:T(8,128)(2,1)}), bf16[32,8,2048]{2,1,0:T(8,128)(2,1)S(1)}, u32[]{:S(2)}, u32[]{:S(2)}) async-start(bf16[32,8,2048]{2,1,0:T(8,128)(2,1)} %fusion.1), calls=%async_computation.1 | async-start | bytes 2097152 | tf_op jit(solution)/shard_map/all_to_all | solution.py:1101
  81.9 103.3 %entry.1 = (bf16[256,2048]{1,0:T(8,128)(2,1)}, bf16[8,256,2048]{2,1,0:T(8,128)(2,1)}, s32[8,8,128]{2,1,0:T(8,128)}, f32[8,2048]{1,0:T(8,128)}) custom-call(bf16[256,2048]{1,0:T(8,128)(2,1)} %bitcast.91, bf16[256,256]{1,0:T(8,128)(2,1)} %fusion.6.mix, f32[8,512]{1,0:T(8,128)} %fusion.23.gains, s32[8,128]{1,0:T(8,128)} %pad.6.lens), custom_call_target="tpu_custom_call" | custom-call | flops 49999998976 | bytes 150000000 | tf_op jit(solution)/shard_map/entry/pallas_call | solution.py:358
  186.3 1.2 slice.31
  188.2 1.1 constant_dynamic-slice_fusion
  189.8 10.3 %dynamic-slice_reduce_fusion = (bf16[512,4,128]{2,1,0:T(4,128)(2,1)S(1)}, bf16[512,4,128]{2,1,0:T(4,128)(2,1)S(1)}) fusion(bf16[512,4,8,128]{3,2,1,0:T(8,128)(2,1)} %bitcast.76, s32[]{:T(128)S(6)} %select_n.49, bf16[512,4,8,128]{3,2,1,0:T(8,128)(2,1)} %bitcast.77), kind=kLoop, calls=%fused_computation.20 | loop fusion | bytes 2097156 | tf_op jit(solution)/shard_map/dynamic_slice | solution.py:1155
  200.3 1.2 pad_maximum_fusion
  201.9 1.3 and_select_fusion.decays
  203.3 5.5 multiply_sine_fusion
  209.7 45.5 %entry_back.1 = (bf16[256,2048]{1,0:T(8,128)(2,1)}, bf16[8,256,2048]{2,1,0:T(8,128)(2,1)}) custom-call(bf16[256,2048]{1,0:T(8,128)(2,1)} %bitcast.90, bf16[256,256]{1,0:T(8,128)(2,1)} %fusion.6.mix, f32[256,1]{1,0:T(8,128)} %copy.47.usable, bf16[256,2048]{1,0:T(8,128)(2,1)} %get-tuple-element.84.x._after), custom_call_target="tpu_custom_call" | custom-call | flops 44999999488 | bytes 135000000 | tf_op jit(solution)/shard_map/entry_back/pallas_call | solution.py:396
  255.3 1.6 slice-done
  256.9 1.6 copy.57
  258.5 29.5 %retain.1 = (bf16[2048,256]{1,0:T(8,128)(2,1)}, bf16[2048,256]{1,0:T(8,128)(2,1)}, bf16[2048,512]{1,0:T(8,128)(2,1)}, bf16[16,128,128]{2,1,0:T(8,128)(2,1)}, f32...) custom-call(bf16[2048,2048]{1,0:T(8,128)(2,1)} %bitcast.100, ...), custom_call_target="tpu_custom_call" | custom-call | flops 24000000000 | bytes 72000000 | tf_op jit(solution)/shard_map/retain/pallas_call | solution.py:521
  288.0 90.1 %make_middle.1 = (f32[256,2048]{1,0:T(8,128)}, bf16[8,256,2048]{2,1,0:T(8,128)(2,1)}) custom-call(bf16[2048,512]{1,0:T(8,128)(2,1)} %get-tuple-element.82.branch, bf16[512,2048]{1,0:T(8,128)(2,1)} %bitcast.111, bf16[256,2048]{1,0:T(8,128)(2,1)} %get-tuple-element.84.x._after, f32[8,2048]{1,0:T(8,128)} %get-tuple-element.85.small), custom_call_target="tpu_custom_call" | custom-call | flops 85000003584 | bytes 255000000 | tf_op jit(solution)/shard_map/make_middle/pallas_call | solution.py:672
  378.2 19.2 %feed.1 = (bf16[2048,512]{1,0:T(8,128)(2,1)}, bf16[2048,1024]{1,0:T(8,128)(2,1)}, bf16[512,2048]{1,0:T(8,128)(2,1)}) custom-call(bf16[2048,2048]{1,0:T(8,128)(2,1)} %bitcast.107, bf16[2048,2048]{1,0:T(8,128)(2,1)} %bitcast.105, bf16[2048,1536]{1,0:T(8,128)(2,1)} %all-gather.7.cloned.1.call-done.w_two.weight), custom_call_target="tpu_custom_call" | custom-call | flops 17999998976 | bytes 54000000 | tf_op jit(solution)/shard_map/feed/pallas_call | solution.py:639
  397.4 9.9 %convolution_convert_fusion.3._after = bf16[512,2048]{1,0:T(8,128)(2,1)} fusion(bf16[2048,512]{1,0:T(8,128)(2,1)} %get-tuple-element.88.hidden, bf16[2048,2048]{1,0:T(8,128)(2,1)} %bitcast.106), kind=kOutput, calls=%fused_computation.4 | convolution fusion | flops 4296015872 | bytes 12582912 | tf_op jit(solution)/shard_map/dot_general | solution.py:54
  407.6 14.0 %convolution_convert_fusion.1._more = bf16[2048,1024]{1,0:T(8,128)(2,1)} fusion(bf16[2048,2048]{1,0:T(8,128)(2,1)} %bitcast.108, bf16[2048,1024]{1,0:T(8,128)(2,1)} %get-tuple-element.91.low), kind=kOutput, calls=%fused_computation.2 | convolution fusion | flops 8592031744 | bytes 16777216 | tf_op jit(solution)/shard_map/dot_general | solution.py:54
  421.7 92.6 %make_back_middle.1 = (f32[256,2048]{1,0:T(8,128)}, f32[8,2048]{1,0:T(8,128)}, bf16[8,256,2048]{2,1,0:T(8,128)(2,1)}) custom-call(bf16[2048,1024]{1,0:T(8,128)(2,1)} %get-tuple-element.91.low, bf16[2048,1536]{1,0:T(8,128)(2,1)} %all-gather.7.cloned.1.call-done.w_two.weight, f32[256,2048]{1,0:T(8,128)} %get-tuple-element.90.middle, ...), custom_call_target="tpu_custom_call" | custom-call | flops 89999998976 | bytes 270000000 | tf_op jit(solution)/shard_map/make_back_middle/pallas_call | solution.py:723
  514.2 9.1 %convolution_convert_fusion.2 = bf16[512,2048]{1,0:T(8,128)(2,1)} fusion(bf16[2048,512]{1,0:T(8,128)(2,1)S(1)} %copy-done.20, bf16[2048,2048]{1,0:T(8,128)(2,1)} %bitcast.109), kind=kOutput, calls=%fused_computation.3 | convolution fusion | flops 4296015872 | bytes 12582912 | tf_op jit(solution)/shard_map/dot_general | solution.py:54
  523.4 28.7 %retain_back.1 = (bf16[2048,1536]{1,0:T(8,128)(2,1)}, bf16[4,128,2048]{2,1,0:T(8,128)(2,1)}) custom-call(bf16[2048,2048]{1,0:T(8,128)(2,1)} %bitcast.110, bf16[512,2048]{1,0:T(8,128)(2,1)} %bitcast.112, bf16[2048,256]{1,0:T(8,128)(2,1)} %get-tuple-element.94.q_in, bf16[2048,256]{1,0:T(8,128)(2,1)} %get-tuple-element.95.k_in, ...), custom_call_target="tpu_custom_call" | custom-call | flops 20000000000 | bytes 60000000 | tf_op jit(solution)/shard_map/retain_back/pallas_call | solution.py:591
  552.5 19.1 %convolution_convert_fusion = bf16[2048,1536]{1,0:T(8,128)(2,1)} fusion(bf16[2048,2048]{1,0:T(8,128)(2,1)} %bitcast.101, bf16[2048,1536]{1,0:T(8,128)(2,1)} %get-tuple-element.100.low), kind=kOutput, calls=%fused_computation.1 | convolution fusion | flops 12888047616 | bytes 20971520 | tf_op jit(solution)/shard_map/dot_general | solution.py:54
  571.7 82.3 %make_back_input.1 = (bf16[256,2048]{1,0:T(8,128)(2,1)}, f32[8,2048]{1,0:T(8,128)}, bf16[512,1024]{1,0:T(8,128)(2,1)}, bf16[128,2048]{1,0:T(8,128)(2,1)}, bf16[5...) custom-call(bf16[2048,1536]{1,0:T(8,128)(2,1)} %get-tuple-element.100.lo, ...), custom_call_target="tpu_custom_call" | custom-call | flops 80000000000 | bytes 240000000 | tf_op jit(solution)/shard_map/make_back_input/pallas_call | solution.py:821
  654.0 86.5 %make_ending.1 = (bf16[256,2048]{1,0:T(8,128)(2,1)}, f32[8,512]{1,0:T(8,128)}, bf16[256,1024]{1,0:T(8,128)(2,1)}, bf16[64,2048]{1,0:T(8,128)(2,1)}, bf16[256,102...) custom-call(bf16[2048,512]{1,0:T(8,128)(2,1)} %get-tuple-element.88., ...), custom_call_target="tpu_custom_call" | custom-call | flops 74999996416 | bytes 225000000 | tf_op jit(solution)/shard_map/make_ending/pallas_call | solution.py:932
  740.5 1.3 slice.38
  741.8 3.4 broadcast_add_fusion
  745.3 1.5 fusion.2
  746.8 3.6 all-to-all-start.2
  750.4 1.5 fusion.3
  752.5 22.9 %all-to-all-done.2 = bf16[32,8,2048]{2,1,0:T(8,128)(2,1)S(1)} async-done(((bf16[32,8,2048]{2,1,0:T(8,128)(2,1)}), bf16[32,8,2048]{2,1,0:T(8,128)(2,1)S(1)}, u32[]{:S(2)}, u32[]{:S(2)}) %all-to-all-start.2) | async-done | bytes 1048608 | tf_op jit(solution)/shard_map/all_to_all | solution.py:1101
  775.4 4.6 all-to-all-start.3
  780.0 17.1 %widen_two.1 = (f32[512,4096]{1,0:T(8,128)}, f32[512,4096]{1,0:T(8,128)}, f32[8,128,2048]{2,1,0:T(8,128)}, f32[8,128,2048]{2,1,0:T(8,128)}) custom-call(bf16[512,1024]{1,0:T(8,128)(2,1)} %reduce-scatter.5.cloned.1.call-done.refs_0_, bf16[512,1024]{1,0:T(8,128)(2,1)} %get-tuple-element.106.refs_0_.refs_1_, bf16[512,1024]{1,0:T(8,128)(2,1)} %get-tuple-element.108.refs_2_, ...), custom_call_target="tpu_custom_call" | custom-call | flops 24999999488 | bytes 75000000 | tf_op jit(solution)/shard_map/widen_two/pallas_call | solution.py:1018
  797.2 1.5 convolution_convert_fusion.6
  798.6 6.4 all-to-all-done.3
  805.1 1.5 convolution_convert_fusion.4
  806.5 24.1 %all-gather.9.cloned.1.call-done = bf16[4096,1536]{1,0:T(8,128)(2,1)} async-done(((bf16[512,1536]{1,0:T(8,128)(2,1)}), bf16[4096,1536]{1,0:T(8,128)(2,1)}) %all-gather.9.cloned.1.call-update) | async-done | bytes 12582928 | tf_op jit(solution)/shard_map/all_gather | solution.py:1226
  830.6 14.0 %widen_one.1 = (f32[512,2048]{1,0:T(8,128)}, f32[512,2048]{1,0:T(8,128)}, f32[512,4096]{1,0:T(8,128)}, f32[512,4096]{1,0:T(8,128)}) custom-call(bf16[8,512,1536]{2,1,0:T(8,128)(2,1)} %bitcast.99, f32[1024,2048]{1,0:T(8,128)} %bitcast.102), custom_call_target="tpu_custom_call" | custom-call | flops 14000000000 | bytes 42000000 | tf_op jit(solution)/shard_map/widen_one/pallas_call | solution.py:1043
  (98 shorter events, 11.3 us)
Async XLA Ops:
  7.2 9.6 %copy-start = (bf16[256,2048]{1,0:T(8,128)(2,1)S(1)}, bf16[256,2048]{1,0:T(8,128)(2,1)}, u32[]{:S(2)}) copy-start(bf16[256,2048]{1,0:T(8,128)(2,1)} %param.16) | copy-start | bytes 3145732
  7.2 248.0 %all-gather.5.cloned.1.call-start = ((), (), s32[]{:S(2)}) async-start(), calls=%async_computation.8 | async-start | bytes 10485760 | tf_op jit(solution)/shard_map/all_gather | solution.py:1110
  8.4 8.1 copy-start.9
  12.8 12.7 %copy-start.15 = (s32[2,4]{1,0:T(2,128)S(1)}, s32[2,4]{1,0:T(2,128)}, u32[]{:S(2)}) copy-start(s32[2,4]{1,0:T(2,128)} %param.19) | copy-start | bytes 100
  12.8 13.5 %copy-start.16 = (bf16[512]{0:T(512)(128)(2,1)S(1)}, bf16[512]{0:T(512)(128)(2,1)}, u32[]{:S(2)}) copy-start(bf16[512]{0:T(512)(128)(2,1)} %param.31) | copy-start | bytes 3076
  12.8 13.5 %copy-start.17 = (bf16[512]{0:T(512)(128)(2,1)S(1)}, bf16[512]{0:T(512)(128)(2,1)}, u32[]{:S(2)}) copy-start(bf16[512]{0:T(512)(128)(2,1)} %param.30) | copy-start | bytes 3076
  12.8 13.5 %copy-start.18 = (bf16[512]{0:T(512)(128)(2,1)S(1)}, bf16[512]{0:T(512)(128)(2,1)}, u32[]{:S(2)}) copy-start(bf16[512]{0:T(512)(128)(2,1)} %param.29) | copy-start | bytes 3076
  12.8 13.5 %copy-start.19 = (bf16[512]{0:T(512)(128)(2,1)S(1)}, bf16[512]{0:T(512)(128)(2,1)}, u32[]{:S(2)}) copy-start(bf16[512]{0:T(512)(128)(2,1)} %param.28) | copy-start | bytes 3076
  15.1 1.3 copy-start.3
  16.8 22.3 %copy-start.10 = (s32[256]{0:T(256)}, s32[256]{0:T(256)S(1)}, u32[]{:S(2)}) copy-start(s32[256]{0:T(256)S(1)} %convert_reduce_fusion.1) | copy-start | bytes 3076
  18.2 51.2 %all-to-all-start = ((bf16[32,8,2048]{2,1,0:T(8,128)(2,1)}), bf16[32,8,2048]{2,1,0:T(8,128)(2,1)S(1)}, u32[]{:S(2)}, u32[]{:S(2)}) async-start(bf16[32,8,2048]{2,1,0:T(8,128)(2,1)} %fusion), calls=%async_computation | async-start | bytes 2097152 | tf_op jit(solution)/shard_map/all_to_all | solution.py:1101
  27.5 6.2 copy-start.2
  33.7 5.4 copy-start.6
  39.1 30.3 %copy-start.12 = (s32[256]{0:T(256)}, s32[256]{0:T(256)S(1)}, u32[]{:S(2)}) copy-start(s32[256]{0:T(256)S(1)} %convert_reduce_fusion) | copy-start | bytes 3076
  69.4 12.6 %copy-start.5 = (bf16[32,8,2048]{2,1,0:T(8,128)(2,1)}, bf16[32,8,2048]{2,1,0:T(8,128)(2,1)S(1)}, u32[]{:S(2)}) copy-start(bf16[32,8,2048]{2,1,0:T(8,128)(2,1)S(1)} %all-to-all-done) | copy-start | bytes 3145732
  69.4 139.4 %all-to-all-start.1 = ((bf16[32,8,2048]{2,1,0:T(8,128)(2,1)}), bf16[32,8,2048]{2,1,0:T(8,128)(2,1)S(1)}, u32[]{:S(2)}, u32[]{:S(2)}) async-start(bf16[32,8,2048]{2,1,0:T(8,128)(2,1)} %fusion.1), calls=%async_computation.1 | async-start | bytes 2097152 | tf_op jit(solution)/shard_map/all_to_all | solution.py:1101
  81.4 296.8 %all-gather.7.cloned.1.call-start = ((), (), s32[]{:S(2)}) async-start(), calls=%async_computation.9 | async-start | bytes 7864320 | tf_op jit(solution)/shard_map/all_gather | solution.py:1110
  201.5 370.1 %reduce-scatter.7.cloned.1.call-start = ((), (), s32[]{:S(2)}) async-start(), calls=%async_computation.11 | async-start | bytes 2621440 | tf_op jit(solution)/shard_map/reduce_scatter | solution.py:1183
  208.8 1.0 copy-start.4
  255.2 1.6 slice-start
  407.3 164.3 %reduce-scatter.5.cloned.1.call-start = ((), (), s32[]{:S(2)}) async-start(), calls=%async_computation.10 | async-start | bytes 5242880 | tf_op jit(solution)/shard_map/reduce_scatter | solution.py:1183
  421.6 232.4 %reduce-scatter.9.cloned.1.call-start = ((), (), s32[]{:S(2)}) async-start(), calls=%async_computation.12 | async-start | bytes 2621440 | tf_op jit(solution)/shard_map/reduce_scatter | solution.py:1183
  421.7 92.6 %copy-start.20 = (bf16[2048,512]{1,0:T(8,128)(2,1)S(1)}, bf16[2048,512]{1,0:T(8,128)(2,1)}, u32[]{:S(2)}) copy-start(bf16[2048,512]{1,0:T(8,128)(2,1)} %get-tuple-element.82.branch) | copy-start | bytes 6291460
  552.1 189.7 %reduce-scatter.11.cloned.1.call-start = ((), (), s32[]{:S(2)}) async-start(), calls=%async_computation.13 | async-start | bytes 7864320 | tf_op jit(solution)/shard_map/reduce_scatter | solution.py:1183
  571.7 259.0 %all-gather.9.cloned.1.call-start = ((), (), s32[]{:S(2)}) async-start(), calls=%async_computation.14 | async-start | bytes 14155776 | tf_op jit(solution)/shard_map/all_gather | solution.py:1226
  740.5 4.7 copy-start.8
  740.5 4.7 copy-start.13
  741.8 8.6 %copy-start.7 = (bf16[256,2048]{1,0:T(8,128)(2,1)S(1)}, bf16[256,2048]{1,0:T(8,128)(2,1)}, u32[]{:S(2)}) copy-start(bf16[256,2048]{1,0:T(8,128)(2,1)} %get-tuple-element.112) | copy-start | bytes 3145732
  745.2 6.7 copy-start.14
  746.8 28.7 %all-to-all-start.2 = ((bf16[32,8,2048]{2,1,0:T(8,128)(2,1)}), bf16[32,8,2048]{2,1,0:T(8,128)(2,1)S(1)}, u32[]{:S(2)}, u32[]{:S(2)}) async-start(bf16[32,8,2048]{2,1,0:T(8,128)(2,1)} %fusion.2), calls=%async_computation.5 | async-start | bytes 2097152 | tf_op jit(solution)/shard_map/all_to_all | solution.py:1101
  775.4 29.6 %all-to-all-start.3 = ((bf16[32,8,2048]{2,1,0:T(8,128)(2,1)}), bf16[32,8,2048]{2,1,0:T(8,128)(2,1)S(1)}, u32[]{:S(2)}, u32[]{:S(2)}) async-start(bf16[32,8,2048]{2,1,0:T(8,128)(2,1)} %fusion.3), calls=%async_computation.6 | async-start | bytes 2097152 | tf_op jit(solution)/shard_map/all_to_all | solution.py:1101
  780.0 17.2 %copy-start.11 = (s32[256]{0:T(256)S(1)}, s32[256]{0:T(256)}, u32[]{:S(2)}) copy-start(s32[256]{0:T(256)} %copy-done.10) | copy-start | bytes 3076
  830.6 14.0 %copy-start.1 = (bf16[256,2048]{1,0:T(8,128)(2,1)S(1)}, bf16[256,2048]{1,0:T(8,128)(2,1)}, u32[]{:S(2)}) copy-start(bf16[256,2048]{1,0:T(8,128)(2,1)} %param.16) | copy-start | bytes 3145732
Sparse Core Ops, SparseCore 0:
  16.6 194.2 all-gather.4
  213.0 114.4 all-gather.6
  407.5 41.9 reduce-scatter.6
  452.3 76.0 reduce-scatter.4
  552.2 43.1 reduce-scatter.8
  598.3 111.1 reduce-scatter.10
  745.4 85.2 all-gather.8

commit v3 on v2

--- a/solution.py
+++ b/solution.py
@@ -109,49 +109,62 @@
     )
 
 
-def gather_steps(me, own, out, send, recv):
-    rows = own.shape[0]
-    half = rows // 2
-    sib, xn, yn, dn = flip(me, 1), flip(me, 2), flip(me, 4), flip(me, 6)
-
-    def cp(i, src, goal, peer):
-        return push(src, goal, send.at[i], recv.at[i], peer)
-
+def gather_begin(me, own, out, send, recv):
+    half = own.shape[0] // 2
+    xn, yn = flip(me, 2), flip(me, 4)
     low, high = pl.ds(0, half), pl.ds(half, half)
     first = [
-        cp(0, own, out.at[me], xn),
-        cp(1, own, out.at[me], yn),
-        cp(2, own, out.at[me], sib),
+        push(own.at[part], out.at[me, part], send.at[i], recv.at[i], peer)
+        for i, (part, peer) in enumerate(((low, xn), (high, yn), (high, xn), (low, yn)))
     ]
+    first.append(push(own, out.at[me], send.at[4], recv.at[4], flip(me, 1)))
     for c in first:
         c.start()
+    return first
+
+
+def gather_end(me, own, out, send, recv, first):
+    half = own.shape[0] // 2
+    sib, xn, yn, dn = flip(me, 1), flip(me, 2), flip(me, 4), flip(me, 6)
+    low, high = pl.ds(0, half), pl.ds(half, half)
+    started = list(first)
+
+    def on(slot, part, peer):
+        i = len(started)
+        place = out.at[slot, part]
+        c = push(place, place, send.at[i], recv.at[i], peer)
+        c.start()
+        started.append(c)
+        return c
+
     first[0].wait_recv()
-    c3 = cp(3, out.at[xn, low], out.at[xn, low], yn)
-    c3.start()
-    c4 = cp(4, out.at[xn], out.at[xn], sib)
-    c4.start()
+    d_low = on(xn, low, yn)
     first[1].wait_recv()
-    c5 = cp(5, out.at[yn, high], out.at[yn, high], xn)
-    c5.start()
-    c6 = cp(6, out.at[yn], out.at[yn], sib)
-    c6.start()
-    c3.wait_recv()
-    c7 = cp(7, out.at[dn, low], out.at[dn, low], sib)
-    c7.start()
-    c5.wait_recv()
-    c8 = cp(8, out.at[dn, high], out.at[dn, high], sib)
-    c8.start()
+    d_high = on(yn, high, xn)
+    on(xn, low, sib)
+    on(yn, high, sib)
     first[2].wait_recv()
-    for c in (c4, c6, c7, c8):
-        c.wait_recv()
-    for c in first + [c3, c4, c5, c6, c7, c8]:
+    on(xn, high, sib)
+    first[3].wait_recv()
+    on(yn, low, sib)
+    d_low.wait_recv()
+    on(dn, low, sib)
+    d_high.wait_recv()
+    on(dn, high, sib)
+    for i in (4, 7, 8, 9, 10, 11, 12):
+        started[i].wait_recv()
+    for c in started:
         c.wait_send()
 
 
+def gather_steps(me, own, out, send, recv):
+    gather_end(me, own, out, send, recv, gather_begin(me, own, out, send, recv))
+
+
 COLS = 512
 
 
-def reduce_steps(me, pairs, transposed, tosib, fromsib, hold, hop, final, total, send, recv, between=None):
+def reduce_steps(me, pairs, transposed, tosib, fromsib, hold, hop, final, total, send, recv, hooks=()):
     rows, width = total.shape
     half = rows // 2
     sib, xn, yn = flip(me, 1), flip(me, 2), flip(me, 4)
@@ -205,6 +218,10 @@
             else:
                 total[:, at] = value
 
+    def hook(i):
+        if hooks:
+            hooks[i]()
+
     for_sibling(0)
     for_sibling(1)
     for_own_core(0)
@@ -212,6 +229,7 @@
     dy = cp(5, hold.at[0, high], hop.at[1], yn)
     dx.start()
     dy.start()
+    hook(0)
     for_sibling(2)
     for_own_core(1)
     xa = cp(6, hold.at[1, low], final.at[0, low], xn)
@@ -221,8 +239,7 @@
     yb = cp(7, hold.at[2, high], final.at[1, high], yn)
     yb.start()
     for_own_core(3)
-    if between is not None:
-        between()
+    hook(1)
     dy.wait_recv()
     hold[1, high] = (hold[1, high].astype(f32) + hop[1].astype(f32)).astype(bf16)
     xb = cp(8, hold.at[1, high], final.at[0, high], xn)
@@ -231,6 +248,7 @@
     hold[2, low] = (hold[2, low].astype(f32) + hop[0].astype(f32)).astype(bf16)
     ya = cp(9, hold.at[2, low], final.at[1, low], yn)
     ya.start()
+    hook(2)
     xa.wait_recv()
     yb.wait_recv()
     xb.wait_recv()
@@ -303,8 +321,8 @@
 def gather_scratch(rows, width):
     return [
         pltpu.VMEM((rows, width), bf16),
-        pltpu.SemaphoreType.DMA((9,)),
-        pltpu.SemaphoreType.DMA((9,)),
+        pltpu.SemaphoreType.DMA((13,)),
+        pltpu.SemaphoreType.DMA((13,)),
         pltpu.SemaphoreType.DMA,
     ]
 
@@ -316,35 +334,13 @@
     mine.wait()
 
 
-def entry_kernel(
-    came, mix, gains, lens, x_out, normed_all, lens_all, small,
-    own, send, recv, sem, send2, recv2, sem2, all_gains, send3, recv3,
-):
-    me = greet(True)
-    z = lax.axis_index("shard")
-    copies = []
-    for k, other in enumerate(others()):
-        c = pltpu.make_async_remote_copy(
-            src_ref=gains,
-            dst_ref=all_gains.at[z],
-            send_sem=send3.at[k],
-            recv_sem=recv3.at[k],
-            device_id={"shard": other},
-            device_id_type=MESHID,
-        )
-        c.start()
-        copies.append(c)
-    all_gains[z] = gains[...]
-    gather_all(me, lens, lens_all, send2, recv2, sem2)
-    for c in copies:
-        c.wait()
-    part = gains.shape[1]
-    for i in range(all_gains.shape[0]):
-        small[:, i * part : (i + 1) * part] = all_gains[i]
+def entry_kernel(came, mix, small, x_out, normed_all, own, send, recv, sem):
+    me = greet()
+    width = x_out.shape[1]
 
     @by_rows(came.shape[0])
     def _(at):
-        value = jnp.dot(mix[at, :], came[...], preferred_element_type=f32)
+        value = jnp.dot(mix[at, :], came[:, :width], preferred_element_type=f32)
         x_out[at, :] = value.astype(bf16)
         unit, _ = centre(value, layer_epsilon)
         own[at, :] = (unit * small[0:1, :] + small[1:2, :]).astype(bf16)
@@ -352,30 +348,21 @@
     gather_all(me, own, normed_all, send, recv, sem)
 
 
-def entry(came, mix, gains, lens, cid):
-    rows, width = came.shape
-    shards = lax.axis_size("shard")
+def entry(came, mix, small, cid):
+    rows, width = came.shape[0], small.shape[1]
     return pl.pallas_call(
         entry_kernel,
         out_shape=(
             jax.ShapeDtypeStruct((rows, width), bf16),
             jax.ShapeDtypeStruct((8, rows, width), bf16),
-            jax.ShapeDtypeStruct((8,) + lens.shape, lens.dtype),
-            jax.ShapeDtypeStruct((8, width), f32),
         ),
-        in_specs=[WHOLE] * 3 + [ANY],
-        out_specs=(WHOLE, ANY, ANY, WHOLE),
-        scratch_shapes=gather_scratch(rows, width)
-        + gather_scratch(rows, width)[1:]
-        + [
-            pltpu.VMEM((shards, 8, width // shards), f32),
-            pltpu.SemaphoreType.DMA((shards - 1,)),
-            pltpu.SemaphoreType.DMA((shards - 1,)),
-        ],
+        in_specs=[WHOLE] * 3,
+        out_specs=(WHOLE, ANY),
+        scratch_shapes=gather_scratch(rows, width),
         compiler_params=params(cid),
         cost_estimate=cost(50),
         name="entry",
-    )(came, mix, gains, lens)
+    )(came, mix, small)
 
 
 def entry_back_kernel(came, mix, usable, _after, back_out, back_all, own, send, recv, sem):
@@ -417,8 +404,7 @@
     return me, goals, sources, (me // heads if back else me % count), me // count == me % heads
 
 
-def deal_start(back, pieces, out, send, recv, local_sem):
-    count = pieces.shape[0]
+def deal_start(back, count, source, goal, send, recv, local_sem):
     me, goals, sources, slot, inside = deal_plan(back, count)
     barrier = pltpu.get_barrier_semaphore()
     for i in range(count):
@@ -434,29 +420,36 @@
 
         @pl.when(goals[i] == me)
         def _():
-            pltpu.make_async_copy(pieces.at[i], out.at[slot], local_sem).start()
+            pltpu.make_async_copy(source(i), goal(slot), local_sem).start()
 
         @pl.when(goals[i] != me)
         def _():
-            push(pieces.at[i], out.at[slot], send.at[i], recv.at[slot], goals[i]).start()
-
-
-def deal_wait(back, pieces, out, send, recv, local_sem):
-    count = pieces.shape[0]
+            push(source(i), goal(slot), send.at[i], recv.at[slot], goals[i]).start()
+
+
+def deal_wait(back, count, source, goal, send, recv, local_sem):
     me, goals, sources, slot, _ = deal_plan(back, count)
     for i in range(count):
 
         @pl.when(goals[i] == me)
         def _():
-            pltpu.make_async_copy(pieces.at[i], out.at[slot], local_sem).wait()
+            pltpu.make_async_copy(source(i), goal(slot), local_sem).wait()
 
         @pl.when(goals[i] != me)
         def _():
-            push(pieces.at[i], out.at[slot], send.at[i], recv.at[slot], goals[i]).wait_send()
+            push(source(i), goal(slot), send.at[i], recv.at[slot], goals[i]).wait_send()
 
         @pl.when(sources[i] != me)
         def _():
-            push(pieces.at[i], out.at[i], send.at[i], recv.at[i], sources[i]).wait_recv()
+            push(source(i), goal(i), send.at[i], recv.at[i], sources[i]).wait_recv()
+
+
+def blocks(ref):
+    return lambda i: ref.at[i]
+
+
+def column_blocks(ref, size):
+    return lambda i: ref.at[:, pl.ds(pl.multiple_of(i * size, size), size)]
 
 
 def deal_scratch(count):
@@ -467,6 +460,63 @@
     ]
 
 
+def phase_one_copies(me, values, by_x, by_y, by_sib, send, recv):
+    copies = []
+    for k, value in enumerate(values):
+        for i, (goal, mask) in enumerate(((by_x, 2), (by_y, 4), (by_sib, 1))):
+            n = 3 * k + i
+            copies.append(push(value, goal[k], send.at[n], recv.at[n], flip(me, mask)))
+    return copies
+
+
+def phase_one(*args):
+    copies = phase_one_copies(*args)
+    for c in copies:
+        c.start()
+    return copies
+
+
+def phase_two(me, by_x, by_y, low, high, sib_x, sib_y, send, recv):
+    copies = []
+    for k in range(len(by_x)):
+        half = by_x[k].shape[0] // 2
+        for i, (source, goal, mask) in enumerate(
+            (
+                (by_x[k].at[pl.ds(0, half)], low[k], 4),
+                (by_y[k].at[pl.ds(half, half)], high[k], 2),
+                (by_x[k], sib_x[k], 1),
+                (by_y[k], sib_y[k], 1),
+            )
+        ):
+            n = 4 * k + i
+            copies.append(push(source, goal, send.at[n], recv.at[n], flip(me, mask)))
+    for c in copies:
+        c.start()
+    return copies
+
+
+def phase_three(me, low, high, sib_low, sib_high, send, recv):
+    copies = []
+    for k in range(len(low)):
+        for i, (source, goal) in enumerate(((low[k], sib_low[k]), (high[k], sib_high[k]))):
+            n = 2 * k + i
+            copies.append(push(source, goal, send.at[n], recv.at[n], flip(me, 1)))
+    for c in copies:
+        c.start()
+    return copies
+
+
+def pair(count):
+    return [pltpu.SemaphoreType.DMA((count,)), pltpu.SemaphoreType.DMA((count,))]
+
+
+def same(values, halves=False):
+    return [
+        jax.ShapeDtypeStruct((v.shape[0] // 2 if halves else v.shape[0], v.shape[1]), v.dtype)
+        for v in values
+    ]
+
+
 def turn(value, cosine, sine):
     half = value.shape[-1] // 2
     a, b = value[:, :half], value[:, half:]
@@ -479,7 +529,7 @@
 ):
     @pl.when(pl.program_id(0) == 0)
     def _():
-        deal_start(False, pieces, wo, *sems)
+        deal_start(False, pieces.shape[0], blocks(pieces), blocks(wo), *sems)
 
     packs, span = decays.shape[0], decays.shape[1]
     value_at = 2 * KH
@@ -508,7 +558,7 @@
 
     @pl.when(pl.program_id(0) == pl.num_programs(0) - 1)
     def _():
-        deal_wait(False, pieces, wo, *sems)
+        deal_wait(False, pieces.shape[0], blocks(pieces), blocks(wo), *sems)
 
 
 def retain(normed, weight, value_size, cosine, sine, decays, pieces, block, cid):
@@ -542,13 +592,21 @@
     )(normed, weight, cosine, sine, decays, pieces)
 
 
+def phase_one_of(value, by, sems):
+    return phase_one_copies(lax.axis_index("tp"), [value], by[:1], by[1:2], by[2:], *sems)
+
+
 def retain_back_kernel(
-    middle_low, wo, q_in, k_in, v_in, w_in, g_in, r_in, cosine, sine, decays, pieces,
-    low, dealt, *sems
+    middle_low, wo, q_in, k_in, v_in, w_in, g_in, r_in, cosine, sine, decays, value,
+    low, by_x, by_y, by_sib, *sems
 ):
+    by = (by_x, by_y, by_sib)
+
     @pl.when(pl.program_id(0) == 0)
     def _():
-        deal_start(True, pieces, dealt, *sems)
+        greet()
+        for c in phase_one_of(value, by, sems):
+            c.start()
 
     packs, span = decays.shape[0], decays.shape[1]
     value_at = 2 * KH
@@ -579,10 +637,11 @@
 
     @pl.when(pl.program_id(0) == pl.num_programs(0) - 1)
     def _():
-        deal_wait(True, pieces, dealt, *sems)
-
-
-def retain_back(middle_low, wo, q, k, v, w, g, r, cosine, sine, decays, pieces, block, cid):
+        for c in phase_one_of(value, by, sems):
+            c.wait()
+
+
+def retain_back(middle_low, wo, q, k, v, w, g, r, cosine, sine, decays, value, block, cid):
     total, width = middle_low.shape
     span = decays.shape[1]
     value_size = v.shape[1]
@@ -595,23 +654,29 @@
             row(width), WHOLE, row(KH), row(KH), row(value_size), square, row(value_size),
             row(value_size), row(KH // 2), row(KH // 2), square, ANY,
         ],
-        out_specs=(row(2 * KH + 2 * value_size), ANY),
-        out_shape=(
+        out_specs=[row(2 * KH + 2 * value_size)] + [ANY] * 3,
+        out_shape=[
             jax.ShapeDtypeStruct((total, 2 * KH + 2 * value_size), bf16),
-            jax.ShapeDtypeStruct(pieces.shape, bf16),
-        ),
-        scratch_shapes=deal_scratch(pieces.shape[0]),
+        ]
+        + same([value]) * 3,
+        scratch_shapes=pair(3),
         compiler_params=params(cid),
         cost_estimate=cost(20),
         name="retain_back",
-    )(middle_low, wo, q, k, v, w, g, r, cosine, sine, decays, pieces)
-
-
-def feed_kernel(shards, normed_two, back_low, w_two, hidden, low, w_down):
+    )(middle_low, wo, q, k, v, w, g, r, cosine, sine, decays, value)
+
+
+def feed_kernel(shards, count, normed_two, back_low, w_two, branch, hidden, low, w_down, dealt, *sems):
     size = hidden.shape[1]
+    views = (
+        column_blocks(branch, branch.shape[1] // count) if count else None,
+        column_blocks(dealt, branch.shape[1] // count) if count else None,
+    )
 
     @pl.when(pl.program_id(0) == 0)
     def _():
+        if count:
+            deal_start(True, count, *views, *sems)
         unit = size // shards
         span = w_two.shape[0] // shards
         part = w_two.shape[1] - 2 * size
@@ -632,24 +697,76 @@
     low[:, :size] = (back * up * slope).astype(bf16)
     low[:, size:] = (back * value).astype(bf16)
 
-
-def feed(normed_two, back_low, w_two, size, shards, block):
+    if count:
+
+        @pl.when(pl.program_id(0) == pl.num_programs(0) - 1)
+        def _():
+            deal_wait(True, count, *views, *sems)
+
+
+def feed(normed_two, back_low, w_two, branch, size, shards, block, cid):
     total, width = normed_two.shape
     row = lambda w: pl.BlockSpec((block, w), lambda i: (i, 0))
-    return pl.pallas_call(
-        functools.partial(feed_kernel, shards),
+    count = shards if branch.shape[1] // shards % 128 == 0 else 0
+    hidden, low, w_down, dealt = pl.pallas_call(
+        functools.partial(feed_kernel, shards, count),
         grid=(total // block,),
-        in_specs=[row(width), row(width), WHOLE],
-        out_specs=(row(size), row(2 * size), pl.BlockSpec((size, width), lambda i: (0, 0))),
+        in_specs=[row(width), row(width), WHOLE, ANY],
+        out_specs=(row(size), row(2 * size), pl.BlockSpec((size, width), lambda i: (0, 0)), ANY),
         out_shape=(
             jax.ShapeDtypeStruct((total, size), bf16),
             jax.ShapeDtypeStruct((total, 2 * size), bf16),
             jax.ShapeDtypeStruct((size, width), bf16),
+            jax.ShapeDtypeStruct(branch.shape if count else (8, 128), bf16),
         ),
-        compiler_params=params(),
-        cost_estimate=cost(18),
+        scratch_shapes=deal_scratch(count) if count else [],
+        compiler_params=params(cid if count else None),
+        cost_estimate=cost(26),
         name="feed",
-    )(normed_two, back_low, w_two)
+    )(normed_two, back_low, w_two, branch)
+    if not count:
+        pieces = jnp.transpose(branch.reshape(total, shards, -1), (1, 0, 2))
+        pieces = lax.all_to_all(pieces, "tp", split_axis=0, concat_axis=0, tiled=True)
+        dealt = jnp.transpose(pieces, (1, 0, 2)).reshape(total, -1)
+    return hidden, low, w_down, dealt
+
+
+def gram_kernel(left, right, value, out_a, out_b, by_x, by_y, by_sib, send, recv):
+    by = (by_x, by_y, by_sib)
+
+    @pl.when(pl.program_id(0) == 0)
+    def _():
+        greet()
+        for c in phase_one_of(value, by, (send, recv)):
+            c.start()
+
+    both = lax.dot_general(
+        left[...], right[...], (((0,), (0,)), ((), ())), preferred_element_type=f32
+    ).astype(bf16)
+    out_a[...] = both[:, : out_a.shape[1]]
+    out_b[...] = both[:, out_a.shape[1] :]
+
+    @pl.when(pl.program_id(0) == pl.num_programs(0) - 1)
+    def _():
+        for c in phase_one_of(value, by, (send, recv)):
+            c.wait()
+
+
+def gram_beside(left, right, value, first, block, cid):
+    total, width = left.shape
+    sizes = (first, right.shape[1] - first)
+    return pl.pallas_call(
+        gram_kernel,
+        grid=(width // block,),
+        in_specs=[pl.BlockSpec((total, block), lambda i: (0, i)), WHOLE, ANY],
+        out_specs=[pl.BlockSpec((block, size), lambda i: (i, 0)) for size in sizes] + [ANY] * 3,
+        out_shape=[jax.ShapeDtypeStruct((width, size), bf16) for size in sizes]
+        + same([value]) * 3,
+        scratch_shapes=pair(3),
+        compiler_params=params(cid),
+        cost_estimate=cost(28),
+        name="gram_beside",
+    )(left, right, value)
 
 
 def middle_kernel(branch, wo, x, small, middle, normed_all, own, send1, recv1, sem1, *scratch):
@@ -736,69 +853,31 @@
     )(low, weight, middle, back_out, small, after, more)
 
 
-def phase_one(me, values, by_x, by_y, by_sib, send, recv):
-    copies = []
-    for k, value in enumerate(values):
-        for i, (goal, mask) in enumerate(((by_x, 2), (by_y, 4), (by_sib, 1))):
-            n = 3 * k + i
-            copies.append(push(value, goal[k], send.at[n], recv.at[n], flip(me, mask)))
-    for c in copies:
-        c.start()
-    return copies
-
-
-def phase_two(me, by_x, by_y, low, high, sib_x, sib_y, send, recv):
-    copies = []
-    for k in range(len(by_x)):
-        half = by_x[k].shape[0] // 2
-        for i, (source, goal, mask) in enumerate(
-            (
-                (by_x[k].at[pl.ds(0, half)], low[k], 4),
-                (by_y[k].at[pl.ds(half, half)], high[k], 2),
-                (by_x[k], sib_x[k], 1),
-                (by_y[k], sib_y[k], 1),
-            )
-        ):
-            n = 4 * k + i
-            copies.append(push(source, goal, send.at[n], recv.at[n], flip(me, mask)))
-    for c in copies:
-        c.start()
-    return copies
-
-
-def phase_three(me, low, high, sib_low, sib_high, send, recv):
-    copies = []
-    for k in range(len(low)):
-        for i, (source, goal) in enumerate(((low[k], sib_low[k]), (high[k], sib_high[k]))):
-            n = 2 * k + i
-            copies.append(push(source, goal, send.at[n], recv.at[n], flip(me, 1)))
-    for c in copies:
-        c.start()
-    return copies
-
-
-def pair(count):
-    return [pltpu.SemaphoreType.DMA((count,)), pltpu.SemaphoreType.DMA((count,))]
-
-
-def same(values, halves=False):
-    return [
-        jax.ShapeDtypeStruct((v.shape[0] // 2 if halves else v.shape[0], v.shape[1]), v.dtype)
-        for v in values
-    ]
-
-
 def back_input_kernel(count, low, weight, x, back_middle, small, *refs):
-    values = refs[:count]
-    out, parts = refs[count : count + 2]
-    by = refs[count + 2 : 4 * count + 2]
-    send, recv = refs[4 * count + 2 : 4 * count + 4]
-    scratch = refs[4 * count + 4 :]
+    refs = list(refs)
+
+    def take(n):
+        got = refs[:n]
+        del refs[:n]
+        return got
+
+    by_x, by_y = take(count), take(count)
+    out, parts = take(2)
+    half_low, half_high, sib_x, sib_y, sib_low, sib_high = (take(count) for _ in range(6))
+    two, three = take(2), take(2)
+    scratch = refs
     me = greet()
-    copies = phase_one(
-        me, values, by[:count], by[count : 2 * count], by[2 * count :], send, recv
-    )
-    reduce_steps(me, [(low, weight)], True, *scratch)
+    started, last = [], []
+
+    def early():
+        started.extend(phase_two(me, by_x, by_y, half_low, half_high, sib_x, sib_y, *two))
+
+    def late():
+        for c in started:
+            c.wait()
+        last.extend(phase_three(me, half_low, half_high, sib_low, sib_high, *three))
+
+    reduce_steps(me, [(low, weight)], True, *scratch, hooks=(early, lambda: None, late))
     final, total = scratch[4], scratch[5]
     parts[...] = jnp.zeros_like(parts)
 
@@ -811,68 +890,75 @@
         value = back_middle[at, :] + through_norm(back * small[0:1, :], unit, root)
         out[at, :] = value.astype(bf16)
 
-    for c in copies:
+    for c in last:
         c.wait()
 
 
-def make_back_input(low, weight, x, back_middle, small, values, cid):
+def make_back_input(low, weight, x, back_middle, small, by_x, by_y, cid):
     rows, width = x.shape
-    count = len(values)
-    out = pl.pallas_call(
-        functools.partial(back_input_kernel, count),
-        out_shape=[
+    count = len(by_x)
+    shapes = (
+        [
             jax.ShapeDtypeStruct((rows, width), bf16),
             jax.ShapeDtypeStruct((8, width), f32),
         ]
-        + same(values) * 3,
-        in_specs=[WHOLE] * 5 + [ANY] * count,
-        out_specs=[WHOLE] * 2 + [ANY] * (3 * count),
-        scratch_shapes=pair(3 * count) + reduce_scratch(rows, width),
+        + same(by_x, True) * 2
+        + same(by_x) * 2
+        + same(by_x, True) * 2
+    )
+    out = pl.pallas_call(
+        functools.partial(back_input_kernel, count),
+        out_shape=shapes,
+        in_specs=[WHOLE] * 5 + [ANY] * (2 * count),
+        out_specs=[WHOLE] * 2 + [ANY] * (len(shapes) - 2),
+        scratch_shapes=pair(4 * count) + pair(2 * count) + reduce_scratch(rows, width),
         compiler_params=params(cid),
-        cost_estimate=cost(80),
+        cost_estimate=cost(70),
         name="make_back_input",
-    )(low, weight, x, back_middle, small, *values)
-    by = out[2:]
-    return out[0], out[1], by[:count], by[count : 2 * count], by[2 * count :]
+    )(low, weight, x, back_middle, small, *by_x, *by_y)
+    rest = out[2:]
+    return out[0], out[1], [rest[i * count : (i + 1) * count] for i in range(6)]
 
 
 def ending_kernel(count, hidden, weight, middle, usable, parts_one, parts_two, *refs):
-    refs = list(refs)
-
-    def take(n):
-        got = refs[:n]
-        del refs[:n]
-        return got
-
-    by_x, by_y, fresh = take(count), take(count), take(1)
-    out, sums = take(2)
-    low, high, sib_x, sib_y, sib_low, sib_high = (take(count) for _ in range(6))
-    f_x, f_y, f_sib, f_low, f_high, f_sib_x, f_sib_y, f_sib_low, f_sib_high = (
-        take(1) for _ in range(9)
-    )
-    parts, turned, far = take(3)
-    send_s, recv_s, send_f, recv_f = take(4)
-    two, three, one_f, two_f, three_f = (take(2) for _ in range(5))
-    scratch = refs
+    fresh, refs = refs[:count], refs[count:]
+    out, sums = refs[:2]
+    fresh_all, refs = refs[2 : 2 + count], refs[2 + count :]
+    parts, turned, far, send_s, recv_s, send_f, recv_f = refs[:7]
+    sems, scratch = [refs[7 + 3 * k : 10 + 3 * k] for k in range(count)], refs[7 + 3 * count :]
     me = greet(True)
     z = lax.axis_index("shard")
     shards = lax.axis_size("shard")
-    started = phase_one(me, fresh, f_x, f_y, f_sib, *one_f)
     parts[...] = jnp.zeros_like(parts)
     parts[0:2, :] = parts_one[0:2, :]
     parts[2:4, :] = parts_two[0:2, :]
-    steps = [
+    part = parts.shape[1] // shards
+    turns = [
         push(parts, turned.at[i], send_s.at[i], recv_s.at[i], flip(me, mask))
         for i, mask in enumerate((1, 2, 4))
     ]
-    waiting = []
+    mine = [pltpu.make_async_copy(a, b.at[me], s[2]) for a, b, s in zip(fresh, fresh_all, sems)]
+    for c in mine:
+        c.start()
+    turns[0].start()
+    started, waiting = [], []
+
+    def add(i):
+        turns[i].wait()
+        parts[...] += turned[i]
+
+    def early():
+        add(0)
+        turns[1].start()
+        for a, b, s in zip(fresh, fresh_all, sems):
+            started.append(gather_begin(me, a, b, s[0], s[1]))
 
     def between():
-        for i, c in enumerate(steps):
-            c.start()
-            c.wait()
-            parts[...] += turned[i]
-        part = parts.shape[1] // shards
+        add(1)
+        turns[2].start()
+
+    def late():
+        add(2)
         for k, other in enumerate(others()):
             c = pltpu.make_async_remote_copy(
                 src_ref=parts.at[:, pl.ds(pl.multiple_of(other * part, part), part)],
@@ -884,13 +970,10 @@
             )
             c.start()
             waiting.append(c)
-        for c in started:
-            c.wait()
-        started.clear()
-        started.extend(phase_two(me, f_x, f_y, f_low, f_high, f_sib_x, f_sib_y, *two_f))
-        started.extend(phase_two(me, by_x, by_y, low, high, sib_x, sib_y, *two))
-
-    reduce_steps(me, [(hidden, weight)], False, *scratch, between=between)
+        for a, b, s, first in zip(fresh, fresh_all, sems, started):
+            gather_end(me, a, b, s[0], s[1], first)
+
+    reduce_steps(me, [(hidden, weight)], False, *scratch, hooks=(early, between, late))
     final, total = scratch[4], scratch[5]
 
     @by_rows(middle.shape[0])
@@ -898,42 +981,28 @@
         value = middle[at, :] + summed(total, final, at)
         out[at, :] = jnp.where(usable[at, :] > 0.5, value, 0.0).astype(bf16)
 
-    for c in started:
-        c.wait()
-    last = phase_three(me, f_low, f_high, f_sib_low, f_sib_high, *three_f)
-    last += phase_three(me, low, high, sib_low, sib_high, *three)
-    part = parts.shape[1] // shards
     value = parts[:, pl.ds(pl.multiple_of(z * part, part), part)]
     for k, c in enumerate(waiting):
         c.wait()
         value = value + far[k]
     sums[...] = value
-    for c in last:
+    for c in mine:
         c.wait()
 
 
-def make_ending(hidden, weight, middle, usable, parts_one, parts_two, by_x, by_y, fresh, cid):
+def make_ending(hidden, weight, middle, usable, parts_one, parts_two, fresh, cid):
     rows, width = middle.shape
     shards = lax.axis_size("shard")
-    count = len(by_x)
-    shapes = (
-        [
+    count = len(fresh)
+    out = pl.pallas_call(
+        functools.partial(ending_kernel, count),
+        out_shape=[
             jax.ShapeDtypeStruct((rows, width), bf16),
             jax.ShapeDtypeStruct((8, width // shards), f32),
         ]
-        + same(by_x, True) * 2
-        + same(by_x) * 2
-        + same(by_x, True) * 2
-        + same([fresh]) * 3
-        + same([fresh], True) * 2
-        + same([fresh]) * 2
-        + same([fresh], True) * 2
-    )
-    out = pl.pallas_call(
-        functools.partial(ending_kernel, count),
-        out_shape=shapes,
-        in_specs=[WHOLE] * 6 + [ANY] * (2 * count + 1),
-        out_specs=[WHOLE] * 2 + [ANY] * (len(shapes) - 2),
+        + [jax.ShapeDtypeStruct((8,) + a.shape, bf16) for a in fresh],
+        in_specs=[WHOLE] * 6 + [ANY] * count,
+        out_specs=[WHOLE, WHOLE] + [ANY] * count,
         scratch_shapes=[
             pltpu.VMEM((8, width), f32),
             pltpu.VMEM((3, 8, width), f32),
@@ -941,21 +1010,13 @@
         ]
         + pair(3)
         + pair(shards - 1)
-        + pair(4 * count)
-        + pair(2 * count)
-        + pair(3)
-        + pair(4)
-        + pair(2)
+        + gather_scratch(rows, width)[1:] * count
         + reduce_scratch(rows, width),
         compiler_params=params(cid),
-        cost_estimate=cost(75),
+        cost_estimate=cost(78),
         name="make_ending",
-    )(hidden, weight, middle, usable, parts_one, parts_two, *by_x, *by_y, fresh)
-    rest = out[2:]
-    groups = [rest[i * count : (i + 1) * count] for i in range(6)]
-    f_x, f_y, f_sib, f_low, f_high, f_sib_x, f_sib_y, f_sib_low, f_sib_high = rest[6 * count :]
-    whole = [fresh, f_x, f_y, f_low, f_high, f_sib, f_sib_x, f_sib_y, f_sib_low, f_sib_high]
-    return out[0], out[1], groups, whole
+    )(hidden, weight, middle, usable, parts_one, parts_two, *fresh)
+    return out[0], out[1], out[2:]
 
 
 MASKS = (0, 2, 4, 6, 6, 1, 3, 5, 7, 7)
@@ -972,14 +1033,14 @@
 def widen_two_kernel(steps, shards, *refs):
     t = lax.axis_index("tp")
     late = (pl.program_id(0) >= steps // 2).astype(jnp.int32)
-    seconds, downs, outs = refs[:10], refs[10:20], refs[20:30]
-    gelu, up, down, out = refs[30:]
+    seconds, downs, outs = refs[:10], refs[10:20], refs[20]
+    gelu, up, down, out = refs[21:]
+    out[...] = outs[...].astype(f32)
     unit = gelu.shape[1] // (8 * shards)
 
     def store(i):
         place = flip(t, MASKS[i])
         down[place] = downs[i][...].astype(f32)
-        out[place] = outs[i][...].astype(f32)
         for z in range(shards):
             at = pl.ds(pl.multiple_of((8 * z + place) * unit, unit), unit)
             gelu[:, at] = seconds[i][:, z * unit : (z + 1) * unit].astype(f32)
@@ -1018,14 +1079,16 @@
     gelu, up, down, out = pl.pallas_call(
         functools.partial(widen_two_kernel, steps, shards),
         grid=(steps,),
-        in_specs=specs(seconds) + specs(downs) + specs(outs),
+        in_specs=specs(seconds)
+        + specs(downs)
+        + [pl.BlockSpec((8, count // steps, width), lambda i: (0, i, 0))],
         out_specs=[pl.BlockSpec((rows // steps, 4 * columns), lambda i: (i, 0))] * 2
         + [pl.BlockSpec((8, count // steps, width), lambda i: (0, i, 0))] * 2,
         out_shape=[units, units, stack, stack],
         compiler_params=params(),
         cost_estimate=cost(25),
         name="widen_two",
-    )(*seconds, *downs, *outs)
+    )(*seconds, *downs, outs)
     return gelu, up, down.reshape(8 * count, width), out.reshape(8 * count, width)
 
 
@@ -1036,7 +1099,7 @@
             goal[:, i * size : (i + 1) * size] = parts[i, :, begin:end].astype(f32)
 
 
-def widen_one(parts, edges, after):
+def widen_one(parts, edges, after, name):
     _, rows, columns = parts.shape
     sizes = [b - a for a, b in zip(edges, edges[1:])]
     block = 64
@@ -1048,7 +1111,7 @@
         out_shape=[jax.ShapeDtypeStruct((rows, 8 * size), f32) for size in sizes],
         compiler_params=params(),
         cost_estimate=cost(14),
-        name="widen_one",
+        name=name,
     )(parts, after)
 
 
@@ -1099,19 +1162,38 @@
 
     def exchange(value):
         return lax.all_to_all(
-            value.reshape(device_count, rows // device_count, width),
+            value.reshape(device_count, rows // device_count, value.shape[1]),
             every,
             split_axis=0,
             concat_axis=0,
             tiled=True,
-        ).reshape(rows, width)
+        ).reshape(rows, value.shape[1])
+
+    piece = rows // device_count
+    part = gain_one.shape[0]
+    extra = jnp.concatenate(
+        [gain_one, shift_one, gain_two, shift_two, lengths.reshape(-1).astype(bf16)]
+    )
+    extra_columns = -(-extra.shape[0] // (piece * 128)) * 128
+    extra = jnp.pad(extra, (0, piece * extra_columns - extra.shape[0]))
+    extra = jnp.tile(extra.reshape(piece, extra_columns), (device_count, 1))
+    came = exchange(
+        jnp.concatenate([forward_dot(send_mix, tokens).astype(bf16), extra], axis=1)
+    )
+    t_early = t + (came[0, 0].astype(f32) > 100.0).astype(jnp.int32)
+    arrived = came[:, width:].reshape(outer, tp, shards, -1)
+    small = jnp.transpose(arrived[0, 0, :, : 4 * part].reshape(shards, 4, part), (1, 0, 2))
+    small = small.reshape(4, width).astype(f32)
+    small = jnp.concatenate([small, jnp.zeros((4, width), f32)], axis=0)
+    all_lengths = arrived[lax.axis_index("outer"), :, z, 4 * part : 4 * part + lengths.size]
+    all_lengths = all_lengths.reshape(group_packs, -1).astype(f32).astype(jnp.int32)
 
     def along_z(piece):
         return lax.all_gather(piece, "shard", axis=0, tiled=True)
 
     def cut(weight):
         part = weight.shape[1] // tp
-        return lax.dynamic_slice_in_dim(weight, t * part, part, axis=1)
+        return lax.dynamic_slice_in_dim(weight, t_early * part, part, axis=1)
 
     out_unit = out_weight.shape[0] // tp
     unit = down_weight.shape[0] // tp
@@ -1131,7 +1213,7 @@
         value = value.reshape(shards, cuts, count, width // cuts)
         return jnp.transpose(value, (0, 2, 1, 3)).reshape(shards, count, width)
 
-    out_piece = lax.dynamic_slice_in_dim(out_weight, t * out_unit, out_unit, axis=0)
+    out_piece = lax.dynamic_slice_in_dim(out_weight, t_early * out_unit, out_unit, axis=0)
     w_one = along_z(
         jnp.concatenate(
             [cut(w) for w in (query_weight, key_weight, value_weight, gate_weight)]
@@ -1142,28 +1224,24 @@
     ends = jnp.cumsum(lengths, axis=1, dtype=jnp.int32)[:, -2]
     usable = (jnp.arange(pack_rows, dtype=jnp.int32)[None, :] < ends[:, None]).astype(f32)
     usable = usable.reshape(rows, 1)
-    lens = jnp.pad(lengths, ((0, 8 - packs), (0, 128 - lengths.shape[1])))
-    came = exchange(forward_dot(send_mix, tokens).astype(bf16))
     came_back = exchange(forward_dot(send_mix, cotangent).astype(bf16))
-    gains = jnp.stack([gain_one, shift_one, gain_two, shift_two]).astype(f32)
-    gains = jnp.concatenate([gains, jnp.zeros_like(gains)], axis=0)
-    x, normed, all_lengths, small = entry(came, work_mix, gains, lens, 0)
-    t_late = t + jnp.minimum(all_lengths[0, 0, 0], 0)
+    x, normed = entry(came, work_mix, small, 0)
+    t_late = t + (x[0, 0].astype(f32) > 100.0).astype(jnp.int32)
 
     def unit_columns(weight):
-        split = weight.reshape(weight.shape[0], shards, tp, unit)
-        split = lax.dynamic_slice_in_dim(split, t_late, 1, axis=2)
-        return split.reshape(weight.shape[0], hidden_part)
+        return [
+            lax.dynamic_slice_in_dim(weight, (k * tp + t_late) * unit, unit, axis=1)
+            for k in range(shards)
+        ]
 
     down_piece = lax.dynamic_slice_in_dim(down_weight, t_late * unit, unit, axis=0)
     w_two = along_z(
         jnp.concatenate(
-            [unit_columns(gelu_weight), unit_columns(up_weight), fold(down_piece)], axis=1
+            unit_columns(gelu_weight) + unit_columns(up_weight) + [fold(down_piece)], axis=1
         )
     )
     back_out, back_low = entry_back(came_back, work_mix, usable, x, 7)
     normed, back_low = normed.reshape(group_rows, width), back_low.reshape(group_rows, width)
-    all_lengths = all_lengths[:, :packs, : lengths.shape[1]].reshape(group_packs, -1)
     cosine, sine, decays, _ = pack_tables(all_lengths, pack_rows, t + jnp.arange(1))
     cosine, sine = cosine.reshape(group_rows, -1), sine.reshape(group_rows, -1)
     decays = decays[0]
@@ -1175,7 +1253,9 @@
     middle, normed_two = make_middle(branch, wo, x, small, 2)
     normed_two = normed_two.reshape(group_rows, width)
 
-    hidden, second_low, w_down = feed(normed_two, back_low, w_two, hidden_part, shards, rows)
+    hidden, second_low, w_down, branch_rows = feed(
+        normed_two, back_low, w_two, branch, hidden_part, shards, rows, 6
+    )
     down_gram = gram_rows(hidden, back_low).astype(bf16)
     second_gram = gram_rows(normed_two, second_low).astype(bf16)
 
@@ -1188,29 +1268,29 @@
         second_low, w_two, middle, back_out, small, down_gram, second_gram, 3
     )
     middle_low = middle_low.reshape(group_rows, width)
-    out_gram = gram_rows(branch, middle_low).astype(bf16).reshape(shards, out_unit, width)
-    first_low, dealt = retain_back(
+    out_sum = to_owner(gram_rows(branch_rows, middle_low).astype(bf16))
+    first_low, *down_by = retain_back(
         middle_low, wo, q_rot, k_rot, v_low, weights_low, gating, retained, cosine, sine, decays,
-        out_gram, rows, 8,
-    )
-    out_sum = to_owner(dealt.reshape(shards * out_unit, width))
-    first_gram = gram_rows(normed, first_low).astype(bf16)
-    first_gram, second_sum, down_sum = lax.optimization_barrier((first_gram, second_sum, down_sum))
-    first_sum = to_owner(first_gram)
-    values = [second_sum, down_sum]
-    back_inputs, parts_one, by_x, by_y, by_sib = make_back_input(
-        first_low, w_one, x, back_middle, small, values, 4
-    )
-    ending, sums, groups, outs = make_ending(
-        hidden, w_down, middle, usable, parts_one, parts_two, by_x, by_y, out_sum, 5
+        down_sum, rows, 8,
+    )
+    first_gram, third_gram, *second_by = gram_beside(
+        normed, first_low, second_sum, edges[2], 256, 9
+    )
+    first_sum, third_sum = to_owner(first_gram), to_owner(third_gram)
+    by_x, by_y, by_sib = ([a, b] for a, b in zip(second_by, down_by))
+    back_inputs, parts_one, groups = make_back_input(
+        first_low, w_one, x, back_middle, small, by_x, by_y, 4
+    )
+    ending, sums, (outs, firsts) = make_ending(
+        hidden, w_down, middle, usable, parts_one, parts_two, [out_sum, first_sum], 5
     )
     low, high, sib_x, sib_y, sib_low, sib_high = groups
     seconds, downs = (
         [
-            values[k], by_x[k], by_y[k], low[k], high[k],
+            value, by_x[k], by_y[k], low[k], high[k],
             by_sib[k], sib_x[k], sib_y[k], sib_low[k], sib_high[k],
         ]
-        for k in range(2)
+        for k, value in enumerate((second_sum, down_sum))
     )
 
     if unit % 128 == 0:
@@ -1219,22 +1299,21 @@
         )
     else:
         down_gradient = in_order(downs).reshape(-1, width).astype(f32)
-        out_gradient = in_order(outs).reshape(-1, width).astype(f32)
+        out_gradient = outs.reshape(-1, width).astype(f32)
         both = in_order(seconds).reshape(tp, piece_rows, 2, shards, unit)
         both = jnp.transpose(both, (2, 1, 3, 0, 4)).reshape(2, piece_rows, -1).astype(f32)
         gelu_gradient, up_gradient = both[0], both[1]
-    firsts = lax.all_gather(first_sum + sums[5, 0].astype(bf16), "tp", axis=0)
-    query_gradient, key_gradient, value_gradient, gate_gradient = widen_one(
-        firsts, edges + (first_size,), down_gradient
+    thirds = lax.all_gather(third_sum + sums[5, 0].astype(bf16), "tp", axis=0)
+    query_gradient, key_gradient = widen_one(firsts, edges[:3], down_gradient, "widen_one")
+    value_gradient, gate_gradient = widen_one(
+        thirds, (0, value_part, 2 * value_part), query_gradient, "widen_three"
     )
     smalls = lax.psum(sums, "outer") if outer > 1 else sums
 
-    def give_back(value):
-        home = exchange(gram_rows(work_mix, value).astype(bf16))
-        return gram_rows(send_mix, home).astype(bf16)
-
-    result = give_back(ending)
-    token_gradient = give_back(back_inputs)
+    home = jnp.concatenate([ending, back_inputs], axis=1)
+    home = exchange(gram_rows(work_mix, home).astype(bf16))
+    home = gram_rows(send_mix, home).astype(bf16)
+    result, token_gradient = home[:, :width], home[:, width:]
     return (
         result,
         token_gradient,

time: 857 us -> 807 us (0.942)
  Pallas kernels: 609 us -> 576 us
  waiting for transfers between devices: 81.7 us -> 105 us
  matrix products: 60.9 us -> 37.8 us
  starting transfers between devices: 29 us -> 16.9 us
  local copies, waits for them, and re-layouts: 40.4 us -> 31.1 us
    pallas_call x1, Pallas kernels: 103 us -> 47.9 us  [entry(): pl.pallas_call(entry_kernel, out_shape=(jax.ShapeDtypeStruct((rows, width...]
    all_gather x2, waiting for transfers between devices: 0.04 us -> 37.4 us  [along_z(): return lax.all_gather(piece, 'shard', axis=0, tiled=True)]
    pallas_call x3 -> x4, Pallas kernels: 188 us -> 219 us  [the longest x1 88.4 us: make_ending(): pl.pallas_call(functools.partial(ending_kernel, count), out_shape=[jax.Sh...]
    dot_general x8 -> x5, matrix products: 58.1 us -> 35.9 us  [gram_rows(): lax.dot_general(leading, trailing, (((0,), (0,)), ((), ())), preferred_el...]
    all_to_all x4 -> x3, starting transfers between devices: 27.4 us -> 15.9 us  [exchange(): lax.all_to_all(value.reshape(device_count, rows // device_count, value.sh...]
    dynamic_slice x2, local copies, waits for them, and re-layouts: 11.5 us -> 1.1 us  [the longest x1 1.09 us: local(): lax.dynamic_slice_in_dim(out_weight, t_early * out_unit, out_unit, axis=0)]
    all_to_all x4 -> x3, waiting for transfers between devices: 57.5 us -> 48.6 us  [exchange(): lax.all_to_all(value.reshape(device_count, rows // device_count, value.sh...]
    pallas_call x1, Pallas kernels: 28.7 us -> 19.8 us  [retain_back(): pl.pallas_call(retain_back_kernel, grid=(total // block,), in_specs=[row(...]
  transfers between devices with their start and end apart: 11 -> 11, of which waited for: 4 -> 4; matrix products, arithmetic and copies ran while one was open for 11% -> 8% of each run, Pallas kernels for 68% -> 67%
where the time goes in v3:
time: 807 us; the launch traced here: 799 us
  Pallas kernels  576 us (71%)
  waiting for transfers between devices  105 us (13%)
  matrix products  37.8 us (5%)
  local copies, waits for them, and re-layouts  31.1 us (4%)
  starting transfers between devices  16.9 us (2%)
  between operations  16.6 us (2%)
  other arithmetic  16.1 us (2%)
    pallas_call x1, Pallas kernels, make_back_middle(): pl.pallas_call(back_middle_kernel, out_shape=(jax.ShapeDtypeStruct((rows,...  92 us
    pallas_call x1, Pallas kernels, make_ending(): pl.pallas_call(functools.partial(ending_kernel, count), out_shape=[jax.Sh...  88.4 us
    pallas_call x1, Pallas kernels, make_middle(): pl.pallas_call(middle_kernel, out_shape=(jax.ShapeDtypeStruct((rows, widt...  88.1 us
    pallas_call x1, Pallas kernels, make_back_input(): pl.pallas_call(functools.partial(back_input_kernel, count), out_shape=sha...  71.4 us
    all_to_all x3, waiting for transfers between devices, exchange(): lax.all_to_all(value.reshape(device_count, rows // device_count, value.sh...  48.6 us
    pallas_call x1, Pallas kernels, entry(): pl.pallas_call(entry_kernel, out_shape=(jax.ShapeDtypeStruct((rows, width...  47.9 us
    pallas_call x1, Pallas kernels, entry_back(): pl.pallas_call(entry_back_kernel, out_shape=(jax.ShapeDtypeStruct((rows,...  44.7 us
    all_gather x2, waiting for transfers between devices, along_z(): return lax.all_gather(piece, 'shard', axis=0, tiled=True)  37.4 us
  transfers between devices with their start and end apart: 11, of which 4 were waited for; matrix products, arithmetic and copies ran while one was open for 8% of the time, Pallas kernels for 67%

profile of v3, /device:TPU:0, one launch (start us, length us, event | category | flops | bytes accessed | tf_op | source)
XLA Modules:
  0.0 799.3 jit_solution(16003705233300495731)
XLA Ops:
  13.0 1.1 pad_maximum_fusion
  14.1 7.3 all-to-all-start
  22.9 1.4 fusion.2
  24.3 26.3 %all-to-all-done = bf16[32,8,2432]{2,1,0:T(8,128)(2,1)S(1)} async-done(((bf16[32,8,2432]{2,1,0:T(8,128)(2,1)}), bf16[32,8,2432]{2,1,0:T(8,128)(2,1)S(1)}, u32[]{:S(2)}, u32[]{:S(2)}) %all-to-all-start) | async-done | bytes 1245216 | tf_op jit(solution)/shard_map/all_to_all | solution.py:1164
  50.6 4.6 all-to-all-start.1
  56.5 1.1 constant_dynamic-slice_fusion.2
  58.1 1.0 dynamic-slice_dynamic-update-slice_fusion.3
  59.1 1.0 dynamic-slice_dynamic-update-slice_fusion.2
  60.0 1.1 dynamic-slice_dynamic-update-slice_fusion.1
  61.2 1.1 dynamic-slice_dynamic-update-slice_fusion
  62.4 1.3 copy-done.2
  63.8 1.2 select_reduce_fusion
  66.5 0.9 slice.53
  68.6 47.9 %entry.1 = (bf16[256,2048]{1,0:T(8,128)(2,1)}, bf16[8,256,2048]{2,1,0:T(8,128)(2,1)}) custom-call(bf16[256,2432]{1,0:T(8,128)(2,1)} %bitcast.67, bf16[256,256]{1,0:T(8,128)(2,1)} %fusion.7.mix, f32[8,2048]{1,0:T(8,128)} %pad_convert_fusion.small), custom_call_target="tpu_custom_call" | custom-call | flops 49999998976 | bytes 150000000 | tf_op jit(solution)/shard_map/entry/pallas_call | solution.py:353
  116.5 1.2 slice.45
  118.5 1.1 constant_dynamic-slice_fusion
  121.1 0.9 dynamic-slice_dynamic-update-slice_fusion.10
  122.0 0.9 dynamic-slice_dynamic-update-slice_fusion.9
  123.0 0.9 dynamic-slice_dynamic-update-slice_fusion.8
  123.9 0.9 dynamic-slice_dynamic-update-slice_fusion.7
  124.9 0.9 dynamic-slice_dynamic-update-slice_fusion.6
  127.8 5.5 multiply_sine_fusion
  133.3 44.7 %entry_back.1 = (bf16[256,2048]{1,0:T(8,128)(2,1)}, bf16[8,256,2048]{2,1,0:T(8,128)(2,1)}) custom-call(bf16[256,2048]{1,0:T(8,128)(2,1)} %bitcast.15.came, bf16[256,256]{1,0:T(8,128)(2,1)} %fusion.7.mix, f32[256,1]{1,0:T(8,128)} %copy.46.usable, bf16[256,2048]{1,0:T(8,128)(2,1)} %get-tuple-element.73.x._after), custom_call_target="tpu_custom_call" | custom-call | flops 44999999488 | bytes 135000000 | tf_op jit(solution)/shard_map/entry_back/pallas_call | solution.py:383
  178.3 1.3 and_select_fusion.decays
  179.6 37.4 %all-gather.5.cloned.1.call-done.weight = bf16[2048,2048]{1,0:T(8,128)(2,1)} async-done(((bf16[512,2048]{1,0:T(8,128)(2,1)}), bf16[2048,2048]{1,0:T(8,128)(2,1)}) %all-gather.5.cloned.1.call-update) | async-done | bytes 8388624 | tf_op jit(solution)/shard_map/all_gather | solution.py:1192
  217.0 1.6 slice-done
  218.6 1.6 copy.53
  220.2 30.4 %retain.1 = (bf16[2048,256]{1,0:T(8,128)(2,1)}, bf16[2048,256]{1,0:T(8,128)(2,1)}, bf16[2048,512]{1,0:T(8,128)(2,1)}, bf16[16,128,128]{2,1,0:T(8,128)(2,1)}, f32...) custom-call(bf16[2048,2048]{1,0:T(8,128)(2,1)} %bitcast.76, ...), custom_call_target="tpu_custom_call" | custom-call | flops 24000000000 | bytes 72000000 | tf_op jit(solution)/shard_map/retain/pallas_call | solution.py:571
  250.6 88.1 %make_middle.1 = (f32[256,2048]{1,0:T(8,128)}, bf16[8,256,2048]{2,1,0:T(8,128)(2,1)}) custom-call(bf16[2048,512]{1,0:T(8,128)(2,1)} %get-tuple-element.71.branch, bf16[512,2048]{1,0:T(8,128)(2,1)} %bitcast.87, bf16[256,2048]{1,0:T(8,128)(2,1)} %get-tuple-element.73.x._after, f32[8,2048]{1,0:T(8,128)} %pad_convert_fusion.small), custom_call_target="tpu_custom_call" | custom-call | flops 85000003584 | bytes 255000000 | tf_op jit(solution)/shard_map/make_middle/pallas_call | solution.py:789
  338.7 29.3 %feed.1 = (bf16[2048,512]{1,0:T(8,128)(2,1)}, bf16[2048,1024]{1,0:T(8,128)(2,1)}, bf16[512,2048]{1,0:T(8,128)(2,1)}, bf16[2048,512]{1,0:T(8,128)(2,1)}) custom-call(bf16[2048,2048]{1,0:T(8,128)(2,1)} %bitcast.85, bf16[2048,2048]{1,0:T(8,128)(2,1)} %bitcast.81, bf16[2048,1536]{1,0:T(8,128)(2,1)} %all-gather.7.cloned.1.call-done.w_two.weight, ...), custom_call_target="tpu_custom_call" | custom-call | flops 25999998976 | bytes 78000000 | tf_op jit(solution)/shard_map/feed/pallas_call | solution.py:711
  368.0 9.9 %convolution_convert_fusion.4._after = bf16[512,2048]{1,0:T(8,128)(2,1)} fusion(bf16[2048,512]{1,0:T(8,128)(2,1)} %get-tuple-element.76.hidden, bf16[2048,2048]{1,0:T(8,128)(2,1)} %bitcast.82), kind=kOutput, calls=%fused_computation.6 | convolution fusion | flops 4296015872 | bytes 12582912 | tf_op jit(solution)/shard_map/dot_general | solution.py:54
  378.2 14.0 %convolution_convert_fusion.2._more = bf16[2048,1024]{1,0:T(8,128)(2,1)} fusion(bf16[2048,2048]{1,0:T(8,128)(2,1)} %bitcast.86, bf16[2048,1024]{1,0:T(8,128)(2,1)} %get-tuple-element.79.low), kind=kOutput, calls=%fused_computation.4 | convolution fusion | flops 8592031744 | bytes 16777216 | tf_op jit(solution)/shard_map/dot_general | solution.py:54
  392.2 92.0 %make_back_middle.1 = (f32[256,2048]{1,0:T(8,128)}, f32[8,2048]{1,0:T(8,128)}, bf16[8,256,2048]{2,1,0:T(8,128)(2,1)}) custom-call(bf16[2048,1024]{1,0:T(8,128)(2,1)} %get-tuple-element.79.low, bf16[2048,1536]{1,0:T(8,128)(2,1)} %all-gather.7.cloned.1.call-done.w_two.weight, f32[256,2048]{1,0:T(8,128)} %get-tuple-element.78.middle, ...), custom_call_target="tpu_custom_call" | custom-call | flops 89999998976 | bytes 270000000 | tf_op jit(solution)/shard_map/make_back_middle/pallas_call | solution.py:840
  484.2 9.1 %convolution_convert_fusion.3 = bf16[512,2048]{1,0:T(8,128)(2,1)} fusion(bf16[2048,512]{1,0:T(8,128)(2,1)S(1)} %copy-done.15, bf16[2048,2048]{1,0:T(8,128)(2,1)} %bitcast.83), kind=kOutput, calls=%fused_computation.5 | convolution fusion | flops 4296015872 | bytes 12582912 | tf_op jit(solution)/shard_map/dot_general | solution.py:54
  493.7 19.8 %retain_back.1 = (bf16[2048,1536]{1,0:T(8,128)(2,1)}, bf16[128,2048]{1,0:T(8,128)(2,1)}, bf16[128,2048]{1,0:T(8,128)(2,1)}, bf16[128,2048]{1,0:T(8,128)(2,1)}) custom-call(bf16[2048,2048]{1,0:T(8,128)(2,1)} %bitcast.84, bf16[512,2048]{1,0:T(8,128)(2,1)} %bitcast.88, bf16[2048,256]{1,0:T(8,128)(2,1)} %get-tuple-element.82.q_in, ...), custom_call_target="tpu_custom_call" | custom-call | flops 20000000000 | bytes 60000000 | tf_op jit(solution)/shard_map/retain_back/pallas_call | solution.py:650
  513.5 29.6 %gram_beside.1 = (bf16[2048,512]{1,0:T(8,128)(2,1)}, bf16[2048,1024]{1,0:T(8,128)(2,1)}, bf16[512,1024]{1,0:T(8,128)(2,1)}, bf16[512,1024]{1,0:T(8,128)(2,1)}, bf16[512,1024]{1,0:T(8,128)(2,1)}) custom-call(bf16[2048,2048]{1,0:T(8,128)(2,1)} %bitcast.77, bf16[2048,1536]{1,0:T(8,128)(2,1)} %get-tuple-element.88.right.low, ...), custom_call_target="tpu_custom_call" | custom-call | flops 28000000000 | bytes 84000000 | tf_op jit(solution)/shard_map/gram_beside/pallas_call | solution.py:758
  544.0 71.4 %make_back_input.1 = (bf16[256,2048]{1,0:T(8,128)(2,1)}, f32[8,2048]{1,0:T(8,128)}, bf16[256,1024]{1,0:T(8,128)(2,1)}, bf16[64,2048]{1,0:T(8,128)(2,1)}, bf16[25...) custom-call(bf16[2048,1536]{1,0:T(8,128)(2,1)} %get-tuple-element.88, ...), custom_call_target="tpu_custom_call" | custom-call | flops 70000001024 | bytes 210000000 | tf_op jit(solution)/shard_map/make_back_input/pallas_call | solution.py:909
  615.5 88.4 %make_ending.1 = (bf16[256,2048]{1,0:T(8,128)(2,1)}, f32[8,512]{1,0:T(8,128)}, bf16[8,128,2048]{2,1,0:T(8,128)(2,1)}, bf16[8,512,512]{2,1,0:T(8,128)(2,1)}) custom-call(bf16[2048,512]{1,0:T(8,128)(2,1)} %get-tuple-element.76.hidden, bf16[512,2048]{1,0:T(8,128)(2,1)} %get-tuple-element.77.weight, f32[256,2048]{1,0:T(8,128)} %get-tuple-element.78.middle, ...), custom_call_target="tpu_custom_call" | custom-call | flops 77999996928 | bytes 234000000 | tf_op jit(solution)/shard_map/make_ending/pallas_call | solution.py:997
  703.9 1.3 slice.59
  705.3 2.9 broadcast_add_fusion
  708.2 2.1 fusion
  710.4 4.0 all-to-all-start.2
  715.0 17.0 %widen_two.1 = (f32[512,4096]{1,0:T(8,128)}, f32[512,4096]{1,0:T(8,128)}, f32[8,128,2048]{2,1,0:T(8,128)}, f32[8,128,2048]{2,1,0:T(8,128)}) custom-call(bf16[512,1024]{1,0:T(8,128)(2,1)} %reduce-scatter.8.cloned.1.call-done.value.refs_0_, bf16[512,1024]{1,0:T(8,128)(2,1)} %get-tuple-element.90.refs_0_.refs_1_, bf16[512,1024]{1,0:T(8,128)(2,1)} %get-tuple-element.92.refs_2_, ...), custom_call_target="tpu_custom_call" | custom-call | flops 24999999488 | bytes 75000000 | tf_op jit(solution)/shard_map/widen_two/pallas_call | solution.py:1079
  732.0 7.2 widen_one.1
  739.2 22.3 %all-to-all-done.2 = bf16[32,8,4096]{2,1,0:T(8,128)(2,1)S(1)} async-done(((bf16[32,8,4096]{2,1,0:T(8,128)(2,1)}), bf16[32,8,4096]{2,1,0:T(8,128)(2,1)S(1)}, u32[]{:S(2)}, u32[]{:S(2)}) %all-to-all-start.2) | async-done | bytes 2097184 | tf_op jit(solution)/shard_map/all_to_all | solution.py:1164
  762.3 1.5 fusion.16
  763.7 18.0 %all-gather.9.cloned.1.call-done = bf16[4096,1024]{1,0:T(8,128)(2,1)} async-done(((bf16[512,1024]{1,0:T(8,128)(2,1)}), bf16[4096,1024]{1,0:T(8,128)(2,1)}) %all-gather.9.cloned.1.call-update) | async-done | bytes 8388624 | tf_op jit(solution)/shard_map/all_gather | solution.py:1306
  781.7 10.2 %widen_three.1 = (f32[512,4096]{1,0:T(8,128)}, f32[512,4096]{1,0:T(8,128)}) custom-call(bf16[8,512,1024]{2,1,0:T(8,128)(2,1)} %bitcast.75, f32[512,2048]{1,0:T(8,128)} %get-tuple-element.58._after), custom_call_target="tpu_custom_call" | custom-call | flops 14000000000 | bytes 42000000 | tf_op jit(solution)/shard_map/widen_three/pallas_call | solution.py:1106
  (106 shorter events, 17.6 us)
Async XLA Ops:
  7.2 5.3 copy-start
  12.5 10.4 %copy-start.9 = (s32[256]{0:T(256)}, s32[256]{0:T(256)S(1)}, u32[]{:S(2)}) copy-start(s32[256]{0:T(256)S(1)} %convert_reduce_fusion.1) | copy-start | bytes 3076
  13.0 8.5 %copy-start.14 = (s32[2,4]{1,0:T(2,128)S(1)}, s32[2,4]{1,0:T(2,128)}, u32[]{:S(2)}) copy-start(s32[2,4]{1,0:T(2,128)} %param.19) | copy-start | bytes 100
  13.0 9.9 %copy-start.5 = (bf16[256,2048]{1,0:T(8,128)(2,1)S(1)}, bf16[256,2048]{1,0:T(8,128)(2,1)}, u32[]{:S(2)}) copy-start(bf16[256,2048]{1,0:T(8,128)(2,1)} %param.17) | copy-start | bytes 3145732
  14.1 36.4 %all-to-all-start = ((bf16[32,8,2432]{2,1,0:T(8,128)(2,1)}), bf16[32,8,2432]{2,1,0:T(8,128)(2,1)S(1)}, u32[]{:S(2)}, u32[]{:S(2)}) async-start(bf16[32,8,2432]{2,1,0:T(8,128)(2,1)} %pad_maximum_fusion), calls=%async_computation | async-start | bytes 2490368 | tf_op jit(solution)/shard_map/all_to_all | solution.py:1164
  50.6 7.3 copy-start.4
  50.6 82.7 %all-to-all-start.1 = ((bf16[32,8,2048]{2,1,0:T(8,128)(2,1)}), bf16[32,8,2048]{2,1,0:T(8,128)(2,1)}, u32[]{:S(2)}, u32[]{:S(2)}) async-start(bf16[32,8,2048]{2,1,0:T(8,128)(2,1)} %fusion.2), calls=%async_computation.1 | async-start | bytes 2097152 | tf_op jit(solution)/shard_map/all_to_all | solution.py:1164
  55.3 161.7 %all-gather.5.cloned.1.call-start = ((), (), s32[]{:S(2)}) async-start(), calls=%async_computation.8 | async-start | bytes 10485760 | tf_op jit(solution)/shard_map/all_gather | solution.py:1192
  61.2 2.6 copy-start.8
  62.4 1.3 copy-start.2
  63.7 274.9 %all-gather.7.cloned.1.call-start = ((), (), s32[]{:S(2)}) async-start(), calls=%async_computation.9 | async-start | bytes 7864320 | tf_op jit(solution)/shard_map/all_gather | solution.py:1192
  65.2 0.6 copy-start.11
  127.8 50.2 %copy-start.3 = (bf16[512,1536]{1,0:T(8,128)(2,1)}, bf16[512,1536]{1,0:T(8,128)(2,1)S(1)}, u32[]{:S(2)}) copy-start(bf16[512,1536]{1,0:T(8,128)(2,1)S(1)} %constant_dynamic-update-slice_fusion.1) | copy-start | bytes 4718596
  178.0 315.6 %reduce-scatter.6.cloned.1.call-start = ((), (), s32[]{:S(2)}) async-start(), calls=%async_computation.10 | async-start | bytes 2621440 | tf_op jit(solution)/shard_map/reduce_scatter | solution.py:1263
  217.0 1.6 slice-start
  377.9 135.6 %reduce-scatter.8.cloned.1.call-start = ((), (), s32[]{:S(2)}) async-start(), calls=%async_computation.11 | async-start | bytes 5242880 | tf_op jit(solution)/shard_map/reduce_scatter | solution.py:1263
  392.2 223.3 %reduce-scatter.10.cloned.1.call-start = ((), (), s32[]{:S(2)}) async-start(), calls=%async_computation.12 | async-start | bytes 2621440 | tf_op jit(solution)/shard_map/reduce_scatter | solution.py:1263
  392.2 92.0 %copy-start.15 = (bf16[2048,512]{1,0:T(8,128)(2,1)S(1)}, bf16[2048,512]{1,0:T(8,128)(2,1)}, u32[]{:S(2)}) copy-start(bf16[2048,512]{1,0:T(8,128)(2,1)} %get-tuple-element.96) | copy-start | bytes 6291460
  493.4 122.1 %reduce-scatter.12.cloned.1.call-start = ((), (), s32[]{:S(2)}) async-start(), calls=%async_computation.13 | async-start | bytes 2621440 | tf_op jit(solution)/shard_map/reduce_scatter | solution.py:1263
  543.2 162.0 %reduce-scatter.14.cloned.1.call-start = ((), (), s32[]{:S(2)}) async-start(), calls=%async_computation.14 | async-start | bytes 5242880 | tf_op jit(solution)/shard_map/reduce_scatter | solution.py:1263
  544.0 237.8 %all-gather.9.cloned.1.call-start = ((), (), s32[]{:S(2)}) async-start(), calls=%async_computation.15 | async-start | bytes 9437184 | tf_op jit(solution)/shard_map/all_gather | solution.py:1306
  703.9 4.3 copy-start.6
  703.9 4.3 copy-start.7
  703.9 4.3 copy-start.12
  710.4 4.0 copy-start.13
  710.4 51.1 %all-to-all-start.2 = ((bf16[32,8,4096]{2,1,0:T(8,128)(2,1)}), bf16[32,8,4096]{2,1,0:T(8,128)(2,1)S(1)}, u32[]{:S(2)}, u32[]{:S(2)}) async-start(bf16[32,8,4096]{2,1,0:T(8,128)(2,1)} %fusion), calls=%async_computation.6 | async-start | bytes 4194304 | tf_op jit(solution)/shard_map/all_to_all | solution.py:1164
  732.0 29.5 %copy-start.10 = (s32[256]{0:T(256)S(1)}, s32[256]{0:T(256)}, u32[]{:S(2)}) copy-start(s32[256]{0:T(256)} %copy-done.9) | copy-start | bytes 3076
  781.7 10.2 %copy-start.1 = (bf16[256,2048]{1,0:T(8,128)(2,1)S(1)}, bf16[256,2048]{1,0:T(8,128)(2,1)}, u32[]{:S(2)}) copy-start(bf16[256,2048]{1,0:T(8,128)(2,1)} %param.16) | copy-start | bytes 3145732
Sparse Core Ops, SparseCore 0:
  63.9 153.0 all-gather.4
  219.1 114.3 all-gather.6
  378.0 43.5 reduce-scatter.5
  424.5 76.0 reduce-scatter.7
  503.3 44.3 reduce-scatter.9
  550.0 43.1 reduce-scatter.11
  595.4 76.0 reduce-scatter.13
  708.3 73.3 all-gather.8

commit v4 on v3

--- a/solution.py
+++ b/solution.py
@@ -109,17 +109,20 @@
     )
 
 
-def gather_begin(me, own, out, send, recv):
+def gather_begin(me, own, out, send, recv, halves=(True, True), first=None):
     half = own.shape[0] // 2
     xn, yn = flip(me, 2), flip(me, 4)
     low, high = pl.ds(0, half), pl.ds(half, half)
-    first = [
-        push(own.at[part], out.at[me, part], send.at[i], recv.at[i], peer)
-        for i, (part, peer) in enumerate(((low, xn), (high, yn), (high, xn), (low, yn)))
-    ]
-    first.append(push(own, out.at[me], send.at[4], recv.at[4], flip(me, 1)))
-    for c in first:
-        c.start()
+    first = first if first is not None else [None] * 5
+    ways = ((low, xn), (high, yn), (high, xn), (low, yn))
+    for i in (0, 3, 1, 2):
+        part, peer = ways[i]
+        if halves[0 if part is low else 1]:
+            first[i] = push(own.at[part], out.at[me, part], send.at[i], recv.at[i], peer)
+            first[i].start()
+    if halves[1]:
+        first[4] = push(own, out.at[me], send.at[4], recv.at[4], flip(me, 1))
+        first[4].start()
     return first
 
 
@@ -164,7 +167,7 @@
 COLS = 512
 
 
-def reduce_steps(me, pairs, transposed, tosib, fromsib, hold, hop, final, total, send, recv, hooks=()):
+def reduce_stages(me, pairs, transposed, tosib, fromsib, hold, hop, final, total, send, recv):
     rows, width = total.shape
     half = rows // 2
     sib, xn, yn = flip(me, 1), flip(me, 2), flip(me, 4)
@@ -218,10 +221,6 @@
             else:
                 total[:, at] = value
 
-    def hook(i):
-        if hooks:
-            hooks[i]()
-
     for_sibling(0)
     for_sibling(1)
     for_own_core(0)
@@ -229,7 +228,6 @@
     dy = cp(5, hold.at[0, high], hop.at[1], yn)
     dx.start()
     dy.start()
-    hook(0)
     for_sibling(2)
     for_own_core(1)
     xa = cp(6, hold.at[1, low], final.at[0, low], xn)
@@ -239,7 +237,7 @@
     yb = cp(7, hold.at[2, high], final.at[1, high], yn)
     yb.start()
     for_own_core(3)
-    hook(1)
+    yield
     dy.wait_recv()
     hold[1, high] = (hold[1, high].astype(f32) + hop[1].astype(f32)).astype(bf16)
     xb = cp(8, hold.at[1, high], final.at[0, high], xn)
@@ -248,13 +246,18 @@
     hold[2, low] = (hold[2, low].astype(f32) + hop[0].astype(f32)).astype(bf16)
     ya = cp(9, hold.at[2, low], final.at[1, low], yn)
     ya.start()
-    hook(2)
+    yield
     xa.wait_recv()
     yb.wait_recv()
     xb.wait_recv()
     ya.wait_recv()
     for c in over + [dx, dy, xa, yb, xb, ya]:
         c.wait_send()
+
+
+def reduce_steps(*args):
+    for _ in reduce_stages(*args):
+        pass
 
 
 def summed(total, final, at):
@@ -287,13 +290,25 @@
     return pltpu.CompilerParams(collective_id=cid, has_side_effects=True, vmem_limit_bytes=60 << 20)
 
 
-def by_rows(count):
+def by_rows(count, begin=0):
     def run(body):
-        @pl.loop(0, count // CHUNK)
+        @pl.loop(begin // CHUNK, count // CHUNK)
         def _(i):
             body(pl.ds(pl.multiple_of(i * CHUNK, CHUNK), CHUNK))
 
     return run
+
+
+def gather_as_made(me, make, own, out, send, recv, local_sem):
+    rows = own.shape[0]
+    by_rows(rows // 2)(make)
+    first = gather_begin(me, own, out, send, recv, (True, False))
+    by_rows(rows, rows // 2)(make)
+    gather_begin(me, own, out, send, recv, (False, True), first)
+    mine = pltpu.make_async_copy(own, out.at[me], local_sem)
+    mine.start()
+    gather_end(me, own, out, send, recv, first)
+    mine.wait()
 
 
 def centre(value, epsilon):
@@ -731,7 +746,7 @@
     return hidden, low, w_down, dealt
 
 
-def gram_kernel(left, right, value, out_a, out_b, by_x, by_y, by_sib, send, recv):
+def gram_kernel(left, right, value, out, by_x, by_y, by_sib, send, recv):
     by = (by_x, by_y, by_sib)
 
     @pl.when(pl.program_id(0) == 0)
@@ -740,11 +755,9 @@
         for c in phase_one_of(value, by, (send, recv)):
             c.start()
 
-    both = lax.dot_general(
+    out[...] = lax.dot_general(
         left[...], right[...], (((0,), (0,)), ((), ())), preferred_element_type=f32
     ).astype(bf16)
-    out_a[...] = both[:, : out_a.shape[1]]
-    out_b[...] = both[:, out_a.shape[1] :]
 
     @pl.when(pl.program_id(0) == pl.num_programs(0) - 1)
     def _():
@@ -752,19 +765,18 @@
             c.wait()
 
 
-def gram_beside(left, right, value, first, block, cid):
+def gram_beside(left, right, value, block, cid):
     total, width = left.shape
-    sizes = (first, right.shape[1] - first)
+    columns = right.shape[1]
     return pl.pallas_call(
         gram_kernel,
         grid=(width // block,),
         in_specs=[pl.BlockSpec((total, block), lambda i: (0, i)), WHOLE, ANY],
-        out_specs=[pl.BlockSpec((block, size), lambda i: (i, 0)) for size in sizes] + [ANY] * 3,
-        out_shape=[jax.ShapeDtypeStruct((width, size), bf16) for size in sizes]
-        + same([value]) * 3,
+        out_specs=[pl.BlockSpec((block, columns), lambda i: (i, 0))] + [ANY] * 3,
+        out_shape=[jax.ShapeDtypeStruct((width, columns), bf16)] + same([value]) * 3,
         scratch_shapes=pair(3),
         compiler_params=params(cid),
-        cost_estimate=cost(28),
+        cost_estimate=cost(21),
         name="gram_beside",
     )(left, right, value)
 
@@ -774,14 +786,13 @@
     reduce_steps(me, [(branch, wo)], False, *scratch)
     final, total = scratch[4], scratch[5]
 
-    @by_rows(x.shape[0])
-    def _(at):
+    def make(at):
         value = x[at, :].astype(f32) + summed(total, final, at)
         middle[at, :] = value
         unit, _ = centre(value, layer_epsilon)
         own[at, :] = (unit * small[2:3, :] + small[3:4, :]).astype(bf16)
 
-    gather_all(me, own, normed_all, send1, recv1, sem1)
+    gather_as_made(me, make, own, normed_all, send1, recv1, sem1)
 
 
 def make_middle(branch, wo, x, small, cid):
@@ -801,29 +812,24 @@
     )(branch, wo, x, small)
 
 
-def column_sums(out, row, value, first):
-    total = jnp.sum(value, axis=0, keepdims=True)
-
-    @pl.when(first)
-    def _():
-        out[row : row + 1, :] = total
-
-    @pl.when(jnp.logical_not(first))
-    def _():
-        out[row : row + 1, :] += total
-
-
 def back_middle_kernel(
-    low, weight, middle, back_out, small, _after, _more, back_middle, parts, middle_all,
-    own, send1, recv1, sem1, *scratch,
+    low_in, weight_in, middle, back_out, small, _after, _more, back_middle, parts, middle_all,
+    low, weight, load, own, send1, recv1, sem1, *scratch,
 ):
+    loads = [
+        pltpu.make_async_copy(low_in, low, load.at[0]),
+        pltpu.make_async_copy(weight_in.at[:, pl.ds(0, weight.shape[1])], weight, load.at[1]),
+    ]
+    for c in loads:
+        c.start()
     me = greet()
+    parts[...] = jnp.zeros_like(parts)
+    for c in loads:
+        c.wait()
     reduce_steps(me, [(low, weight)], True, *scratch)
     final, total = scratch[4], scratch[5]
-    parts[...] = jnp.zeros_like(parts)
-
-    @by_rows(middle.shape[0])
-    def _(at):
+
+    def make(at):
         back = summed(total, final, at)
         unit, root = centre(middle[at, :], layer_epsilon)
         parts[0:1, :] += jnp.sum(back * unit, axis=0, keepdims=True)
@@ -832,7 +838,7 @@
         back_middle[at, :] = value
         own[at, :] = value.astype(bf16)
 
-    gather_all(me, own, middle_all, send1, recv1, sem1)
+    gather_as_made(me, make, own, middle_all, send1, recv1, sem1)
 
 
 def make_back_middle(low, weight, middle, back_out, small, after, more, cid):
@@ -844,16 +850,24 @@
             jax.ShapeDtypeStruct((8, width), f32),
             jax.ShapeDtypeStruct((8, rows, width), bf16),
         ),
-        in_specs=[WHOLE] * 5 + [ANY, ANY],
+        in_specs=[ANY, ANY] + [WHOLE] * 3 + [ANY, ANY],
         out_specs=(WHOLE, WHOLE, ANY),
-        scratch_shapes=gather_scratch(rows, width) + reduce_scratch(rows, width),
+        scratch_shapes=[
+            pltpu.VMEM(low.shape, bf16),
+            pltpu.VMEM((width, low.shape[1]), bf16),
+            pltpu.SemaphoreType.DMA((2,)),
+        ]
+        + gather_scratch(rows, width)
+        + reduce_scratch(rows, width),
         compiler_params=params(cid),
         cost_estimate=cost(90),
         name="make_back_middle",
     )(low, weight, middle, back_out, small, after, more)
 
 
-def back_input_kernel(count, low, weight, x, back_middle, small, *refs):
+def ending_kernel(
+    count, low_in, weight_in, hidden_in, down_in, x, back_middle, middle, usable, small, *refs,
+):
     refs = list(refs)
 
     def take(n):
@@ -862,43 +876,67 @@
         return got
 
     by_x, by_y = take(count), take(count)
-    out, parts = take(2)
+    back_input, out, parts = take(3)
     half_low, half_high, sib_x, sib_y, sib_low, sib_high = (take(count) for _ in range(6))
+    low, weight, hidden, down, load = take(5)
     two, three = take(2), take(2)
-    scratch = refs
+    first, second = take(8), take(8)
+    loads = [
+        pltpu.make_async_copy(low_in, low, load.at[0]),
+        pltpu.make_async_copy(weight_in.at[:, pl.ds(0, weight.shape[1])], weight, load.at[1]),
+        pltpu.make_async_copy(hidden_in, hidden, load.at[2]),
+        pltpu.make_async_copy(down_in, down, load.at[3]),
+    ]
+    for c in loads:
+        c.start()
     me = greet()
-    started, last = [], []
-
-    def early():
-        started.extend(phase_two(me, by_x, by_y, half_low, half_high, sib_x, sib_y, *two))
-
-    def late():
-        for c in started:
-            c.wait()
-        last.extend(phase_three(me, half_low, half_high, sib_low, sib_high, *three))
-
-    reduce_steps(me, [(low, weight)], True, *scratch, hooks=(early, lambda: None, late))
-    final, total = scratch[4], scratch[5]
+    started = phase_two(me, by_x, by_y, half_low, half_high, sib_x, sib_y, *two)
     parts[...] = jnp.zeros_like(parts)
+    loads[0].wait()
+    loads[1].wait()
+    one = reduce_stages(me, [(low, weight)], True, *first)
+    other = reduce_stages(me, [(hidden, down)], False, *second)
+    next(one)
+    loads[2].wait()
+    loads[3].wait()
+    next(other)
+    next(one)
+    next(other)
+    for _ in one:
+        pass
 
     @by_rows(x.shape[0])
     def _(at):
-        back = summed(total, final, at)
+        back = summed(first[5], first[4], at)
         unit, root = centre(x[at, :].astype(f32), layer_epsilon)
         parts[0:1, :] += jnp.sum(back * unit, axis=0, keepdims=True)
         parts[1:2, :] += jnp.sum(back, axis=0, keepdims=True)
         value = back_middle[at, :] + through_norm(back * small[0:1, :], unit, root)
-        out[at, :] = value.astype(bf16)
+        back_input[at, :] = value.astype(bf16)
+
+    for _ in other:
+        pass
+    for c in started:
+        c.wait()
+    last = phase_three(me, half_low, half_high, sib_low, sib_high, *three)
+
+    @by_rows(middle.shape[0])
+    def _(at):
+        value = middle[at, :] + summed(second[5], second[4], at)
+        out[at, :] = jnp.where(usable[at, :] > 0.5, value, 0.0).astype(bf16)
 
     for c in last:
         c.wait()
 
 
-def make_back_input(low, weight, x, back_middle, small, by_x, by_y, cid):
+def make_ending(
+    low, weight, hidden, down, x, back_middle, middle, usable, small, by_x, by_y, cid
+):
     rows, width = x.shape
     count = len(by_x)
     shapes = (
         [
+            jax.ShapeDtypeStruct((rows, width), bf16),
             jax.ShapeDtypeStruct((rows, width), bf16),
             jax.ShapeDtypeStruct((8, width), f32),
         ]
@@ -907,116 +945,82 @@
         + same(by_x, True) * 2
     )
     out = pl.pallas_call(
-        functools.partial(back_input_kernel, count),
+        functools.partial(ending_kernel, count),
         out_shape=shapes,
-        in_specs=[WHOLE] * 5 + [ANY] * (2 * count),
-        out_specs=[WHOLE] * 2 + [ANY] * (len(shapes) - 2),
-        scratch_shapes=pair(4 * count) + pair(2 * count) + reduce_scratch(rows, width),
+        in_specs=[ANY] * 4 + [WHOLE] * 5 + [ANY] * (2 * count),
+        out_specs=[WHOLE] * 3 + [ANY] * (len(shapes) - 3),
+        scratch_shapes=[
+            pltpu.VMEM(low.shape, bf16),
+            pltpu.VMEM((width, low.shape[1]), bf16),
+            pltpu.VMEM(hidden.shape, bf16),
+            pltpu.VMEM(down.shape, bf16),
+            pltpu.SemaphoreType.DMA((4,)),
+        ]
+        + pair(4 * count)
+        + pair(2 * count)
+        + reduce_scratch(rows, width)
+        + reduce_scratch(rows, width),
         compiler_params=params(cid),
-        cost_estimate=cost(70),
-        name="make_back_input",
-    )(low, weight, x, back_middle, small, *by_x, *by_y)
-    rest = out[2:]
-    return out[0], out[1], [rest[i * count : (i + 1) * count] for i in range(6)]
-
-
-def ending_kernel(count, hidden, weight, middle, usable, parts_one, parts_two, *refs):
-    fresh, refs = refs[:count], refs[count:]
-    out, sums = refs[:2]
-    fresh_all, refs = refs[2 : 2 + count], refs[2 + count :]
-    parts, turned, far, send_s, recv_s, send_f, recv_f = refs[:7]
-    sems, scratch = [refs[7 + 3 * k : 10 + 3 * k] for k in range(count)], refs[7 + 3 * count :]
+        cost_estimate=cost(100),
+        name="make_ending",
+    )(
+        low, weight, hidden, down, x, back_middle, middle, usable, small,
+        *by_x, *by_y,
+    )
+    rest = out[3:]
+    return *out[:3], [rest[i * count : (i + 1) * count] for i in range(6)]
+
+
+def small_sums_kernel(parts_one, parts_two, _after, sums, parts, turned, far, send_s, recv_s, send_f, recv_f):
     me = greet(True)
     z = lax.axis_index("shard")
-    shards = lax.axis_size("shard")
     parts[...] = jnp.zeros_like(parts)
     parts[0:2, :] = parts_one[0:2, :]
     parts[2:4, :] = parts_two[0:2, :]
-    part = parts.shape[1] // shards
-    turns = [
-        push(parts, turned.at[i], send_s.at[i], recv_s.at[i], flip(me, mask))
-        for i, mask in enumerate((1, 2, 4))
-    ]
-    mine = [pltpu.make_async_copy(a, b.at[me], s[2]) for a, b, s in zip(fresh, fresh_all, sems)]
-    for c in mine:
+    for i, mask in enumerate((1, 2, 4)):
+        c = push(parts, turned.at[i], send_s.at[i], recv_s.at[i], flip(me, mask))
         c.start()
-    turns[0].start()
-    started, waiting = [], []
-
-    def add(i):
-        turns[i].wait()
+        c.wait()
         parts[...] += turned[i]
-
-    def early():
-        add(0)
-        turns[1].start()
-        for a, b, s in zip(fresh, fresh_all, sems):
-            started.append(gather_begin(me, a, b, s[0], s[1]))
-
-    def between():
-        add(1)
-        turns[2].start()
-
-    def late():
-        add(2)
-        for k, other in enumerate(others()):
-            c = pltpu.make_async_remote_copy(
-                src_ref=parts.at[:, pl.ds(pl.multiple_of(other * part, part), part)],
-                dst_ref=far.at[k],
-                send_sem=send_f.at[k],
-                recv_sem=recv_f.at[k],
-                device_id={"shard": other},
-                device_id_type=MESHID,
-            )
-            c.start()
-            waiting.append(c)
-        for a, b, s, first in zip(fresh, fresh_all, sems, started):
-            gather_end(me, a, b, s[0], s[1], first)
-
-    reduce_steps(me, [(hidden, weight)], False, *scratch, hooks=(early, between, late))
-    final, total = scratch[4], scratch[5]
-
-    @by_rows(middle.shape[0])
-    def _(at):
-        value = middle[at, :] + summed(total, final, at)
-        out[at, :] = jnp.where(usable[at, :] > 0.5, value, 0.0).astype(bf16)
-
+    part = parts.shape[1] // lax.axis_size("shard")
+    waiting = []
+    for k, other in enumerate(others()):
+        c = pltpu.make_async_remote_copy(
+            src_ref=parts.at[:, pl.ds(pl.multiple_of(other * part, part), part)],
+            dst_ref=far.at[k],
+            send_sem=send_f.at[k],
+            recv_sem=recv_f.at[k],
+            device_id={"shard": other},
+            device_id_type=MESHID,
+        )
+        c.start()
+        waiting.append(c)
     value = parts[:, pl.ds(pl.multiple_of(z * part, part), part)]
     for k, c in enumerate(waiting):
         c.wait()
         value = value + far[k]
     sums[...] = value
-    for c in mine:
-        c.wait()
-
-
-def make_ending(hidden, weight, middle, usable, parts_one, parts_two, fresh, cid):
-    rows, width = middle.shape
+
+
+def small_sums(parts_one, parts_two, after, cid):
+    width = parts_one.shape[1]
     shards = lax.axis_size("shard")
-    count = len(fresh)
-    out = pl.pallas_call(
-        functools.partial(ending_kernel, count),
-        out_shape=[
-            jax.ShapeDtypeStruct((rows, width), bf16),
-            jax.ShapeDtypeStruct((8, width // shards), f32),
-        ]
-        + [jax.ShapeDtypeStruct((8,) + a.shape, bf16) for a in fresh],
-        in_specs=[WHOLE] * 6 + [ANY] * count,
-        out_specs=[WHOLE, WHOLE] + [ANY] * count,
+    return pl.pallas_call(
+        small_sums_kernel,
+        out_shape=jax.ShapeDtypeStruct((8, width // shards), f32),
+        in_specs=[WHOLE, WHOLE, ANY],
+        out_specs=WHOLE,
         scratch_shapes=[
             pltpu.VMEM((8, width), f32),
             pltpu.VMEM((3, 8, width), f32),
             pltpu.VMEM((shards - 1, 8, width // shards), f32),
         ]
         + pair(3)
-        + pair(shards - 1)
-        + gather_scratch(rows, width)[1:] * count
-        + reduce_scratch(rows, width),
+        + pair(shards - 1),
         compiler_params=params(cid),
-        cost_estimate=cost(78),
-        name="make_ending",
-    )(hidden, weight, middle, usable, parts_one, parts_two, *fresh)
-    return out[0], out[1], out[2:]
+        cost_estimate=cost(15),
+        name="small_sums",
+    )(parts_one, parts_two, after)
 
 
 MASKS = (0, 2, 4, 6, 6, 1, 3, 5, 7, 7)
@@ -1028,6 +1032,23 @@
     corner, sib_corner = jnp.concatenate([low, high]), jnp.concatenate([sib_low, sib_high])
     stacked = jnp.stack([value, sib, by_x, sib_x, by_y, sib_y, corner, sib_corner])
     return jnp.take(stacked, jnp.arange(8) ^ lax.axis_index("tp"), axis=0)
+
+
+def collect_kernel(own, _after, out, send, recv, local_sem):
+    gather_all(greet(), own, out, send, recv, local_sem)
+
+
+def plane_collect(value, after, cid):
+    return pl.pallas_call(
+        collect_kernel,
+        out_shape=jax.ShapeDtypeStruct((8,) + value.shape, value.dtype),
+        in_specs=[ANY, ANY],
+        out_specs=ANY,
+        scratch_shapes=gather_scratch(*value.shape)[1:],
+        compiler_params=params(cid),
+        cost_estimate=cost(22),
+        name="plane_collect",
+    )(value, after)
 
 
 def widen_two_kernel(steps, shards, *refs):
@@ -1180,7 +1201,8 @@
     came = exchange(
         jnp.concatenate([forward_dot(send_mix, tokens).astype(bf16), extra], axis=1)
     )
-    t_early = t + (came[0, 0].astype(f32) > 100.0).astype(jnp.int32)
+    sent_back = forward_dot(send_mix, cotangent).astype(bf16)
+    came_back = exchange(sent_back)
     arrived = came[:, width:].reshape(outer, tp, shards, -1)
     small = jnp.transpose(arrived[0, 0, :, : 4 * part].reshape(shards, 4, part), (1, 0, 2))
     small = small.reshape(4, width).astype(f32)
@@ -1193,7 +1215,7 @@
 
     def cut(weight):
         part = weight.shape[1] // tp
-        return lax.dynamic_slice_in_dim(weight, t_early * part, part, axis=1)
+        return lax.dynamic_slice_in_dim(weight, t * part, part, axis=1)
 
     out_unit = out_weight.shape[0] // tp
     unit = down_weight.shape[0] // tp
@@ -1213,7 +1235,7 @@
         value = value.reshape(shards, cuts, count, width // cuts)
         return jnp.transpose(value, (0, 2, 1, 3)).reshape(shards, count, width)
 
-    out_piece = lax.dynamic_slice_in_dim(out_weight, t_early * out_unit, out_unit, axis=0)
+    out_piece = lax.dynamic_slice_in_dim(out_weight, t * out_unit, out_unit, axis=0)
     w_one = along_z(
         jnp.concatenate(
             [cut(w) for w in (query_weight, key_weight, value_weight, gate_weight)]
@@ -1224,22 +1246,20 @@
     ends = jnp.cumsum(lengths, axis=1, dtype=jnp.int32)[:, -2]
     usable = (jnp.arange(pack_rows, dtype=jnp.int32)[None, :] < ends[:, None]).astype(f32)
     usable = usable.reshape(rows, 1)
-    came_back = exchange(forward_dot(send_mix, cotangent).astype(bf16))
     x, normed = entry(came, work_mix, small, 0)
-    t_late = t + (x[0, 0].astype(f32) > 100.0).astype(jnp.int32)
-
     def unit_columns(weight):
         return [
-            lax.dynamic_slice_in_dim(weight, (k * tp + t_late) * unit, unit, axis=1)
+            lax.dynamic_slice_in_dim(weight, (k * tp + t) * unit, unit, axis=1)
             for k in range(shards)
         ]
 
-    down_piece = lax.dynamic_slice_in_dim(down_weight, t_late * unit, unit, axis=0)
-    w_two = along_z(
+    down_piece = lax.dynamic_slice_in_dim(down_weight, t * unit, unit, axis=0)
+    second_piece = lax.optimization_barrier(
         jnp.concatenate(
             unit_columns(gelu_weight) + unit_columns(up_weight) + [fold(down_piece)], axis=1
         )
     )
+    w_two = along_z(second_piece + jnp.isnan(x[0, 0]).astype(bf16))
     back_out, back_low = entry_back(came_back, work_mix, usable, x, 7)
     normed, back_low = normed.reshape(group_rows, width), back_low.reshape(group_rows, width)
     cosine, sine, decays, _ = pack_tables(all_lengths, pack_rows, t + jnp.arange(1))
@@ -1273,17 +1293,13 @@
         middle_low, wo, q_rot, k_rot, v_low, weights_low, gating, retained, cosine, sine, decays,
         down_sum, rows, 8,
     )
-    first_gram, third_gram, *second_by = gram_beside(
-        normed, first_low, second_sum, edges[2], 256, 9
-    )
-    first_sum, third_sum = to_owner(first_gram), to_owner(third_gram)
+    first_gram, *second_by = gram_beside(normed, first_low, second_sum, 256, 9)
+    first_sum = to_owner(first_gram)
     by_x, by_y, by_sib = ([a, b] for a, b in zip(second_by, down_by))
-    back_inputs, parts_one, groups = make_back_input(
-        first_low, w_one, x, back_middle, small, by_x, by_y, 4
-    )
-    ending, sums, (outs, firsts) = make_ending(
-        hidden, w_down, middle, usable, parts_one, parts_two, [out_sum, first_sum], 5
-    )
+    back_inputs, ending, parts_one, groups = make_ending(
+        first_low, w_one, hidden, w_down, x, back_middle, middle, usable, small, by_x, by_y, 5
+    )
+    outs = plane_collect(out_sum, ending, 10)
     low, high, sib_x, sib_y, sib_low, sib_high = groups
     seconds, downs = (
         [
@@ -1303,10 +1319,11 @@
         both = in_order(seconds).reshape(tp, piece_rows, 2, shards, unit)
         both = jnp.transpose(both, (2, 1, 3, 0, 4)).reshape(2, piece_rows, -1).astype(f32)
         gelu_gradient, up_gradient = both[0], both[1]
-    thirds = lax.all_gather(third_sum + sums[5, 0].astype(bf16), "tp", axis=0)
-    query_gradient, key_gradient = widen_one(firsts, edges[:3], down_gradient, "widen_one")
-    value_gradient, gate_gradient = widen_one(
-        thirds, (0, value_part, 2 * value_part), query_gradient, "widen_three"
+    nothing = parts_one[5, 0].astype(bf16) + jnp.isnan(outs[0, 0, 0]).astype(bf16)
+    firsts = lax.all_gather(first_sum + nothing, "tp", axis=0)
+    sums = small_sums(parts_one, parts_two, down_gradient, 11)
+    query_gradient, key_gradient, value_gradient, gate_gradient = widen_one(
+        firsts, edges + (first_size,), sums, "widen_one"
     )
     smalls = lax.psum(sums, "outer") if outer > 1 else sums
 

time: 807 us -> 784 us (0.971)
  waiting for transfers between devices: 105 us -> 79.2 us
    all_gather x2, waiting for transfers between devices: 37.4 us -> 5.97 us  [along_z(): return lax.all_gather(piece, 'shard', axis=0, tiled=True)]
    all_gather x1, waiting for transfers between devices: 18 us -> 31.4 us  [local(): firsts = lax.all_gather(first_sum + nothing, 'tp', axis=0)]
    pallas_call x2 -> x3, Pallas kernels: 160 us -> 152 us  [the longest x1 95 us: make_ending(): pl.pallas_call(functools.partial(ending_kernel, count), out_shape=shapes,...]
    pallas_call x2 -> x1, Pallas kernels: 17.4 us -> 14 us  [widen_one(): pl.pallas_call(functools.partial(widen_one_kernel, edges), grid=(rows //...]
    unnamed x51 -> x57, local copies, waits for them, and re-layouts: 17.7 us -> 15.6 us
  transfers between devices with their start and end apart: 11 -> 10, of which waited for: 4 -> 3; matrix products, arithmetic and copies ran while one was open for 8% -> 8% of each run, Pallas kernels for 67% -> 68%
where the time goes in v4:
time: 784 us; the launch traced here: 777 us
  Pallas kernels  570 us (73%)
  waiting for transfers between devices  79.2 us (10%)
  matrix products  39.1 us (5%)
  local copies, waits for them, and re-layouts  31.2 us (4%)
  starting transfers between devices  23.4 us (3%)
  between operations  18.5 us (2%)
  other arithmetic  15.8 us (2%)
    pallas_call x1, Pallas kernels, make_ending(): pl.pallas_call(functools.partial(ending_kernel, count), out_shape=shapes,...  95 us
    pallas_call x1, Pallas kernels, make_back_middle(): pl.pallas_call(back_middle_kernel, out_shape=(jax.ShapeDtypeStruct((rows,...  90.3 us
    pallas_call x1, Pallas kernels, make_middle(): pl.pallas_call(middle_kernel, out_shape=(jax.ShapeDtypeStruct((rows, widt...  88.4 us
    pallas_call x1, Pallas kernels, entry(): pl.pallas_call(entry_kernel, out_shape=(jax.ShapeDtypeStruct((rows, width...  53.9 us
    pallas_call x1, Pallas kernels, entry_back(): pl.pallas_call(entry_back_kernel, out_shape=(jax.ShapeDtypeStruct((rows,...  45.9 us
    all_to_all x3, waiting for transfers between devices, exchange(): lax.all_to_all(value.reshape(device_count, rows // device_count, value.sh...  41.6 us
    dot_general x5, matrix products, gram_rows(): lax.dot_general(leading, trailing, (((0,), (0,)), ((), ())), preferred_el...  36 us
    pallas_call x1, Pallas kernels, small_sums(): pl.pallas_call(small_sums_kernel, out_shape=jax.ShapeDtypeStruct((8, widt...  33.6 us
  transfers between devices with their start and end apart: 10, of which 3 were waited for; matrix products, arithmetic and copies ran while one was open for 8% of the time, Pallas kernels for 68%

profile of v4, /device:TPU:0, one launch (start us, length us, event | category | flops | bytes accessed | tf_op | source)
XLA Modules:
  0.0 777.1 jit_solution(12817606326566573493)
XLA Ops:
  7.2 2.2 constant_dynamic-slice_fusion
  9.7 1.0 copy.41
  10.7 1.0 dynamic-slice_dynamic-update-slice_fusion.3
  11.7 1.0 dynamic-slice_dynamic-update-slice_fusion.2
  12.7 1.1 dynamic-slice_dynamic-update-slice_fusion.1
  13.9 1.1 dynamic-slice_dynamic-update-slice_fusion
  15.1 1.3 copy-done.2
  18.3 1.1 pad_maximum_fusion
  19.4 7.4 all-to-all-start
  30.6 1.0 dynamic-slice_dynamic-update-slice_fusion.9
  31.6 1.0 dynamic-slice_dynamic-update-slice_fusion.8
  32.5 1.0 dynamic-slice_dynamic-update-slice_fusion.7
  36.5 1.2 select_reduce_fusion
  37.9 2.6 fusion.2
  41.3 41.6 %all-to-all-done = bf16[32,8,2432]{2,1,0:T(8,128)(2,1)} async-done(((bf16[32,8,2432]{2,1,0:T(8,128)(2,1)}), bf16[32,8,2432]{2,1,0:T(8,128)(2,1)}, u32[]{:S(2)}, u32[]{:S(2)}) %all-to-all-start) | async-done | bytes 1245216 | tf_op jit(solution)/shard_map/all_to_all | solution.py:1185
  82.9 12.2 %all-to-all-start.1 = ((bf16[32,8,2048]{2,1,0:T(8,128)(2,1)}), bf16[32,8,2048]{2,1,0:T(8,128)(2,1)S(1)}, u32[]{:S(2)}, u32[]{:S(2)}) async-start(bf16[32,8,2048]{2,1,0:T(8,128)(2,1)} %fusion.2), calls=%async_computation.1 | async-start | bytes 2097152 | tf_op jit(solution)/shard_map/all_to_all | solution.py:1185
  96.8 53.9 %entry.1 = (bf16[256,2048]{1,0:T(8,128)(2,1)}, bf16[8,256,2048]{2,1,0:T(8,128)(2,1)}) custom-call(bf16[256,2432]{1,0:T(8,128)(2,1)} %bitcast.1.came, bf16[256,256]{1,0:T(8,128)(2,1)} %fusion.7.mix, f32[8,2048]{1,0:T(8,128)} %pad_convert_fusion.small), custom_call_target="tpu_custom_call" | custom-call | flops 49999998976 | bytes 150000000 | tf_op jit(solution)/shard_map/entry/pallas_call | solution.py:368
  151.1 1.2 slice.44
  153.6 1.2 broadcast_add_fusion.1
  155.3 5.5 multiply_sine_fusion
  160.9 1.0 copy-done.5
  161.8 45.9 %entry_back.1 = (bf16[256,2048]{1,0:T(8,128)(2,1)}, bf16[8,256,2048]{2,1,0:T(8,128)(2,1)}) custom-call(bf16[256,2048]{1,0:T(8,128)(2,1)} %bitcast.65, bf16[256,256]{1,0:T(8,128)(2,1)} %fusion.7.mix, f32[256,1]{1,0:T(8,128)} %copy.46.usable, bf16[256,2048]{1,0:T(8,128)(2,1)} %get-tuple-element.69.x._after), custom_call_target="tpu_custom_call" | custom-call | flops 44999999488 | bytes 135000000 | tf_op jit(solution)/shard_map/entry_back/pallas_call | solution.py:398
  207.7 1.3 and_select_fusion.decays
  209.0 5.9 all-gather.5.cloned.1.call-done.weight.weight_in
  215.0 1.6 slice-done
  216.5 1.6 copy.53
  218.2 30.4 %retain.1 = (bf16[2048,256]{1,0:T(8,128)(2,1)}, bf16[2048,256]{1,0:T(8,128)(2,1)}, bf16[2048,512]{1,0:T(8,128)(2,1)}, bf16[16,128,128]{2,1,0:T(8,128)(2,1)}, f32...) custom-call(bf16[2048,2048]{1,0:T(8,128)(2,1)} %bitcast.74, ...), custom_call_target="tpu_custom_call" | custom-call | flops 24000000000 | bytes 72000000 | tf_op jit(solution)/shard_map/retain/pallas_call | solution.py:586
  248.6 88.4 %make_middle.1 = (f32[256,2048]{1,0:T(8,128)}, bf16[8,256,2048]{2,1,0:T(8,128)(2,1)}) custom-call(bf16[2048,512]{1,0:T(8,128)(2,1)} %get-tuple-element.67.branch, bf16[512,2048]{1,0:T(8,128)(2,1)} %bitcast.85, bf16[256,2048]{1,0:T(8,128)(2,1)} %get-tuple-element.69.x._after, f32[8,2048]{1,0:T(8,128)} %pad_convert_fusion.small), custom_call_target="tpu_custom_call" | custom-call | flops 85000003584 | bytes 255000000 | tf_op jit(solution)/shard_map/make_middle/pallas_call | solution.py:800
  337.0 29.4 %feed.1 = (bf16[2048,512]{1,0:T(8,128)(2,1)}, bf16[2048,1024]{1,0:T(8,128)(2,1)}, bf16[512,2048]{1,0:T(8,128)(2,1)}, bf16[2048,512]{1,0:T(8,128)(2,1)}) custom-call(bf16[2048,2048]{1,0:T(8,128)(2,1)} %bitcast.83, bf16[2048,2048]{1,0:T(8,128)(2,1)} %bitcast.79, bf16[2048,1536]{1,0:T(8,128)(2,1)} %all-gather.7.cloned.1.call-done.w_two.weight_in, ...), custom_call_target="tpu_custom_call" | custom-call | flops 25999998976 | bytes 78000000 | tf_op jit(solution)/shard_map/feed/pallas_call | solution.py:726
  366.4 9.9 %convolution_convert_fusion.4._after = bf16[512,2048]{1,0:T(8,128)(2,1)} fusion(bf16[2048,512]{1,0:T(8,128)(2,1)} %get-tuple-element.75.hidden_in, bf16[2048,2048]{1,0:T(8,128)(2,1)} %bitcast.80), kind=kOutput, calls=%fused_computation.6 | convolution fusion | flops 4296015872 | bytes 12582912 | tf_op jit(solution)/shard_map/dot_general | solution.py:54
  376.6 14.0 %convolution_convert_fusion.2._more = bf16[2048,1024]{1,0:T(8,128)(2,1)} fusion(bf16[2048,2048]{1,0:T(8,128)(2,1)} %bitcast.84, bf16[2048,1024]{1,0:T(8,128)(2,1)} %get-tuple-element.72.low_in), kind=kOutput, calls=%fused_computation.4 | convolution fusion | flops 8592031744 | bytes 16777216 | tf_op jit(solution)/shard_map/dot_general | solution.py:54
  390.6 90.3 %make_back_middle.1 = (f32[256,2048]{1,0:T(8,128)}, f32[8,2048]{1,0:T(8,128)}, bf16[8,256,2048]{2,1,0:T(8,128)(2,1)}) custom-call(bf16[2048,1024]{1,0:T(8,128)(2,1)} %get-tuple-element.72.low_in, bf16[2048,1536]{1,0:T(8,128)(2,1)} %all-gather.7.cloned.1.call-done.w_two.weight_in, f32[256,2048]{1,0:T(8,128)} %get-tuple-element.73.middle, ...), custom_call_target="tpu_custom_call" | custom-call | flops 89999998976 | bytes 270000000 | tf_op jit(solution)/shard_map/make_back_middle/pallas_call | solution.py:846
  480.9 9.2 %convolution_convert_fusion.3 = bf16[512,2048]{1,0:T(8,128)(2,1)} fusion(bf16[2048,512]{1,0:T(8,128)(2,1)S(1)} %copy-done.18, bf16[2048,2048]{1,0:T(8,128)(2,1)} %bitcast.81), kind=kOutput, calls=%fused_computation.5 | convolution fusion | flops 4296015872 | bytes 12582912 | tf_op jit(solution)/shard_map/dot_general | solution.py:54
  490.5 18.8 %retain_back.1 = (bf16[2048,1536]{1,0:T(8,128)(2,1)}, bf16[128,2048]{1,0:T(8,128)(2,1)}, bf16[128,2048]{1,0:T(8,128)(2,1)}, bf16[128,2048]{1,0:T(8,128)(2,1)}) custom-call(bf16[2048,2048]{1,0:T(8,128)(2,1)} %bitcast.82, bf16[512,2048]{1,0:T(8,128)(2,1)} %bitcast.86, bf16[2048,256]{1,0:T(8,128)(2,1)} %get-tuple-element.77.q_in, ...), custom_call_target="tpu_custom_call" | custom-call | flops 20000000000 | bytes 60000000 | tf_op jit(solution)/shard_map/retain_back/pallas_call | solution.py:665
  509.3 29.7 %gram_beside.1 = (bf16[2048,1536]{1,0:T(8,128)(2,1)}, bf16[512,1024]{1,0:T(8,128)(2,1)}, bf16[512,1024]{1,0:T(8,128)(2,1)}, bf16[512,1024]{1,0:T(8,128)(2,1)}) custom-call(bf16[2048,2048]{1,0:T(8,128)(2,1)} %bitcast.75, bf16[2048,1536]{1,0:T(8,128)(2,1)} %get-tuple-element.83.right.low_in, bf16[512,1024]{1,0:T(8,128)(2,1)} %reduce-scatter.7.cloned.1.call-done.value.refs_0_), custom_call_target="tpu_custom_call" | custom-call | flops 20999999488 | bytes 63000000 | tf_op jit(solution)/shard_map/gram_beside/pallas_call | solution.py:771
  539.1 95.0 %make_ending.1 = (bf16[256,2048]{1,0:T(8,128)(2,1)}, bf16[256,2048]{1,0:T(8,128)(2,1)}, f32[8,2048]{1,0:T(8,128)}, bf16[256,1024]{1,0:T(8,128)(2,1)}, bf16[64,20...) custom-call(bf16[2048,1536]{1,0:T(8,128)(2,1)} %get-tuple-element.83, ...), custom_call_target="tpu_custom_call" | custom-call | flops 99999997952 | bytes 300000000 | tf_op jit(solution)/shard_map/make_ending/pallas_call | solution.py:947
  634.1 1.2 slice.58
  635.3 23.6 %plane_collect.1.refs_20_ = bf16[8,128,2048]{2,1,0:T(8,128)(2,1)} custom-call(bf16[128,2048]{1,0:T(8,128)(2,1)} %reduce-scatter.11.cloned.1.call-done.own, bf16[256,2048]{1,0:T(8,128)(2,1)} %get-tuple-element.90._after), custom_call_target="tpu_custom_call" | custom-call | flops 22000001024 | bytes 66000000 | tf_op jit(solution)/shard_map/plane_collect/pallas_call | solution.py:1042
  658.9 1.2 slice.48
  662.1 2.8 broadcast_add_fusion
  664.9 2.1 fusion
  667.1 2.9 all-to-all-start.2
  670.0 17.2 %widen_two.1 = (f32[512,4096]{1,0:T(8,128)}, f32[512,4096]{1,0:T(8,128)}, f32[8,128,2048]{2,1,0:T(8,128)}, f32[8,128,2048]{2,1,0:T(8,128)}) custom-call(bf16[512,1024]{1,0:T(8,128)(2,1)} %reduce-scatter.7.cloned.1.call-done.value.refs_0_, bf16[512,1024]{1,0:T(8,128)(2,1)} %get-tuple-element.86.refs_0_.refs_1_, bf16[512,1024]{1,0:T(8,128)(2,1)} %get-tuple-element.88.refs_2_, ...), custom_call_target="tpu_custom_call" | custom-call | flops 24999999488 | bytes 75000000 | tf_op jit(solution)/shard_map/widen_two/pallas_call | solution.py:1100
  687.2 33.6 %small_sums.1._after = f32[8,512]{1,0:T(8,128)} custom-call(f32[8,2048]{1,0:T(8,128)} %get-tuple-element.93.parts_one, f32[8,2048]{1,0:T(8,128)} %get-tuple-element.95.parts_two, f32[1024,2048]{1,0:T(8,128)} %bitcast.76), custom_call_target="tpu_custom_call" | custom-call | flops 15000000512 | bytes 45000000 | tf_op jit(solution)/shard_map/small_sums/pallas_call | solution.py:1008
  720.8 1.5 fusion.17
  723.0 1.5 fusion.16
  724.5 31.4 %all-gather.9.cloned.1.call-done = bf16[4096,1536]{1,0:T(8,128)(2,1)} async-done(((bf16[512,1536]{1,0:T(8,128)(2,1)}), bf16[4096,1536]{1,0:T(8,128)(2,1)}) %all-gather.9.cloned.1.call-update) | async-done | bytes 12582928 | tf_op jit(solution)/shard_map/all_gather | solution.py:1323
  755.9 14.0 %widen_one.1 = (f32[512,2048]{1,0:T(8,128)}, f32[512,2048]{1,0:T(8,128)}, f32[512,4096]{1,0:T(8,128)}, f32[512,4096]{1,0:T(8,128)}) custom-call(bf16[8,512,1536]{2,1,0:T(8,128)(2,1)} %bitcast.73, f32[8,512]{1,0:T(8,128)} %small_sums.1._after), custom_call_target="tpu_custom_call" | custom-call | flops 14000000000 | bytes 42000000 | tf_op jit(solution)/shard_map/widen_one/pallas_call | solution.py:1127
  (109 shorter events, 13.7 us)
Async XLA Ops:
  7.2 10.6 %copy-start = (bf16[256,2048]{1,0:T(8,128)(2,1)S(1)}, bf16[256,2048]{1,0:T(8,128)(2,1)}, u32[]{:S(2)}) copy-start(bf16[256,2048]{1,0:T(8,128)(2,1)} %param.16) | copy-start | bytes 3145732
  7.2 207.8 %all-gather.5.cloned.1.call-start = ((), (), s32[]{:S(2)}) async-start(), calls=%async_computation.7 | async-start | bytes 10485760 | tf_op jit(solution)/shard_map/all_gather | solution.py:1214
  10.7 4.4 copy-start.4
  13.8 2.7 copy-start.13
  13.9 2.7 copy-start.14
  13.9 2.9 copy-start.15
  13.9 3.1 copy-start.16
  13.9 3.3 copy-start.17
  13.9 3.6 copy-start.8
  15.1 1.3 copy-start.2
  17.8 20.1 %copy-start.9 = (s32[256]{0:T(256)}, s32[256]{0:T(256)S(1)}, u32[]{:S(2)}) copy-start(s32[256]{0:T(256)S(1)} %convert_reduce_fusion.1) | copy-start | bytes 3076
  18.3 9.9 %copy-start.3 = (bf16[128,2048]{1,0:T(8,128)(2,1)S(1)}, bf16[128,2048]{1,0:T(8,128)(2,1)}, u32[]{:S(2)}) copy-start(bf16[128,2048]{1,0:T(8,128)(2,1)} %get-tuple-element.126) | copy-start | bytes 1572868
  19.4 63.5 %all-to-all-start = ((bf16[32,8,2432]{2,1,0:T(8,128)(2,1)}), bf16[32,8,2432]{2,1,0:T(8,128)(2,1)}, u32[]{:S(2)}, u32[]{:S(2)}) async-start(bf16[32,8,2432]{2,1,0:T(8,128)(2,1)} %pad_maximum_fusion), calls=%async_computation | async-start | bytes 2490368 | tf_op jit(solution)/shard_map/all_to_all | solution.py:1185
  37.9 45.0 %copy-start.11 = (s32[256]{0:T(256)}, s32[256]{0:T(256)S(1)}, u32[]{:S(2)}) copy-start(s32[256]{0:T(256)S(1)} %convert_reduce_fusion) | copy-start | bytes 3076
  82.9 77.9 %all-to-all-start.1 = ((bf16[32,8,2048]{2,1,0:T(8,128)(2,1)}), bf16[32,8,2048]{2,1,0:T(8,128)(2,1)S(1)}, u32[]{:S(2)}, u32[]{:S(2)}) async-start(bf16[32,8,2048]{2,1,0:T(8,128)(2,1)} %fusion.2), calls=%async_computation.1 | async-start | bytes 2097152 | tf_op jit(solution)/shard_map/all_to_all | solution.py:1185
  95.1 241.9 %all-gather.7.cloned.1.call-start = ((), (), s32[]{:S(2)}) async-start(), calls=%async_computation.8 | async-start | bytes 7864320 | tf_op jit(solution)/shard_map/all_gather | solution.py:1214
  154.9 335.6 %reduce-scatter.5.cloned.1.call-start = ((), (), s32[]{:S(2)}) async-start(), calls=%async_computation.9 | async-start | bytes 2621440 | tf_op jit(solution)/shard_map/reduce_scatter | solution.py:1283
  160.8 1.0 copy-start.5
  214.9 1.6 slice-start
  376.3 133.0 %reduce-scatter.7.cloned.1.call-start = ((), (), s32[]{:S(2)}) async-start(), calls=%async_computation.10 | async-start | bytes 5242880 | tf_op jit(solution)/shard_map/reduce_scatter | solution.py:1283
  390.6 244.7 %reduce-scatter.11.cloned.1.call-start = ((), (), s32[]{:S(2)}) async-start(), calls=%async_computation.12 | async-start | bytes 2621440 | tf_op jit(solution)/shard_map/reduce_scatter | solution.py:1283
  390.6 90.3 %copy-start.18 = (bf16[2048,512]{1,0:T(8,128)(2,1)S(1)}, bf16[2048,512]{1,0:T(8,128)(2,1)}, u32[]{:S(2)}) copy-start(bf16[2048,512]{1,0:T(8,128)(2,1)} %get-tuple-element.94) | copy-start | bytes 6291460
  490.2 171.9 %reduce-scatter.9.cloned.1.call-start = ((), (), s32[]{:S(2)}) async-start(), calls=%async_computation.11 | async-start | bytes 7864320 | tf_op jit(solution)/shard_map/reduce_scatter | solution.py:1283
  539.0 216.8 %all-gather.9.cloned.1.call-start = ((), (), s32[]{:S(2)}) async-start(), calls=%async_computation.13 | async-start | bytes 14155776 | tf_op jit(solution)/shard_map/all_gather | solution.py:1323
  662.0 2.9 copy-start.6
  662.0 2.9 copy-start.7
  662.0 2.9 copy-start.12
  667.1 55.2 %all-to-all-start.2 = ((bf16[32,8,4096]{2,1,0:T(8,128)(2,1)}), bf16[32,8,4096]{2,1,0:T(8,128)(2,1)S(1)}, u32[]{:S(2)}, u32[]{:S(2)}) async-start(bf16[32,8,4096]{2,1,0:T(8,128)(2,1)} %fusion), calls=%async_computation.4 | async-start | bytes 4194304 | tf_op jit(solution)/shard_map/all_to_all | solution.py:1185
  687.1 35.1 %copy-start.10 = (s32[256]{0:T(256)S(1)}, s32[256]{0:T(256)}, u32[]{:S(2)}) copy-start(s32[256]{0:T(256)} %copy-done.9) | copy-start | bytes 3076
  755.9 14.0 %copy-start.1 = (bf16[256,2048]{1,0:T(8,128)(2,1)S(1)}, bf16[256,2048]{1,0:T(8,128)(2,1)}, u32[]{:S(2)}) copy-start(bf16[256,2048]{1,0:T(8,128)(2,1)} %param.16) | copy-start | bytes 3145732
Sparse Core Ops, SparseCore 0:
  16.6 198.2 all-gather.4
  217.1 114.3 all-gather.6
  376.4 43.5 reduce-scatter.4
  422.9 76.1 reduce-scatter.6
  501.8 44.3 reduce-scatter.10
  548.4 110.0 reduce-scatter.8
  665.0 90.8 all-gather.8

commit v5 on v4

--- a/solution.py
+++ b/solution.py
@@ -681,12 +681,54 @@
     )(middle_low, wo, q, k, v, w, g, r, cosine, sine, decays, value)
 
 
+def half_views(branch, dealt, count, begin):
+    size = branch.shape[1] // count
+    rows = dealt.shape[0]
+    return (
+        lambda i: branch.at[pl.ds(begin, rows), pl.ds(pl.multiple_of(i * size, size), size)],
+        column_blocks(dealt, size),
+    )
+
+
+def gram_deal_kernel(count, begin, left, right, branch, out, dealt, *sems):
+    views = half_views(branch, dealt, count, begin)
+
+    @pl.when(pl.program_id(0) == 0)
+    def _():
+        deal_start(True, count, *views, *sems)
+
+    out[...] = lax.dot_general(
+        left[...], right[...], (((0,), (0,)), ((), ())), preferred_element_type=f32
+    ).astype(bf16)
+
+    @pl.when(pl.program_id(0) == pl.num_programs(0) - 1)
+    def _():
+        deal_wait(True, count, *views, *sems)
+
+
+def gram_deal(left, right, branch, count, cid):
+    total, width = left.shape
+    columns = right.shape[1]
+    rows = branch.shape[0] // 2
+    return pl.pallas_call(
+        functools.partial(gram_deal_kernel, count, rows),
+        grid=(width // 256,),
+        in_specs=[pl.BlockSpec((total, 256), lambda i: (0, i)), WHOLE, ANY],
+        out_specs=(pl.BlockSpec((256, columns), lambda i: (i, 0)), ANY),
+        out_shape=(
+            jax.ShapeDtypeStruct((width, columns), bf16),
+            jax.ShapeDtypeStruct((rows, branch.shape[1]), bf16),
+        ),
+        scratch_shapes=deal_scratch(count),
+        compiler_params=params(cid),
+        cost_estimate=cost(16),
+        name="gram_deal",
+    )(left, right, branch)
+
+
 def feed_kernel(shards, count, normed_two, back_low, w_two, branch, hidden, low, w_down, dealt, *sems):
     size = hidden.shape[1]
-    views = (
-        column_blocks(branch, branch.shape[1] // count) if count else None,
-        column_blocks(dealt, branch.shape[1] // count) if count else None,
-    )
+    views = half_views(branch, dealt, count, 0) if count else ()
 
     @pl.when(pl.program_id(0) == 0)
     def _():
@@ -732,7 +774,7 @@
             jax.ShapeDtypeStruct((total, size), bf16),
             jax.ShapeDtypeStruct((total, 2 * size), bf16),
             jax.ShapeDtypeStruct((size, width), bf16),
-            jax.ShapeDtypeStruct(branch.shape if count else (8, 128), bf16),
+            jax.ShapeDtypeStruct((total // 2, branch.shape[1]) if count else (8, 128), bf16),
         ),
         scratch_shapes=deal_scratch(count) if count else [],
         compiler_params=params(cid if count else None),
@@ -743,10 +785,10 @@
         pieces = jnp.transpose(branch.reshape(total, shards, -1), (1, 0, 2))
         pieces = lax.all_to_all(pieces, "tp", split_axis=0, concat_axis=0, tiled=True)
         dealt = jnp.transpose(pieces, (1, 0, 2)).reshape(total, -1)
-    return hidden, low, w_down, dealt
-
-
-def gram_kernel(left, right, value, out, by_x, by_y, by_sib, send, recv):
+    return hidden, low, w_down, dealt, count
+
+
+def gram_kernel(left, right, value, out_a, out_b, by_x, by_y, by_sib, send, recv):
     by = (by_x, by_y, by_sib)
 
     @pl.when(pl.program_id(0) == 0)
@@ -755,9 +797,11 @@
         for c in phase_one_of(value, by, (send, recv)):
             c.start()
 
-    out[...] = lax.dot_general(
+    both = lax.dot_general(
         left[...], right[...], (((0,), (0,)), ((), ())), preferred_element_type=f32
     ).astype(bf16)
+    out_a[...] = both[:, : out_a.shape[1]]
+    out_b[...] = both[:, out_a.shape[1] :]
 
     @pl.when(pl.program_id(0) == pl.num_programs(0) - 1)
     def _():
@@ -765,18 +809,19 @@
             c.wait()
 
 
-def gram_beside(left, right, value, block, cid):
+def gram_beside(left, right, value, first, block, cid):
     total, width = left.shape
-    columns = right.shape[1]
+    sizes = (first, right.shape[1] - first)
     return pl.pallas_call(
         gram_kernel,
         grid=(width // block,),
         in_specs=[pl.BlockSpec((total, block), lambda i: (0, i)), WHOLE, ANY],
-        out_specs=[pl.BlockSpec((block, columns), lambda i: (i, 0))] + [ANY] * 3,
-        out_shape=[jax.ShapeDtypeStruct((width, columns), bf16)] + same([value]) * 3,
+        out_specs=[pl.BlockSpec((block, size), lambda i: (i, 0)) for size in sizes] + [ANY] * 3,
+        out_shape=[jax.ShapeDtypeStruct((width, size), bf16) for size in sizes]
+        + same([value]) * 3,
         scratch_shapes=pair(3),
         compiler_params=params(cid),
-        cost_estimate=cost(21),
+        cost_estimate=cost(28),
         name="gram_beside",
     )(left, right, value)
 
@@ -971,18 +1016,40 @@
     return *out[:3], [rest[i * count : (i + 1) * count] for i in range(6)]
 
 
-def small_sums_kernel(parts_one, parts_two, _after, sums, parts, turned, far, send_s, recv_s, send_f, recv_f):
+def last_collect_kernel(count, parts_one, parts_two, *refs):
+    fresh, refs = refs[:count], refs[count:]
+    sums, refs = refs[0], refs[1:]
+    fresh_all, refs = refs[:count], refs[count:]
+    parts, turned, far, send_s, recv_s, send_f, recv_f = refs[:7]
+    sems = [refs[7 + 3 * k : 10 + 3 * k] for k in range(count)]
     me = greet(True)
     z = lax.axis_index("shard")
+    shards = lax.axis_size("shard")
     parts[...] = jnp.zeros_like(parts)
     parts[0:2, :] = parts_one[0:2, :]
     parts[2:4, :] = parts_two[0:2, :]
-    for i, mask in enumerate((1, 2, 4)):
-        c = push(parts, turned.at[i], send_s.at[i], recv_s.at[i], flip(me, mask))
+    turns = [
+        push(parts, turned.at[i], send_s.at[i], recv_s.at[i], flip(me, mask))
+        for i, mask in enumerate((2, 4, 1))
+    ]
+    mine = [pltpu.make_async_copy(a, b.at[me], s[2]) for a, b, s in zip(fresh, fresh_all, sems)]
+    turns[0].start()
+    for c in mine:
         c.start()
-        c.wait()
-        parts[...] += turned[i]
-    part = parts.shape[1] // lax.axis_size("shard")
+    started = [
+        gather_begin(me, fresh[0], fresh_all[0], sems[0][0], sems[0][1])
+    ]
+    turns[0].wait()
+    parts[...] += turned[0]
+    turns[1].start()
+    for a, b, s in list(zip(fresh, fresh_all, sems))[1:]:
+        started.append(gather_begin(me, a, b, s[0], s[1]))
+    turns[1].wait()
+    parts[...] += turned[1]
+    turns[2].start()
+    turns[2].wait()
+    parts[...] += turned[2]
+    part = parts.shape[1] // shards
     waiting = []
     for k, other in enumerate(others()):
         c = pltpu.make_async_remote_copy(
@@ -995,32 +1062,40 @@
         )
         c.start()
         waiting.append(c)
+    for a, b, s, first in zip(fresh, fresh_all, sems, started):
+        gather_end(me, a, b, s[0], s[1], first)
     value = parts[:, pl.ds(pl.multiple_of(z * part, part), part)]
     for k, c in enumerate(waiting):
         c.wait()
         value = value + far[k]
     sums[...] = value
-
-
-def small_sums(parts_one, parts_two, after, cid):
+    for c in mine:
+        c.wait()
+
+
+def last_collect(parts_one, parts_two, fresh, cid):
     width = parts_one.shape[1]
     shards = lax.axis_size("shard")
-    return pl.pallas_call(
-        small_sums_kernel,
-        out_shape=jax.ShapeDtypeStruct((8, width // shards), f32),
-        in_specs=[WHOLE, WHOLE, ANY],
-        out_specs=WHOLE,
+    count = len(fresh)
+    out = pl.pallas_call(
+        functools.partial(last_collect_kernel, count),
+        out_shape=[jax.ShapeDtypeStruct((8, width // shards), f32)]
+        + [jax.ShapeDtypeStruct((8,) + a.shape, bf16) for a in fresh],
+        in_specs=[WHOLE, WHOLE] + [ANY] * count,
+        out_specs=[WHOLE] + [ANY] * count,
         scratch_shapes=[
             pltpu.VMEM((8, width), f32),
             pltpu.VMEM((3, 8, width), f32),
             pltpu.VMEM((shards - 1, 8, width // shards), f32),
         ]
         + pair(3)
-        + pair(shards - 1),
+        + pair(shards - 1)
+        + gather_scratch(8, 128)[1:] * count,
         compiler_params=params(cid),
-        cost_estimate=cost(15),
-        name="small_sums",
-    )(parts_one, parts_two, after)
+        cost_estimate=cost(5),
+        name="last_collect",
+    )(parts_one, parts_two, *fresh)
+    return out[0], out[1:]
 
 
 MASKS = (0, 2, 4, 6, 6, 1, 3, 5, 7, 7)
@@ -1032,23 +1107,6 @@
     corner, sib_corner = jnp.concatenate([low, high]), jnp.concatenate([sib_low, sib_high])
     stacked = jnp.stack([value, sib, by_x, sib_x, by_y, sib_y, corner, sib_corner])
     return jnp.take(stacked, jnp.arange(8) ^ lax.axis_index("tp"), axis=0)
-
-
-def collect_kernel(own, _after, out, send, recv, local_sem):
-    gather_all(greet(), own, out, send, recv, local_sem)
-
-
-def plane_collect(value, after, cid):
-    return pl.pallas_call(
-        collect_kernel,
-        out_shape=jax.ShapeDtypeStruct((8,) + value.shape, value.dtype),
-        in_specs=[ANY, ANY],
-        out_specs=ANY,
-        scratch_shapes=gather_scratch(*value.shape)[1:],
-        compiler_params=params(cid),
-        cost_estimate=cost(22),
-        name="plane_collect",
-    )(value, after)
 
 
 def widen_two_kernel(steps, shards, *refs):
@@ -1273,11 +1331,15 @@
     middle, normed_two = make_middle(branch, wo, x, small, 2)
     normed_two = normed_two.reshape(group_rows, width)
 
-    hidden, second_low, w_down, branch_rows = feed(
+    hidden, second_low, w_down, branch_rows, halved = feed(
         normed_two, back_low, w_two, branch, hidden_part, shards, rows, 6
     )
     down_gram = gram_rows(hidden, back_low).astype(bf16)
-    second_gram = gram_rows(normed_two, second_low).astype(bf16)
+    if halved:
+        second_gram, branch_more = gram_deal(normed_two, second_low, branch, shards, 12)
+        branch_rows = jnp.concatenate([branch_rows, branch_more])
+    else:
+        second_gram = gram_rows(normed_two, second_low).astype(bf16)
 
     def to_owner(value):
         part = lax.psum_scatter(value, "shard", scatter_dimension=0, tiled=True)
@@ -1293,13 +1355,15 @@
         middle_low, wo, q_rot, k_rot, v_low, weights_low, gating, retained, cosine, sine, decays,
         down_sum, rows, 8,
     )
-    first_gram, *second_by = gram_beside(normed, first_low, second_sum, 256, 9)
-    first_sum = to_owner(first_gram)
+    first_gram, third_gram, *second_by = gram_beside(
+        normed, first_low, second_sum, edges[3], 256, 9
+    )
+    first_sum, third_sum = to_owner(first_gram), to_owner(third_gram)
     by_x, by_y, by_sib = ([a, b] for a, b in zip(second_by, down_by))
     back_inputs, ending, parts_one, groups = make_ending(
         first_low, w_one, hidden, w_down, x, back_middle, middle, usable, small, by_x, by_y, 5
     )
-    outs = plane_collect(out_sum, ending, 10)
+    sums, (outs, firsts) = last_collect(parts_one, parts_two, [out_sum, first_sum], 10)
     low, high, sib_x, sib_y, sib_low, sib_high = groups
     seconds, downs = (
         [
@@ -1319,16 +1383,16 @@
         both = in_order(seconds).reshape(tp, piece_rows, 2, shards, unit)
         both = jnp.transpose(both, (2, 1, 3, 0, 4)).reshape(2, piece_rows, -1).astype(f32)
         gelu_gradient, up_gradient = both[0], both[1]
-    nothing = parts_one[5, 0].astype(bf16) + jnp.isnan(outs[0, 0, 0]).astype(bf16)
-    firsts = lax.all_gather(first_sum + nothing, "tp", axis=0)
-    sums = small_sums(parts_one, parts_two, down_gradient, 11)
-    query_gradient, key_gradient, value_gradient, gate_gradient = widen_one(
-        firsts, edges + (first_size,), sums, "widen_one"
-    )
+    nothing = jnp.isnan(outs[0, 0, 0]).astype(bf16)
+    thirds = lax.all_gather(third_sum + nothing, "tp", axis=0)
+    query_gradient, key_gradient, value_gradient = widen_one(
+        firsts, edges, down_gradient, "widen_one"
+    )
+    (gate_gradient,) = widen_one(thirds, (0, value_part), query_gradient, "widen_three")
     smalls = lax.psum(sums, "outer") if outer > 1 else sums
 
     home = jnp.concatenate([ending, back_inputs], axis=1)
-    home = exchange(gram_rows(work_mix, home).astype(bf16))
+    home = exchange(gram_rows(work_mix + nothing, home).astype(bf16))
     home = gram_rows(send_mix, home).astype(bf16)
     result, token_gradient = home[:, :width], home[:, width:]
     return (

time: 784 us -> 778 us (level)
  Pallas kernels: 570 us -> 590 us
  matrix products: 39.1 us -> 25.1 us
  waiting for transfers between devices: 79.2 us -> 70.3 us
    all_gather x1, waiting for transfers between devices: 31.4 us -> 2.08 us  [local(): thirds = lax.all_gather(third_sum + nothing, 'tp', axis=0)]
    pallas_call x2, Pallas kernels: 57.2 us -> 82.2 us  [the longest x1 65 us: last_collect(): pl.pallas_call(functools.partial(last_collect_kernel, count), out_shape=[...]
    all_to_all x3, waiting for transfers between devices: 41.6 us -> 61.3 us  [exchange(): lax.all_to_all(value.reshape(device_count, rows // device_count, value.sh...]
    dot_general x5 -> x4, matrix products: 36 us -> 22 us  [gram_rows(): lax.dot_general(leading, trailing, (((0,), (0,)), ((), ())), preferred_el...]
    pallas_call x1, Pallas kernels: 29.4 us -> 21 us  [feed(): pl.pallas_call(functools.partial(feed_kernel, shards, count), grid=(total...]
    pallas_call x1 -> x2, Pallas kernels: 14 us -> 17.6 us  [widen_one(): pl.pallas_call(functools.partial(widen_one_kernel, edges), grid=(rows //...]
  transfers between devices with their start and end apart: 10 -> 11, of which waited for: 3 -> 4; matrix products, arithmetic and copies ran while one was open for 8% -> 6% of each run, Pallas kernels for 68% -> 73%
where the time goes in v5:
time: 778 us; the launch traced here: 771 us
  Pallas kernels  590 us (76%)
  waiting for transfers between devices  70.3 us (9%)
  local copies, waits for them, and re-layouts  29.2 us (4%)
  matrix products  25.1 us (3%)
  starting transfers between devices  24.3 us (3%)
  between operations  17.9 us (2%)
  other arithmetic  14.8 us (2%)
    pallas_call x1, Pallas kernels, make_ending(): pl.pallas_call(functools.partial(ending_kernel, count), out_shape=shapes,...  95 us
    pallas_call x1, Pallas kernels, make_back_middle(): pl.pallas_call(back_middle_kernel, out_shape=(jax.ShapeDtypeStruct((rows,...  90.3 us
    pallas_call x1, Pallas kernels, make_middle(): pl.pallas_call(middle_kernel, out_shape=(jax.ShapeDtypeStruct((rows, widt...  88.4 us
    pallas_call x1, Pallas kernels, last_collect(): pl.pallas_call(functools.partial(last_collect_kernel, count), out_shape=[...  65 us
    all_to_all x3, waiting for transfers between devices, exchange(): lax.all_to_all(value.reshape(device_count, rows // device_count, value.sh...  61.3 us
    pallas_call x1, Pallas kernels, entry(): pl.pallas_call(entry_kernel, out_shape=(jax.ShapeDtypeStruct((rows, width...  53.8 us
    pallas_call x1, Pallas kernels, entry_back(): pl.pallas_call(entry_back_kernel, out_shape=(jax.ShapeDtypeStruct((rows,...  45.8 us
    pallas_call x1, Pallas kernels, retain(): pl.pallas_call(retain_kernel, grid=(grid,), in_specs=[row(width), leading...  30.4 us
  transfers between devices with their start and end apart: 11, of which 4 were waited for; matrix products, arithmetic and copies ran while one was open for 6% of the time, Pallas kernels for 73%

profile of v5, /device:TPU:0, one launch (start us, length us, event | category | flops | bytes accessed | tf_op | source)
XLA Modules:
  0.0 771.2 jit_solution(18210616001131334309)
XLA Ops:
  7.2 2.2 constant_dynamic-slice_fusion
  9.7 1.0 copy.41
  10.7 1.0 dynamic-slice_dynamic-update-slice_fusion.3
  11.7 1.0 dynamic-slice_dynamic-update-slice_fusion.2
  12.7 1.1 dynamic-slice_dynamic-update-slice_fusion.1
  13.9 1.1 dynamic-slice_dynamic-update-slice_fusion
  15.1 1.3 copy-done.2
  18.3 1.1 pad_maximum_fusion
  19.4 7.4 all-to-all-start
  28.7 1.0 dynamic-slice_dynamic-update-slice_fusion.11
  30.6 1.0 dynamic-slice_dynamic-update-slice_fusion.9
  31.6 1.0 dynamic-slice_dynamic-update-slice_fusion.8
  32.5 1.0 dynamic-slice_dynamic-update-slice_fusion.7
  36.5 1.2 select_reduce_fusion
  37.9 2.6 fusion.2
  41.3 41.6 %all-to-all-done = bf16[32,8,2432]{2,1,0:T(8,128)(2,1)} async-done(((bf16[32,8,2432]{2,1,0:T(8,128)(2,1)}), bf16[32,8,2432]{2,1,0:T(8,128)(2,1)}, u32[]{:S(2)}, u32[]{:S(2)}) %all-to-all-start) | async-done | bytes 1245216 | tf_op jit(solution)/shard_map/all_to_all | solution.py:1243
  82.9 12.2 %all-to-all-start.1 = ((bf16[32,8,2048]{2,1,0:T(8,128)(2,1)}), bf16[32,8,2048]{2,1,0:T(8,128)(2,1)S(1)}, u32[]{:S(2)}, u32[]{:S(2)}) async-start(bf16[32,8,2048]{2,1,0:T(8,128)(2,1)} %fusion.2), calls=%async_computation.1 | async-start | bytes 2097152 | tf_op jit(solution)/shard_map/all_to_all | solution.py:1243
  96.8 53.8 %entry.1 = (bf16[256,2048]{1,0:T(8,128)(2,1)}, bf16[8,256,2048]{2,1,0:T(8,128)(2,1)}) custom-call(bf16[256,2432]{1,0:T(8,128)(2,1)} %bitcast.1.came, bf16[256,256]{1,0:T(8,128)(2,1)} %fusion.12.mix, f32[8,2048]{1,0:T(8,128)} %pad_convert_fusion.small), custom_call_target="tpu_custom_call" | custom-call | flops 49999998976 | bytes 150000000 | tf_op jit(solution)/shard_map/entry/pallas_call | solution.py:368
  151.1 1.2 slice.40
  153.6 1.2 broadcast_add_fusion
  155.3 5.5 multiply_sine_fusion
  160.8 1.0 copy-done.5
  161.8 45.8 %entry_back.1 = (bf16[256,2048]{1,0:T(8,128)(2,1)}, bf16[8,256,2048]{2,1,0:T(8,128)(2,1)}) custom-call(bf16[256,2048]{1,0:T(8,128)(2,1)} %bitcast.61, bf16[256,256]{1,0:T(8,128)(2,1)} %fusion.12.mix, f32[256,1]{1,0:T(8,128)} %copy.46.usable, bf16[256,2048]{1,0:T(8,128)(2,1)} %get-tuple-element.74.x._after), custom_call_target="tpu_custom_call" | custom-call | flops 44999999488 | bytes 135000000 | tf_op jit(solution)/shard_map/entry_back/pallas_call | solution.py:398
  207.6 1.3 and_select_fusion.decays
  208.9 6.0 all-gather.5.cloned.1.call-done.weight.weight_in
  215.0 1.6 slice-done
  216.5 1.6 copy.53
  218.2 30.4 %retain.1 = (bf16[2048,256]{1,0:T(8,128)(2,1)}, bf16[2048,256]{1,0:T(8,128)(2,1)}, bf16[2048,512]{1,0:T(8,128)(2,1)}, bf16[16,128,128]{2,1,0:T(8,128)(2,1)}, f32...) custom-call(bf16[2048,2048]{1,0:T(8,128)(2,1)} %bitcast.70, ...), custom_call_target="tpu_custom_call" | custom-call | flops 24000000000 | bytes 72000000 | tf_op jit(solution)/shard_map/retain/pallas_call | solution.py:586
  248.6 88.4 %make_middle.1 = (f32[256,2048]{1,0:T(8,128)}, bf16[8,256,2048]{2,1,0:T(8,128)(2,1)}) custom-call(bf16[2048,512]{1,0:T(8,128)(2,1)} %get-tuple-element.72.branch, bf16[512,2048]{1,0:T(8,128)(2,1)} %bitcast.81, bf16[256,2048]{1,0:T(8,128)(2,1)} %get-tuple-element.74.x._after, f32[8,2048]{1,0:T(8,128)} %pad_convert_fusion.small), custom_call_target="tpu_custom_call" | custom-call | flops 85000003584 | bytes 255000000 | tf_op jit(solution)/shard_map/make_middle/pallas_call | solution.py:845
  337.0 21.0 %feed.1 = (bf16[2048,512]{1,0:T(8,128)(2,1)}, bf16[2048,1024]{1,0:T(8,128)(2,1)}, bf16[512,2048]{1,0:T(8,128)(2,1)}, bf16[1024,512]{1,0:T(8,128)(2,1)}) custom-call(bf16[2048,2048]{1,0:T(8,128)(2,1)} %bitcast.79, bf16[2048,2048]{1,0:T(8,128)(2,1)} %bitcast.75, bf16[2048,1536]{1,0:T(8,128)(2,1)} %all-gather.7.cloned.1.call-done.w_two.weight_in, ...), custom_call_target="tpu_custom_call" | custom-call | flops 25999998976 | bytes 78000000 | tf_op jit(solution)/shard_map/feed/pallas_call | solution.py:768
  358.0 9.9 %convolution_convert_fusion.3._after = bf16[512,2048]{1,0:T(8,128)(2,1)} fusion(bf16[2048,512]{1,0:T(8,128)(2,1)} %get-tuple-element.80.hidden_in, bf16[2048,2048]{1,0:T(8,128)(2,1)} %bitcast.76), kind=kOutput, calls=%fused_computation.5 | convolution fusion | flops 4296015872 | bytes 12582912 | tf_op jit(solution)/shard_map/dot_general | solution.py:54
  368.2 17.2 %gram_deal.1 = (bf16[2048,1024]{1,0:T(8,128)(2,1)}, bf16[1024,512]{1,0:T(8,128)(2,1)}) custom-call(bf16[2048,2048]{1,0:T(8,128)(2,1)} %bitcast.80, bf16[2048,1024]{1,0:T(8,128)(2,1)} %get-tuple-element.77.right.low_in, bf16[2048,512]{1,0:T(8,128)(2,1)} %get-tuple-element.72.branch), custom_call_target="tpu_custom_call" | custom-call | flops 16000000000 | bytes 48000000 | tf_op jit(solution)/shard_map/gram_deal/pallas_call | solution.py:713
  385.5 90.3 %make_back_middle.1 = (f32[256,2048]{1,0:T(8,128)}, f32[8,2048]{1,0:T(8,128)}, bf16[8,256,2048]{2,1,0:T(8,128)(2,1)}) custom-call(bf16[2048,1024]{1,0:T(8,128)(2,1)} %get-tuple-element.77.right.low_in, bf16[2048,1536]{1,0:T(8,128)(2,1)} %all-gather.7.cloned.1.call-done.w_two.weight_in, f32[256,2048]{1,0:T(8,128)} %get-tuple-element.78.middle, ...), custom_call_target="tpu_custom_call" | custom-call | flops 89999998976 | bytes 270000000 | tf_op jit(solution)/shard_map/make_back_middle/pallas_call | solution.py:891
  475.8 9.2 %convolution_convert_fusion.2 = bf16[512,2048]{1,0:T(8,128)(2,1)} fusion(bf16[2048,2048]{1,0:T(8,128)(2,1)} %bitcast.77, bf16[1024,512]{1,0:T(8,128)(2,1)S(1)} %copy-done.20, bf16[1024,512]{1,0:T(8,128)(2,1)S(1)} %copy-done.19), kind=kOutput, calls=%fused_computation.4 | convolution fusion | flops 4300210176 | bytes 12582912 | tf_op jit(solution)/shard_map/dot_general | solution.py:54
  485.1 18.7 %retain_back.1 = (bf16[2048,1536]{1,0:T(8,128)(2,1)}, bf16[128,2048]{1,0:T(8,128)(2,1)}, bf16[128,2048]{1,0:T(8,128)(2,1)}, bf16[128,2048]{1,0:T(8,128)(2,1)}) custom-call(bf16[2048,2048]{1,0:T(8,128)(2,1)} %bitcast.78, bf16[512,2048]{1,0:T(8,128)(2,1)} %bitcast.82, bf16[2048,256]{1,0:T(8,128)(2,1)} %get-tuple-element.83.q_in, ...), custom_call_target="tpu_custom_call" | custom-call | flops 20000000000 | bytes 60000000 | tf_op jit(solution)/shard_map/retain_back/pallas_call | solution.py:665
  503.9 29.8 %gram_beside.1 = (bf16[2048,1024]{1,0:T(8,128)(2,1)}, bf16[2048,512]{1,0:T(8,128)(2,1)}, bf16[512,1024]{1,0:T(8,128)(2,1)}, bf16[512,1024]{1,0:T(8,128)(2,1)}, bf16[512,1024]{1,0:T(8,128)(2,1)}) custom-call(bf16[2048,2048]{1,0:T(8,128)(2,1)} %bitcast.71, bf16[2048,1536]{1,0:T(8,128)(2,1)} %get-tuple-element.89.right.low_in, ...), custom_call_target="tpu_custom_call" | custom-call | flops 28000000000 | bytes 84000000 | tf_op jit(solution)/shard_map/gram_beside/pallas_call | solution.py:815
  534.7 95.0 %make_ending.1 = (bf16[256,2048]{1,0:T(8,128)(2,1)}, bf16[256,2048]{1,0:T(8,128)(2,1)}, f32[8,2048]{1,0:T(8,128)}, bf16[256,1024]{1,0:T(8,128)(2,1)}, bf16[64,20...) custom-call(bf16[2048,1536]{1,0:T(8,128)(2,1)} %get-tuple-element.89, ...), custom_call_target="tpu_custom_call" | custom-call | flops 99999997952 | bytes 300000000 | tf_op jit(solution)/shard_map/make_ending/pallas_call | solution.py:992
  629.8 65.0 %last_collect.1 = (f32[8,512]{1,0:T(8,128)}, bf16[8,128,2048]{2,1,0:T(8,128)(2,1)}, bf16[8,512,1024]{2,1,0:T(8,128)(2,1)}) custom-call(f32[8,2048]{1,0:T(8,128)} %get-tuple-element.96.parts_one, f32[8,2048]{1,0:T(8,128)} %get-tuple-element.97.parts_two, bf16[128,2048]{1,0:T(8,128)(2,1)} %reduce-scatter.10.cloned.1.call-done.refs_0_, ...), custom_call_target="tpu_custom_call" | custom-call | flops 5000000000 | bytes 15000000 | tf_op jit(solution)/shard_map/last_collect/pallas_call | solution.py:1080
  694.8 1.3 slice.41
  697.4 1.9 broadcast_add_fusion.1
  699.3 2.1 fusion
  701.5 3.7 all-to-all-start.2
  705.8 16.7 %widen_two.1 = (f32[512,4096]{1,0:T(8,128)}, f32[512,4096]{1,0:T(8,128)}, f32[8,128,2048]{2,1,0:T(8,128)}, f32[8,128,2048]{2,1,0:T(8,128)}) custom-call(bf16[512,1024]{1,0:T(8,128)(2,1)} %reduce-scatter.8.cloned.1.call-done.value.refs_0_, bf16[512,1024]{1,0:T(8,128)(2,1)} %get-tuple-element.92.refs_0_.refs_1_, bf16[512,1024]{1,0:T(8,128)(2,1)} %get-tuple-element.94.refs_2_, ...), custom_call_target="tpu_custom_call" | custom-call | flops 24999999488 | bytes 75000000 | tf_op jit(solution)/shard_map/widen_two/pallas_call | solution.py:1158
  722.4 10.2 %widen_one.1 = (f32[512,2048]{1,0:T(8,128)}, f32[512,2048]{1,0:T(8,128)}, f32[512,4096]{1,0:T(8,128)}) custom-call(bf16[8,512,1024]{2,1,0:T(8,128)(2,1)} %get-tuple-element.104.parts, f32[1024,2048]{1,0:T(8,128)} %bitcast.72), custom_call_target="tpu_custom_call" | custom-call | flops 14000000000 | bytes 42000000 | tf_op jit(solution)/shard_map/widen_one/pallas_call | solution.py:1185
  732.6 19.6 %all-to-all-done.2 = bf16[32,8,4096]{2,1,0:T(8,128)(2,1)S(1)} async-done(((bf16[32,8,4096]{2,1,0:T(8,128)(2,1)}), bf16[32,8,4096]{2,1,0:T(8,128)(2,1)S(1)}, u32[]{:S(2)}, u32[]{:S(2)}) %all-to-all-start.2) | async-done | bytes 2097184 | tf_op jit(solution)/shard_map/all_to_all | solution.py:1243
  753.0 1.5 fusion.22
  754.5 2.1 all-gather.9.cloned.1.call-done
  756.6 7.4 widen_three.1
  (115 shorter events, 14.2 us)
Async XLA Ops:
  7.2 10.6 %copy-start = (bf16[256,2048]{1,0:T(8,128)(2,1)S(1)}, bf16[256,2048]{1,0:T(8,128)(2,1)}, u32[]{:S(2)}) copy-start(bf16[256,2048]{1,0:T(8,128)(2,1)} %param.16) | copy-start | bytes 3145732
  7.2 207.8 %all-gather.5.cloned.1.call-start = ((), (), s32[]{:S(2)}) async-start(), calls=%async_computation.8 | async-start | bytes 10485760 | tf_op jit(solution)/shard_map/all_gather | solution.py:1272
  10.7 4.4 copy-start.4
  13.8 2.7 copy-start.14
  13.9 2.7 copy-start.15
  13.9 2.9 copy-start.16
  13.9 3.1 copy-start.17
  13.9 3.3 copy-start.18
  13.9 3.6 copy-start.8
  15.1 1.3 copy-start.2
  17.8 20.1 %copy-start.9 = (s32[256]{0:T(256)}, s32[256]{0:T(256)S(1)}, u32[]{:S(2)}) copy-start(s32[256]{0:T(256)S(1)} %convert_reduce_fusion.1) | copy-start | bytes 3076
  18.3 9.9 %copy-start.3 = (bf16[128,2048]{1,0:T(8,128)(2,1)S(1)}, bf16[128,2048]{1,0:T(8,128)(2,1)}, u32[]{:S(2)}) copy-start(bf16[128,2048]{1,0:T(8,128)(2,1)} %get-tuple-element.136) | copy-start | bytes 1572868
  19.4 63.5 %all-to-all-start = ((bf16[32,8,2432]{2,1,0:T(8,128)(2,1)}), bf16[32,8,2432]{2,1,0:T(8,128)(2,1)}, u32[]{:S(2)}, u32[]{:S(2)}) async-start(bf16[32,8,2432]{2,1,0:T(8,128)(2,1)} %pad_maximum_fusion), calls=%async_computation | async-start | bytes 2490368 | tf_op jit(solution)/shard_map/all_to_all | solution.py:1243
  37.9 45.0 %copy-start.11 = (s32[256]{0:T(256)}, s32[256]{0:T(256)S(1)}, u32[]{:S(2)}) copy-start(s32[256]{0:T(256)S(1)} %convert_reduce_fusion) | copy-start | bytes 3076
  82.9 77.9 %all-to-all-start.1 = ((bf16[32,8,2048]{2,1,0:T(8,128)(2,1)}), bf16[32,8,2048]{2,1,0:T(8,128)(2,1)S(1)}, u32[]{:S(2)}, u32[]{:S(2)}) async-start(bf16[32,8,2048]{2,1,0:T(8,128)(2,1)} %fusion.2), calls=%async_computation.1 | async-start | bytes 2097152 | tf_op jit(solution)/shard_map/all_to_all | solution.py:1243
  95.1 241.9 %all-gather.7.cloned.1.call-start = ((), (), s32[]{:S(2)}) async-start(), calls=%async_computation.9 | async-start | bytes 7864320 | tf_op jit(solution)/shard_map/all_gather | solution.py:1272
  154.9 330.2 %reduce-scatter.6.cloned.1.call-start = ((), (), s32[]{:S(2)}) async-start(), calls=%async_computation.10 | async-start | bytes 2621440 | tf_op jit(solution)/shard_map/reduce_scatter | solution.py:1345
  160.8 1.0 copy-start.5
  214.9 1.6 slice-start
  367.9 136.0 %reduce-scatter.8.cloned.1.call-start = ((), (), s32[]{:S(2)}) async-start(), calls=%async_computation.11 | async-start | bytes 5242880 | tf_op jit(solution)/shard_map/reduce_scatter | solution.py:1345
  385.4 244.4 %reduce-scatter.10.cloned.1.call-start = ((), (), s32[]{:S(2)}) async-start(), calls=%async_computation.12 | async-start | bytes 2621440 | tf_op jit(solution)/shard_map/reduce_scatter | solution.py:1345
  385.4 90.3 %copy-start.19 = (bf16[1024,512]{1,0:T(8,128)(2,1)S(1)}, bf16[1024,512]{1,0:T(8,128)(2,1)}, u32[]{:S(2)}) copy-start(bf16[1024,512]{1,0:T(8,128)(2,1)} %get-tuple-element.98) | copy-start | bytes 3145732
  385.4 90.3 %copy-start.20 = (bf16[1024,512]{1,0:T(8,128)(2,1)S(1)}, bf16[1024,512]{1,0:T(8,128)(2,1)}, u32[]{:S(2)}) copy-start(bf16[1024,512]{1,0:T(8,128)(2,1)} %get-tuple-element.99) | copy-start | bytes 3145732
  485.0 144.7 %reduce-scatter.12.cloned.1.call-start = ((), (), s32[]{:S(2)}) async-start(), calls=%async_computation.13 | async-start | bytes 5242880 | tf_op jit(solution)/shard_map/reduce_scatter | solution.py:1345
  533.7 163.7 %reduce-scatter.14.cloned.1.call-start = ((), (), s32[]{:S(2)}) async-start(), calls=%async_computation.14 | async-start | bytes 2621440 | tf_op jit(solution)/shard_map/reduce_scatter | solution.py:1345
  534.4 222.1 %all-gather.9.cloned.1.call-start = ((), (), s32[]{:S(2)}) async-start(), calls=%async_computation.15 | async-start | bytes 4718592 | tf_op jit(solution)/shard_map/all_gather | solution.py:1387
  629.8 69.5 %copy-start.7 = (bf16[256,2048]{1,0:T(8,128)(2,1)S(1)}, bf16[256,2048]{1,0:T(8,128)(2,1)}, u32[]{:S(2)}) copy-start(bf16[256,2048]{1,0:T(8,128)(2,1)} %get-tuple-element.102) | copy-start | bytes 3145732
  629.8 69.5 %copy-start.12 = (s32[256]{0:T(256)S(1)}, s32[256]{0:T(256)}, u32[]{:S(2)}) copy-start(s32[256]{0:T(256)} %copy-done.11) | copy-start | bytes 3076
  694.8 4.5 copy-start.6
  701.5 3.7 copy-start.13
  701.5 50.8 %all-to-all-start.2 = ((bf16[32,8,4096]{2,1,0:T(8,128)(2,1)}), bf16[32,8,4096]{2,1,0:T(8,128)(2,1)S(1)}, u32[]{:S(2)}, u32[]{:S(2)}) async-start(bf16[32,8,4096]{2,1,0:T(8,128)(2,1)} %fusion), calls=%async_computation.6 | async-start | bytes 4194304 | tf_op jit(solution)/shard_map/all_to_all | solution.py:1243
  722.4 29.8 %copy-start.10 = (s32[256]{0:T(256)S(1)}, s32[256]{0:T(256)}, u32[]{:S(2)}) copy-start(s32[256]{0:T(256)} %copy-done.9) | copy-start | bytes 3076
  756.6 7.4 copy-start.1
Sparse Core Ops, SparseCore 0:
  16.6 198.2 all-gather.4
  217.1 114.3 all-gather.6
  368.0 42.8 reduce-scatter.5
  413.1 75.9 reduce-scatter.7
  491.8 44.3 reduce-scatter.9
  538.5 76.0 reduce-scatter.11
  616.9 45.4 reduce-scatter.13
  699.4 57.1 all-gather.8

commit v6 on v5

--- a/solution.py
+++ b/solution.py
@@ -164,7 +164,7 @@
     gather_end(me, own, out, send, recv, gather_begin(me, own, out, send, recv))
 
 
-COLS = 512
+COLS = 1024
 
 
 def reduce_stages(me, pairs, transposed, tosib, fromsib, hold, hop, final, total, send, recv):
@@ -277,7 +277,7 @@
     ]
 
 
-CHUNK = 32
+CHUNK = 64
 
 
 def cost(us):
@@ -1181,7 +1181,7 @@
 def widen_one(parts, edges, after, name):
     _, rows, columns = parts.shape
     sizes = [b - a for a, b in zip(edges, edges[1:])]
-    block = 64
+    block = 128
     return pl.pallas_call(
         functools.partial(widen_one_kernel, edges),
         grid=(rows // block,),

time: 778 us -> 773 us (level)
  Pallas kernels: 590 us -> 582 us
  transfers between devices with their start and end apart: 11 -> 11, of which waited for: 4 -> 4; matrix products, arithmetic and copies ran while one was open for 6% -> 6% of each run, Pallas kernels for 73% -> 72%
where the time goes in v6:
time: 773 us; the launch traced here: 767 us
  Pallas kernels  582 us (75%)
  waiting for transfers between devices  73.6 us (10%)
  local copies, waits for them, and re-layouts  29.2 us (4%)
  matrix products  25 us (3%)
  starting transfers between devices  24.1 us (3%)
  between operations  17.7 us (2%)
  other arithmetic  14.8 us (2%)
    pallas_call x1, Pallas kernels, make_ending(): pl.pallas_call(functools.partial(ending_kernel, count), out_shape=shapes,...  94.6 us
    pallas_call x1, Pallas kernels, make_back_middle(): pl.pallas_call(back_middle_kernel, out_shape=(jax.ShapeDtypeStruct((rows,...  88 us
    pallas_call x1, Pallas kernels, make_middle(): pl.pallas_call(middle_kernel, out_shape=(jax.ShapeDtypeStruct((rows, widt...  87.2 us
    pallas_call x1, Pallas kernels, last_collect(): pl.pallas_call(functools.partial(last_collect_kernel, count), out_shape=[...  64.9 us
    all_to_all x3, waiting for transfers between devices, exchange(): lax.all_to_all(value.reshape(device_count, rows // device_count, value.sh...  62 us
    pallas_call x1, Pallas kernels, entry(): pl.pallas_call(entry_kernel, out_shape=(jax.ShapeDtypeStruct((rows, width...  52.6 us
    pallas_call x1, Pallas kernels, entry_back(): pl.pallas_call(entry_back_kernel, out_shape=(jax.ShapeDtypeStruct((rows,...  44.7 us
    pallas_call x1, Pallas kernels, retain(): pl.pallas_call(retain_kernel, grid=(grid,), in_specs=[row(width), leading...  30.4 us
  transfers between devices with their start and end apart: 11, of which 4 were waited for; matrix products, arithmetic and copies ran while one was open for 6% of the time, Pallas kernels for 72%

profile of v6, /device:TPU:0, one launch (start us, length us, event | category | flops | bytes accessed | tf_op | source)
XLA Modules:
  0.0 766.6 jit_solution(2706634723483640302)
XLA Ops:
  7.2 2.2 constant_dynamic-slice_fusion
  9.7 1.0 copy.41
  10.7 1.0 dynamic-slice_dynamic-update-slice_fusion.3
  11.7 1.0 dynamic-slice_dynamic-update-slice_fusion.2
  12.7 1.1 dynamic-slice_dynamic-update-slice_fusion.1
  13.9 1.1 dynamic-slice_dynamic-update-slice_fusion
  15.1 1.3 copy-done.2
  18.3 1.1 pad_maximum_fusion
  19.4 7.4 all-to-all-start
  28.7 1.0 dynamic-slice_dynamic-update-slice_fusion.11
  30.6 1.0 dynamic-slice_dynamic-update-slice_fusion.9
  31.6 1.0 dynamic-slice_dynamic-update-slice_fusion.8
  32.5 1.0 dynamic-slice_dynamic-update-slice_fusion.7
  36.5 1.2 select_reduce_fusion
  37.9 2.6 fusion.2
  41.3 41.6 %all-to-all-done = bf16[32,8,2432]{2,1,0:T(8,128)(2,1)} async-done(((bf16[32,8,2432]{2,1,0:T(8,128)(2,1)}), bf16[32,8,2432]{2,1,0:T(8,128)(2,1)}, u32[]{:S(2)}, u32[]{:S(2)}) %all-to-all-start) | async-done | bytes 1245216 | tf_op jit(solution)/shard_map/all_to_all | solution.py:1243
  82.9 12.2 %all-to-all-start.1 = ((bf16[32,8,2048]{2,1,0:T(8,128)(2,1)}), bf16[32,8,2048]{2,1,0:T(8,128)(2,1)S(1)}, u32[]{:S(2)}, u32[]{:S(2)}) async-start(bf16[32,8,2048]{2,1,0:T(8,128)(2,1)} %fusion.2), calls=%async_computation.1 | async-start | bytes 2097152 | tf_op jit(solution)/shard_map/all_to_all | solution.py:1243
  96.8 52.6 %entry.1 = (bf16[256,2048]{1,0:T(8,128)(2,1)}, bf16[8,256,2048]{2,1,0:T(8,128)(2,1)}) custom-call(bf16[256,2432]{1,0:T(8,128)(2,1)} %bitcast.1.came, bf16[256,256]{1,0:T(8,128)(2,1)} %fusion.12.mix, f32[8,2048]{1,0:T(8,128)} %pad_convert_fusion.small), custom_call_target="tpu_custom_call" | custom-call | flops 49999998976 | bytes 150000000 | tf_op jit(solution)/shard_map/entry/pallas_call | solution.py:368
  149.8 1.2 slice.40
  152.3 1.2 broadcast_add_fusion
  154.0 5.5 multiply_sine_fusion
  159.6 1.0 copy-done.5
  160.6 44.7 %entry_back.1 = (bf16[256,2048]{1,0:T(8,128)(2,1)}, bf16[8,256,2048]{2,1,0:T(8,128)(2,1)}) custom-call(bf16[256,2048]{1,0:T(8,128)(2,1)} %bitcast.61, bf16[256,256]{1,0:T(8,128)(2,1)} %fusion.12.mix, f32[256,1]{1,0:T(8,128)} %copy.46.usable, bf16[256,2048]{1,0:T(8,128)(2,1)} %get-tuple-element.74.x._after), custom_call_target="tpu_custom_call" | custom-call | flops 44999999488 | bytes 135000000 | tf_op jit(solution)/shard_map/entry_back/pallas_call | solution.py:398
  205.2 1.3 and_select_fusion.decays
  206.5 8.4 %all-gather.5.cloned.1.call-done.weight.weight_in = bf16[2048,2048]{1,0:T(8,128)(2,1)} async-done(((bf16[512,2048]{1,0:T(8,128)(2,1)}), bf16[2048,2048]{1,0:T(8,128)(2,1)}) %all-gather.5.cloned.1.call-update) | async-done | bytes 8388624 | tf_op jit(solution)/shard_map/all_gather | solution.py:1272
  215.0 1.6 slice-done
  216.5 1.6 copy.53
  218.2 30.4 %retain.1 = (bf16[2048,256]{1,0:T(8,128)(2,1)}, bf16[2048,256]{1,0:T(8,128)(2,1)}, bf16[2048,512]{1,0:T(8,128)(2,1)}, bf16[16,128,128]{2,1,0:T(8,128)(2,1)}, f32...) custom-call(bf16[2048,2048]{1,0:T(8,128)(2,1)} %bitcast.70, ...), custom_call_target="tpu_custom_call" | custom-call | flops 24000000000 | bytes 72000000 | tf_op jit(solution)/shard_map/retain/pallas_call | solution.py:586
  248.6 87.2 %make_middle.1 = (f32[256,2048]{1,0:T(8,128)}, bf16[8,256,2048]{2,1,0:T(8,128)(2,1)}) custom-call(bf16[2048,512]{1,0:T(8,128)(2,1)} %get-tuple-element.72.branch, bf16[512,2048]{1,0:T(8,128)(2,1)} %bitcast.81, bf16[256,2048]{1,0:T(8,128)(2,1)} %get-tuple-element.74.x._after, f32[8,2048]{1,0:T(8,128)} %pad_convert_fusion.small), custom_call_target="tpu_custom_call" | custom-call | flops 85000003584 | bytes 255000000 | tf_op jit(solution)/shard_map/make_middle/pallas_call | solution.py:845
  335.8 21.4 %feed.1 = (bf16[2048,512]{1,0:T(8,128)(2,1)}, bf16[2048,1024]{1,0:T(8,128)(2,1)}, bf16[512,2048]{1,0:T(8,128)(2,1)}, bf16[1024,512]{1,0:T(8,128)(2,1)}) custom-call(bf16[2048,2048]{1,0:T(8,128)(2,1)} %bitcast.79, bf16[2048,2048]{1,0:T(8,128)(2,1)} %bitcast.75, bf16[2048,1536]{1,0:T(8,128)(2,1)} %all-gather.7.cloned.1.call-done.w_two.weight_in, ...), custom_call_target="tpu_custom_call" | custom-call | flops 25999998976 | bytes 78000000 | tf_op jit(solution)/shard_map/feed/pallas_call | solution.py:768
  357.2 9.9 %convolution_convert_fusion.3._after = bf16[512,2048]{1,0:T(8,128)(2,1)} fusion(bf16[2048,512]{1,0:T(8,128)(2,1)} %get-tuple-element.80.hidden_in, bf16[2048,2048]{1,0:T(8,128)(2,1)} %bitcast.76), kind=kOutput, calls=%fused_computation.5 | convolution fusion | flops 4296015872 | bytes 12582912 | tf_op jit(solution)/shard_map/dot_general | solution.py:54
  367.2 17.2 %gram_deal.1 = (bf16[2048,1024]{1,0:T(8,128)(2,1)}, bf16[1024,512]{1,0:T(8,128)(2,1)}) custom-call(bf16[2048,2048]{1,0:T(8,128)(2,1)} %bitcast.80, bf16[2048,1024]{1,0:T(8,128)(2,1)} %get-tuple-element.77.right.low_in, bf16[2048,512]{1,0:T(8,128)(2,1)} %get-tuple-element.72.branch), custom_call_target="tpu_custom_call" | custom-call | flops 16000000000 | bytes 48000000 | tf_op jit(solution)/shard_map/gram_deal/pallas_call | solution.py:713
  384.5 88.0 %make_back_middle.1 = (f32[256,2048]{1,0:T(8,128)}, f32[8,2048]{1,0:T(8,128)}, bf16[8,256,2048]{2,1,0:T(8,128)(2,1)}) custom-call(bf16[2048,1024]{1,0:T(8,128)(2,1)} %get-tuple-element.77.right.low_in, bf16[2048,1536]{1,0:T(8,128)(2,1)} %all-gather.7.cloned.1.call-done.w_two.weight_in, f32[256,2048]{1,0:T(8,128)} %get-tuple-element.78.middle, ...), custom_call_target="tpu_custom_call" | custom-call | flops 89999998976 | bytes 270000000 | tf_op jit(solution)/shard_map/make_back_middle/pallas_call | solution.py:891
  472.5 9.1 %convolution_convert_fusion.2 = bf16[512,2048]{1,0:T(8,128)(2,1)} fusion(bf16[2048,2048]{1,0:T(8,128)(2,1)} %bitcast.77, bf16[1024,512]{1,0:T(8,128)(2,1)S(1)} %copy-done.20, bf16[1024,512]{1,0:T(8,128)(2,1)S(1)} %copy-done.19), kind=kOutput, calls=%fused_computation.4 | convolution fusion | flops 4300210176 | bytes 12582912 | tf_op jit(solution)/shard_map/dot_general | solution.py:54
  481.7 19.5 %retain_back.1 = (bf16[2048,1536]{1,0:T(8,128)(2,1)}, bf16[128,2048]{1,0:T(8,128)(2,1)}, bf16[128,2048]{1,0:T(8,128)(2,1)}, bf16[128,2048]{1,0:T(8,128)(2,1)}) custom-call(bf16[2048,2048]{1,0:T(8,128)(2,1)} %bitcast.78, bf16[512,2048]{1,0:T(8,128)(2,1)} %bitcast.82, bf16[2048,256]{1,0:T(8,128)(2,1)} %get-tuple-element.83.q_in, ...), custom_call_target="tpu_custom_call" | custom-call | flops 20000000000 | bytes 60000000 | tf_op jit(solution)/shard_map/retain_back/pallas_call | solution.py:665
  501.2 29.6 %gram_beside.1 = (bf16[2048,1024]{1,0:T(8,128)(2,1)}, bf16[2048,512]{1,0:T(8,128)(2,1)}, bf16[512,1024]{1,0:T(8,128)(2,1)}, bf16[512,1024]{1,0:T(8,128)(2,1)}, bf16[512,1024]{1,0:T(8,128)(2,1)}) custom-call(bf16[2048,2048]{1,0:T(8,128)(2,1)} %bitcast.71, bf16[2048,1536]{1,0:T(8,128)(2,1)} %get-tuple-element.89.right.low_in, ...), custom_call_target="tpu_custom_call" | custom-call | flops 28000000000 | bytes 84000000 | tf_op jit(solution)/shard_map/gram_beside/pallas_call | solution.py:815
  531.7 94.6 %make_ending.1 = (bf16[256,2048]{1,0:T(8,128)(2,1)}, bf16[256,2048]{1,0:T(8,128)(2,1)}, f32[8,2048]{1,0:T(8,128)}, bf16[256,1024]{1,0:T(8,128)(2,1)}, bf16[64,20...) custom-call(bf16[2048,1536]{1,0:T(8,128)(2,1)} %get-tuple-element.89, ...), custom_call_target="tpu_custom_call" | custom-call | flops 99999997952 | bytes 300000000 | tf_op jit(solution)/shard_map/make_ending/pallas_call | solution.py:992
  626.4 64.9 %last_collect.1 = (f32[8,512]{1,0:T(8,128)}, bf16[8,128,2048]{2,1,0:T(8,128)(2,1)}, bf16[8,512,1024]{2,1,0:T(8,128)(2,1)}) custom-call(f32[8,2048]{1,0:T(8,128)} %get-tuple-element.96.parts_one, f32[8,2048]{1,0:T(8,128)} %get-tuple-element.97.parts_two, bf16[128,2048]{1,0:T(8,128)(2,1)} %reduce-scatter.10.cloned.1.call-done.refs_0_, ...), custom_call_target="tpu_custom_call" | custom-call | flops 5000000000 | bytes 15000000 | tf_op jit(solution)/shard_map/last_collect/pallas_call | solution.py:1080
  691.3 1.3 slice.41
  693.9 1.9 broadcast_add_fusion.1
  695.8 2.1 fusion
  697.9 4.0 all-to-all-start.2
  702.6 16.6 %widen_two.1 = (f32[512,4096]{1,0:T(8,128)}, f32[512,4096]{1,0:T(8,128)}, f32[8,128,2048]{2,1,0:T(8,128)}, f32[8,128,2048]{2,1,0:T(8,128)}) custom-call(bf16[512,1024]{1,0:T(8,128)(2,1)} %reduce-scatter.8.cloned.1.call-done.value.refs_0_, bf16[512,1024]{1,0:T(8,128)(2,1)} %get-tuple-element.92.refs_0_.refs_1_, bf16[512,1024]{1,0:T(8,128)(2,1)} %get-tuple-element.94.refs_2_, ...), custom_call_target="tpu_custom_call" | custom-call | flops 24999999488 | bytes 75000000 | tf_op jit(solution)/shard_map/widen_two/pallas_call | solution.py:1158
  719.2 9.5 %widen_one.1 = (f32[512,2048]{1,0:T(8,128)}, f32[512,2048]{1,0:T(8,128)}, f32[512,4096]{1,0:T(8,128)}) custom-call(bf16[8,512,1024]{2,1,0:T(8,128)(2,1)} %get-tuple-element.104.parts, f32[1024,2048]{1,0:T(8,128)} %bitcast.72), custom_call_target="tpu_custom_call" | custom-call | flops 14000000000 | bytes 42000000 | tf_op jit(solution)/shard_map/widen_one/pallas_call | solution.py:1185
  728.7 20.4 %all-to-all-done.2 = bf16[32,8,4096]{2,1,0:T(8,128)(2,1)S(1)} async-done(((bf16[32,8,4096]{2,1,0:T(8,128)(2,1)}), bf16[32,8,4096]{2,1,0:T(8,128)(2,1)S(1)}, u32[]{:S(2)}, u32[]{:S(2)}) %all-to-all-start.2) | async-done | bytes 2097184 | tf_op jit(solution)/shard_map/all_to_all | solution.py:1243
  749.8 1.5 fusion.22
  751.3 2.2 all-gather.9.cloned.1.call-done
  753.5 6.0 widen_three.1
  (115 shorter events, 13.7 us)
Async XLA Ops:
  7.2 10.6 %copy-start = (bf16[256,2048]{1,0:T(8,128)(2,1)S(1)}, bf16[256,2048]{1,0:T(8,128)(2,1)}, u32[]{:S(2)}) copy-start(bf16[256,2048]{1,0:T(8,128)(2,1)} %param.16) | copy-start | bytes 3145732
  7.2 207.8 %all-gather.5.cloned.1.call-start = ((), (), s32[]{:S(2)}) async-start(), calls=%async_computation.8 | async-start | bytes 10485760 | tf_op jit(solution)/shard_map/all_gather | solution.py:1272
  10.7 4.4 copy-start.4
  13.8 2.7 copy-start.14
  13.9 2.7 copy-start.15
  13.9 2.9 copy-start.16
  13.9 3.1 copy-start.17
  13.9 3.3 copy-start.18
  13.9 3.6 copy-start.8
  15.1 1.3 copy-start.2
  17.8 20.1 %copy-start.9 = (s32[256]{0:T(256)}, s32[256]{0:T(256)S(1)}, u32[]{:S(2)}) copy-start(s32[256]{0:T(256)S(1)} %convert_reduce_fusion.1) | copy-start | bytes 3076
  18.3 9.9 %copy-start.3 = (bf16[128,2048]{1,0:T(8,128)(2,1)S(1)}, bf16[128,2048]{1,0:T(8,128)(2,1)}, u32[]{:S(2)}) copy-start(bf16[128,2048]{1,0:T(8,128)(2,1)} %get-tuple-element.136) | copy-start | bytes 1572868
  19.4 63.5 %all-to-all-start = ((bf16[32,8,2432]{2,1,0:T(8,128)(2,1)}), bf16[32,8,2432]{2,1,0:T(8,128)(2,1)}, u32[]{:S(2)}, u32[]{:S(2)}) async-start(bf16[32,8,2432]{2,1,0:T(8,128)(2,1)} %pad_maximum_fusion), calls=%async_computation | async-start | bytes 2490368 | tf_op jit(solution)/shard_map/all_to_all | solution.py:1243
  37.9 45.0 %copy-start.11 = (s32[256]{0:T(256)}, s32[256]{0:T(256)S(1)}, u32[]{:S(2)}) copy-start(s32[256]{0:T(256)S(1)} %convert_reduce_fusion) | copy-start | bytes 3076
  82.9 76.6 %all-to-all-start.1 = ((bf16[32,8,2048]{2,1,0:T(8,128)(2,1)}), bf16[32,8,2048]{2,1,0:T(8,128)(2,1)S(1)}, u32[]{:S(2)}, u32[]{:S(2)}) async-start(bf16[32,8,2048]{2,1,0:T(8,128)(2,1)} %fusion.2), calls=%async_computation.1 | async-start | bytes 2097152 | tf_op jit(solution)/shard_map/all_to_all | solution.py:1243
  95.1 240.7 %all-gather.7.cloned.1.call-start = ((), (), s32[]{:S(2)}) async-start(), calls=%async_computation.9 | async-start | bytes 7864320 | tf_op jit(solution)/shard_map/all_gather | solution.py:1272
  153.6 328.1 %reduce-scatter.6.cloned.1.call-start = ((), (), s32[]{:S(2)}) async-start(), calls=%async_computation.10 | async-start | bytes 2621440 | tf_op jit(solution)/shard_map/reduce_scatter | solution.py:1345
  159.6 1.0 copy-start.5
  215.0 1.6 slice-start
  367.2 134.1 %reduce-scatter.8.cloned.1.call-start = ((), (), s32[]{:S(2)}) async-start(), calls=%async_computation.11 | async-start | bytes 5242880 | tf_op jit(solution)/shard_map/reduce_scatter | solution.py:1345
  384.4 241.9 %reduce-scatter.10.cloned.1.call-start = ((), (), s32[]{:S(2)}) async-start(), calls=%async_computation.12 | async-start | bytes 2621440 | tf_op jit(solution)/shard_map/reduce_scatter | solution.py:1345
  384.4 88.1 %copy-start.19 = (bf16[1024,512]{1,0:T(8,128)(2,1)S(1)}, bf16[1024,512]{1,0:T(8,128)(2,1)}, u32[]{:S(2)}) copy-start(bf16[1024,512]{1,0:T(8,128)(2,1)} %get-tuple-element.98) | copy-start | bytes 3145732
  384.5 88.1 %copy-start.20 = (bf16[1024,512]{1,0:T(8,128)(2,1)S(1)}, bf16[1024,512]{1,0:T(8,128)(2,1)}, u32[]{:S(2)}) copy-start(bf16[1024,512]{1,0:T(8,128)(2,1)} %get-tuple-element.99) | copy-start | bytes 3145732
  481.7 144.7 %reduce-scatter.12.cloned.1.call-start = ((), (), s32[]{:S(2)}) async-start(), calls=%async_computation.13 | async-start | bytes 5242880 | tf_op jit(solution)/shard_map/reduce_scatter | solution.py:1345
  530.9 162.9 %reduce-scatter.14.cloned.1.call-start = ((), (), s32[]{:S(2)}) async-start(), calls=%async_computation.14 | async-start | bytes 2621440 | tf_op jit(solution)/shard_map/reduce_scatter | solution.py:1345
  531.7 221.8 %all-gather.9.cloned.1.call-start = ((), (), s32[]{:S(2)}) async-start(), calls=%async_computation.15 | async-start | bytes 4718592 | tf_op jit(solution)/shard_map/all_gather | solution.py:1387
  626.4 69.4 %copy-start.7 = (bf16[256,2048]{1,0:T(8,128)(2,1)S(1)}, bf16[256,2048]{1,0:T(8,128)(2,1)}, u32[]{:S(2)}) copy-start(bf16[256,2048]{1,0:T(8,128)(2,1)} %get-tuple-element.102) | copy-start | bytes 3145732
  626.4 69.4 %copy-start.12 = (s32[256]{0:T(256)S(1)}, s32[256]{0:T(256)}, u32[]{:S(2)}) copy-start(s32[256]{0:T(256)} %copy-done.11) | copy-start | bytes 3076
  691.3 4.5 copy-start.6
  697.9 4.0 copy-start.13
  697.9 51.1 %all-to-all-start.2 = ((bf16[32,8,4096]{2,1,0:T(8,128)(2,1)}), bf16[32,8,4096]{2,1,0:T(8,128)(2,1)S(1)}, u32[]{:S(2)}, u32[]{:S(2)}) async-start(bf16[32,8,4096]{2,1,0:T(8,128)(2,1)} %fusion), calls=%async_computation.6 | async-start | bytes 4194304 | tf_op jit(solution)/shard_map/all_to_all | solution.py:1243
  719.2 29.9 %copy-start.10 = (s32[256]{0:T(256)S(1)}, s32[256]{0:T(256)}, u32[]{:S(2)}) copy-start(s32[256]{0:T(256)} %copy-done.9) | copy-start | bytes 3076
  753.5 6.0 copy-start.1
Sparse Core Ops, SparseCore 0:
  16.6 198.3 all-gather.4
  217.1 114.3 all-gather.6
  367.3 42.7 reduce-scatter.5
  412.4 76.0 reduce-scatter.7
  491.1 44.3 reduce-scatter.9
  537.8 76.1 reduce-scatter.11
  616.2 45.3 reduce-scatter.13
  695.9 57.5 all-gather.8
